TPU v7x, 32 devices: a whole 2x2x4 slice. The times are simulated.
32 devices in a mesh: seq: 8 (over y, x, core), head: 4 (over z).
Axes of the slice: x: 2, y: 2, z: 4, core: 2. Of those that a mesh axis runs over, the one named last changes fastest.
Arguments:
- queries: float32 [4096, 1024], P('seq', 'head'), may hold values from -6 to 6
- keys: float32 [4096, 1024], P('seq', 'head'), may hold values from -6 to 6
- values: float32 [4096, 1024], P('seq', 'head'), may hold values from -60 to 60
- cotangent: float32 [4096, 1024], P('seq', 'head'), may hold values from -6 to 6
- gain: float32 [1024], P('head'), may hold values from 0.1 to 1.9
Outputs:
- grad_queries: float32 [4096, 1024], P('seq', 'head')
- grad_keys: float32 [4096, 1024], P('seq', 'head')
- grad_values: float32 [4096, 1024], P('seq', 'head')
All inputs are finite; a program needn't handle non-finite values.
Results may differ from a plain program's by a relative error of at most 0.0001.
Values sent between devices are 32-bit elements; how exact they have to be, the bound alone decides.
No kernel may reach another device: no remote copies, remote signals or barrier semaphores. Data moves between devices by JAX's collectives and lax.ppermute only.
A program may use at most 64 MiB of HBM per device.

v0:
```python
import jax
import jax.numpy as jnp
from jax import lax
from jax.sharding import PartitionSpec as P

HD = 128


def carried_in(part, axis, combine, identity, reverse):
    count = lax.axis_size(axis)
    place = lax.axis_index(axis)
    ahead = count - 1 - place if reverse else place
    gathered = lax.all_gather(part, axis)
    state = jnp.zeros_like(part) + jnp.asarray(identity, part.dtype)

    def one(hop, state):
        source = count - 1 - hop if reverse else hop
        return combine(state, lax.dynamic_index_in_dim(gathered, source, 0, False))

    return lax.fori_loop(0, ahead, one, state)


def product(form, left, right):
    return jnp.einsum(form, left, right, precision=lax.Precision.HIGHEST)


def to_blocks(array, block):
    tok_rows, width_here = array.shape
    return array.reshape(tok_rows // block, block, width_here // HD, HD).transpose(0, 2, 1, 3)


def from_blocks(array):
    count, heads_here, block, head_size = array.shape
    return array.transpose(0, 2, 1, 3).reshape(count * block, heads_here * head_size)


def add_states(earlier, later):
    return earlier + later


def shards(queries, keys, values, cotangent, gain):
    tok_rows, width_here = queries.shape
    block = min(512, tok_rows)
    query_blocks = to_blocks(queries, block)
    key_blocks = to_blocks(keys, block)
    value_blocks = to_blocks(values, block)
    causal = (jnp.arange(block)[:, None] >= jnp.arange(block)[None, :]).astype(jnp.float32)
    block_states = product("nhsd,nhse->nhde", key_blocks, value_blocks)
    own_total = jnp.sum(block_states, axis=0)
    incoming = carried_in(own_total, "seq", add_states, jnp.zeros_like(own_total), False)
    state_before = incoming[None] + jnp.cumsum(block_states, axis=0) - block_states
    scores = product("nhtd,nhsd->nhts", query_blocks, key_blocks) * causal
    attended = product("nhts,nhse->nhte", scores, value_blocks) + product(
        "nhtd,nhde->nhte", query_blocks, state_before
    )
    attended_rows = from_blocks(attended)
    scaled_cot = gain[None, :] * cotangent
    squares_part = jnp.sum(attended_rows * attended_rows, axis=1)
    cross_part = jnp.sum(scaled_cot * attended_rows, axis=1)
    squares_sum, cross_sum = lax.psum((squares_part, cross_part), "head")
    full_width = width_here * lax.axis_size("head")
    inverse = lax.rsqrt(squares_sum / full_width + 1e-06)
    cross = cross_sum / full_width
    grad_rows = (
        inverse[:, None] * scaled_cot
        - attended_rows * (inverse * inverse * inverse * cross)[:, None]
    )
    grad_blocks = to_blocks(grad_rows, block)
    grad_states = product("nhtd,nhte->nhde", query_blocks, grad_blocks)
    grad_own = jnp.sum(grad_states, axis=0)
    later_sum = carried_in(grad_own, "seq", add_states, jnp.zeros_like(grad_own), True)
    state_after = later_sum[None] + (grad_own[None] - jnp.cumsum(grad_states, axis=0))
    mixing = product("nhte,nhse->nhts", grad_blocks, value_blocks) * causal
    grad_q = product("nhts,nhsd->nhtd", mixing, key_blocks) + product(
        "nhde,nhte->nhtd", state_before, grad_blocks
    )
    grad_k = product("nhts,nhtd->nhsd", mixing, query_blocks) + product(
        "nhde,nhse->nhsd", state_after, value_blocks
    )
    grad_v = product("nhts,nhte->nhse", scores, grad_blocks) + product(
        "nhde,nhsd->nhse", state_after, key_blocks
    )
    return (from_blocks(grad_q), from_blocks(grad_k), from_blocks(grad_v))


def solution(mesh):
    in_specs = (P("seq", "head"), P("seq", "head"), P("seq", "head"), P("seq", "head"), P("head"))
    out_specs = (P("seq", "head"), P("seq", "head"), P("seq", "head"))
    return jax.shard_map(shards, mesh=mesh, in_specs=in_specs, out_specs=out_specs, check_vma=False)
```

profile of v0, /device:TPU:0, one launch (start us, length us, event | category | flops | bytes accessed | tf_op | source)
XLA Modules:
  0.0 119.3 jit_solution(17501543132378136838)
XLA Ops:
  7.2 1.3 %reshape.118 = f32[1,512,2,128]{3,2,1,0:T(2,128)S(1)} reshape(f32[512,256]{1,0:T(8,128)} %param.10) | data formatting | bytes 1048576 | tf_op jit(solution)/shard_map/reshape | solution.py:29
  8.6 1.5 %reshape.120 = f32[1,512,2,128]{3,2,1,0:T(2,128)S(1)} reshape(f32[512,256]{1,0:T(8,128)} %param.11) | data formatting | bytes 1048576 | tf_op jit(solution)/shard_map/reshape | solution.py:29
  10.1 1.7 %fusion.32 = f32[2,128,128]{2,1,0:T(8,128)} fusion(f32[1,512,2,128]{3,2,1,0:T(2,128)S(1)} %reshape.120, f32[1,512,2,128]{3,2,1,0:T(2,128)S(1)} %reshape.118), kind=kOutput, calls=%fused_computation.32 | convolution fusion | flops 201326592 | bytes 1179648 | tf_op jit(solution)/shard_map/nhsd,nhse->nhde/dot_general | solution.py:24
  13.0 3.0 %fusion.29 = f32[2,512,512]{2,1,0:T(8,128)S(1)} fusion(f32[1,512,2,128]{3,2,1,0:T(2,128)} %copy-done.2, f32[1,512,2,128]{3,2,1,0:T(2,128)} %reshape.116), kind=kOutput, calls=%fused_computation.29 | convolution fusion | flops 805306368 | bytes 3145728 | tf_op jit(solution)/shard_map/nhtd,nhsd->nhts/dot_general | solution.py:24
  16.1 22.0 %all-gather.5.cloned.1.call-done = f32[16,128,128]{2,1,0:T(8,128)} async-done(((f32[2,128,128]{2,1,0:T(8,128)}), f32[16,128,128]{2,1,0:T(8,128)}) %all-gather.5.cloned.1.call-update) | async-done | bytes 1048592 | tf_op jit(solution)/shard_map/all_gather | solution.py:13
  38.2 1.7 %convolution_bitcast_fusion.2 = f32[2,512,128]{1,2,0:T(8,128)S(1)} fusion(f32[1,512,2,128]{3,2,1,0:T(2,128)} %reshape.116, f32[2,128,128]{2,1,0:T(8,128)S(1)} %copy-done.5, f32[2,128,128]{2,1,0:T(8,128)S(1)} %get-tuple-element.82), kind=kOutput, calls=%fused_computation.16 | convolution fusion | flops 201392128 | bytes 1310720 | tf_op jit(solution)/shard_map/nhtd,nhde->nhte/dot_general | solution.py:24
  39.9 4.2 %fusion.25 = (f32[512]{0:T(512)S(1)}, f32[2,512,128]{1,2,0:T(8,128)}) fusion(f32[2,512,128]{1,2,0:T(8,128)S(1)} %convolution_bitcast_fusion.2, f32[1,512,2,128]{3,2,1,0:T(2,128)} %copy-done.1, f32[2,512,512]{2,1,0:T(8,128)S(1)} %fusion.29, f32[512,512]{1,0:T(8,128)S(1)} %fusion.24), kind=kOutput, calls=%fused_computation.25 | convolution fusion | flops 806223360 | bytes 4720640 | tf_op jit(solution)/shard_map/nhts,nhse->nhte/dot_general | solution.py:24
  44.1 2.0 %copy.34 = f32[512,256]{1,0:T(8,128)} copy(f32[512,256]{0,1:T(8,128)} %bitcast.98) | data formatting | bytes 1048576 | tf_op jit(solution)/shard_map/reshape | solution.py:34
  46.1 1.3 %multiply_reduce_fusion = f32[512]{0:T(512)S(1)} fusion(f32[512,256]{1,0:T(8,128)} %copy.34, f32[512,256]{1,0:T(8,128)} %param.12, f32[256]{0:T(256)S(1)} %copy-done.7), kind=kLoop, calls=%fused_computation.42 | loop fusion | flops 392704 | bytes 1051648 | tf_op jit(solution)/shard_map/reduce_sum | solution.py:59
  47.5 11.9 %all-reduce = (f32[512]{0:T(512)S(1)}, f32[512]{0:T(512)S(1)}) all-reduce(f32[512]{0:T(512)S(1)} %multiply_reduce_fusion, f32[512]{0:T(512)S(1)} %get-tuple-element.114), channel_id=1, replica_groups=mesh['seq'=8,'head'=4] {'head'}, use_global_device_ids=true, to_apply=%region_5.6 | all-reduce | flops 1024 | bytes 8192 | tf_op jit(solution)/shard_map/psum | solution.py:60
  59.3 2.2 %multiply_subtract_fusion = f32[512,256]{1,0:T(8,128)} fusion(f32[512,256]{1,0:T(8,128)} %copy.34, f32[512,256]{1,0:T(8,128)} %param.12, f32[512]{0:T(512)S(1)} %get-tuple-element.113, f32[256]{0:T(256)S(1)} %copy-done.7, f32[512]{0:T(512)S(1)} %get-tuple-element.112), kind=kLoop, calls=%fused_computation.41 | loop fusion | flops 524288 | bytes 1577984 | tf_op jit(solution)/shard_map/sub | solution.py:65
  61.5 2.0 %copy.58 = f32[512,256]{0,1:T(8,128)} copy(f32[512,256]{1,0:T(8,128)} %multiply_subtract_fusion) | data formatting | bytes 1048576 | tf_op jit(solution)/shard_map/reshape | solution.py:29
  63.6 1.8 %convolution_bitcast_fusion.3 = f32[2,128,128]{1,2,0:T(8,128)S(1)} fusion(f32[2,512,128]{1,2,0:T(8,128)} %bitcast.93, f32[1,512,2,128]{3,2,1,0:T(2,128)} %reshape.116), kind=kOutput, calls=%fused_computation.17 | convolution fusion | flops 201326592 | bytes 1179648 | tf_op jit(solution)/shard_map/nhtd,nhte->nhde/dot_general | solution.py:24
  66.2 1.7 %fusion.53 = f32[2,512,128]{1,2,0:T(8,128)S(1)} fusion(f32[2,512,128]{1,2,0:T(8,128)} %bitcast.94, f32[2,128,128]{2,1,0:T(8,128)S(1)} %copy-done.5, f32[2,128,128]{2,1,0:T(8,128)S(1)} %get-tuple-element.82), kind=kOutput, calls=%fused_computation.57 | convolution fusion | flops 201392128 | bytes 1310720 | tf_op jit(solution)/shard_map/nhde,nhte->nhtd/dot_general | solution.py:24
  67.9 3.0 %fusion.36 = f32[2,512,512]{2,1,0:T(8,128)S(1)} fusion(f32[2,512,128]{1,2,0:T(8,128)} %bitcast.95, f32[1,512,2,128]{3,2,1,0:T(2,128)} %copy-done.1), kind=kOutput, calls=%fused_computation.36 | convolution fusion | flops 805306368 | bytes 3145728 | tf_op jit(solution)/shard_map/nhte,nhse->nhts/dot_general | solution.py:24
  71.0 3.3 %fusion.14 = f32[2,512,128]{1,2,0:T(8,128)} fusion(f32[2,512,128]{1,2,0:T(8,128)S(1)} %fusion.53, f32[2,512,512]{2,1,0:T(8,128)S(1)} %fusion.36, f32[512,512]{1,0:T(8,128)S(1)} %fusion.24, f32[1,512,2,128]{3,2,1,0:T(2,128)S(1)} %copy-done.3), kind=kOutput, calls=%fused_computation.12 | convolution fusion | flops 805961728 | bytes 4718592 | tf_op jit(solution)/shard_map/nhts,nhsd->nhtd/dot_general | solution.py:24
  74.2 2.0 %copy.43 = f32[512,256]{1,0:T(8,128)} copy(f32[512,256]{0,1:T(8,128)} %bitcast.100) | data formatting | bytes 1048576
  76.3 16.6 %all-gather.7.cloned.1.call-done = f32[16,128,128]{2,1,0:T(8,128)} async-done(((f32[2,128,128]{2,1,0:T(8,128)}), f32[16,128,128]{2,1,0:T(8,128)}) %all-gather.7.cloned.1.call-update) | async-done | bytes 1048592 | tf_op jit(solution)/shard_map/all_gather | solution.py:13
  92.8 6.7 %while.23 = (s32[]{:T(128)}, f32[2,128,128]{2,1,0:T(8,128)S(1)}, s32[]{:T(128)}, f32[8,2,128,128]{3,2,1,0:T(8,128)}, s32[]{:T(128)}, /*index=5*/s32[]{:T(128)}, s32[]{:T(128)}, s32[]{:T(128)}) while((s32[]{:T(128)}, f32[2,128,128]{2,1,0:T(8,128)S(1)}, s32[]{:T(128)}, f32[8,2,128,128]{3,2,1,0:T(8,128)}, s32[]{:T(128)}, /*index=5*/s32[]{:T(128)}, ...), condition=%wide.region_7.8_spmd, body=%wide.region_6.7_spmd.sunk | while | flops 32774 | bytes 393359 | solution.py:20
  99.7 1.7 %convolution_bitcast_fusion = f32[2,512,128]{1,2,0:T(8,128)S(1)} fusion(f32[1,512,2,128]{3,2,1,0:T(2,128)} %copy-done.2, f32[2,128,128]{1,2,0:T(8,128)S(1)} %copy.41, f32[2,128,128]{1,2,0:T(8,128)S(1)} %convolution_bitcast_fusion.3), kind=kOutput, calls=%fused_computation.14 | convolution fusion | flops 201392128 | bytes 1310720 | tf_op jit(solution)/shard_map/nhde,nhsd->nhse/dot_general | solution.py:24
  101.4 2.5 %convolution_bitcast_fusion.1 = f32[2,512,128]{1,2,0:T(8,128)} fusion(f32[1,512,2,128]{3,2,1,0:T(2,128)} %copy-done.1, f32[2,128,128]{1,2,0:T(8,128)S(1)} %copy.41, f32[2,128,128]{1,2,0:T(8,128)S(1)} %convolution_bitcast_fusion.3), kind=kOutput, calls=%fused_computation.15 | convolution fusion | flops 201392128 | bytes 1310720 | tf_op jit(solution)/shard_map/nhde,nhse->nhsd/dot_general | solution.py:24
  103.9 2.2 %fusion.11 = f32[2,512,128]{1,2,0:T(8,128)} fusion(f32[2,512,128]{1,2,0:T(8,128)S(1)} %convolution_bitcast_fusion, f32[2,512,128]{1,2,0:T(8,128)S(1)} %bitcast.96, f32[2,512,512]{2,1,0:T(8,128)S(1)} %fusion.29, f32[512,512]{1,0:T(8,128)S(1)} %fusion.24), kind=kOutput, calls=%fused_computation.11 | convolution fusion | flops 805961728 | bytes 4718592 | tf_op jit(solution)/shard_map/nhts,nhte->nhse/dot_general | solution.py:24
  106.1 2.0 %copy.45 = f32[512,256]{1,0:T(8,128)} copy(f32[512,256]{0,1:T(8,128)} %bitcast.99) | data formatting | bytes 1048576
  108.1 3.3 %fusion.17 = f32[2,512,128]{1,2,0:T(8,128)S(1)} fusion(f32[2,512,128]{1,2,0:T(8,128)} %convolution_bitcast_fusion.1, f32[2,512,512]{2,1,0:T(8,128)} %copy-done, f32[512,512]{1,0:T(8,128)S(1)} %fusion.24, f32[1,512,2,128]{3,2,1,0:T(2,128)} %reshape.116), kind=kOutput, calls=%fused_computation.13 | convolution fusion | flops 805961728 | bytes 4718592 | tf_op jit(solution)/shard_map/nhts,nhtd->nhsd/dot_general | solution.py:24
  (36 shorter events, 9.8 us)
Async XLA Ops:
  7.2 4.7 %copy-start.6 = (f32[512,256]{1,0:T(8,128)S(1)}, f32[512,256]{1,0:T(8,128)}, u32[]{:S(2)}) copy-start(f32[512,256]{1,0:T(8,128)} %param.9) | copy-start | bytes 1572868
  7.2 30.9 %all-gather.5.cloned.1.call-start = ((), (), s32[]{:S(2)}) async-start(), calls=%async_computation | async-start | bytes 1179648 | tf_op jit(solution)/shard_map/all_gather | solution.py:13
  8.6 3.3 %copy-start.2 = (f32[1,512,2,128]{3,2,1,0:T(2,128)}, f32[1,512,2,128]{3,2,1,0:T(2,128)S(1)}, u32[]{:S(2)}) copy-start(f32[1,512,2,128]{3,2,1,0:T(2,128)S(1)} %reshape.118) | copy-start | bytes 1572868
  10.1 1.8 %copy-start.1 = (f32[1,512,2,128]{3,2,1,0:T(2,128)}, f32[1,512,2,128]{3,2,1,0:T(2,128)S(1)}, u32[]{:S(2)}) copy-start(f32[1,512,2,128]{3,2,1,0:T(2,128)S(1)} %reshape.120) | copy-start | bytes 1572868
  11.8 81.0 %all-gather.7.cloned.1.call-start = ((), (), s32[]{:S(2)}) async-start(), calls=%async_computation.1 | async-start | bytes 1179648 | tf_op jit(solution)/shard_map/all_gather | solution.py:13
  13.0 25.1 %copy-start.5 = (f32[2,128,128]{2,1,0:T(8,128)S(1)}, f32[2,128,128]{2,1,0:T(8,128)}, u32[]{:S(2)}) copy-start(f32[2,128,128]{2,1,0:T(8,128)} %fusion.32) | copy-start | bytes 393220
  39.8 6.3 %copy-start.7 = (f32[256]{0:T(256)S(1)}, f32[256]{0:T(256)}, u32[]{:S(2)}) copy-start(f32[256]{0:T(256)} %param.13) | copy-start | bytes 3076
  66.2 4.8 %copy-start.3 = (f32[1,512,2,128]{3,2,1,0:T(2,128)S(1)}, f32[1,512,2,128]{3,2,1,0:T(2,128)}, u32[]{:S(2)}) copy-start(f32[1,512,2,128]{3,2,1,0:T(2,128)} %copy-done.2) | copy-start | bytes 1572868
  71.0 3.3 %copy-start = (f32[2,512,512]{2,1,0:T(8,128)}, f32[2,512,512]{2,1,0:T(8,128)S(1)}, u32[]{:S(2)}) copy-start(f32[2,512,512]{2,1,0:T(8,128)S(1)} %fusion.36) | copy-start | bytes 6291460
  99.7 4.2 %copy-start.4 = (f32[512,256]{0,1:T(8,128)S(1)}, f32[512,256]{0,1:T(8,128)}, u32[]{:S(2)}) copy-start(f32[512,256]{0,1:T(8,128)} %copy.58) | copy-start | bytes 1572868
Sparse Core Ops, SparseCore 0:
  11.9 26.1 all-gather.4
  66.3 26.4 all-gather.6
where the time goes:
time: 120 us; the launch traced here: 119 us
  waiting for transfers between devices  38.6 us (32%)
  matrix products  30.1 us (25%)
  between operations  14.2 us (12%)
  local copies, waits for them, and re-layouts  13.9 us (12%)
  blocking collectives  11.9 us (10%)
  other arithmetic  10.2 us (8%)
    all_gather x2, waiting for transfers between devices, carried_in(): gathered = lax.all_gather(part, axis)  38.6 us
    dot_general x12, matrix products, product(): return jnp.einsum(form, left, right, precision=lax.Precision.HIGHEST)  30.1 us
    psum x1, blocking collectives, shards(): squares_sum, cross_sum = lax.psum((squares_part, cross_part), 'head')  11.9 us
    add x7, other arithmetic, add_states(): return earlier + later  6.56 us
    reshape x4, local copies, waits for them, and re-layouts, to_blocks(): array.reshape(tok_rows // block, block, width_here // HD, HD)  5.92 us
    unnamed x19, local copies, waits for them, and re-layouts  5.11 us
  transfers between devices with their start and end apart: 2, of which 2 were waited for; matrix products, arithmetic and copies ran while one was open for 12% of the time, Pallas kernels for 0%

commit v1 on v0

v1 whole, which is shorter than its diff:
```python
import functools
import jax
import jax.numpy as jnp
from jax import lax
from jax.experimental import pallas as pl
from jax.experimental.pallas import tpu as pltpu
from jax.sharding import PartitionSpec as P

HD = 128
BLOCK = 256
LANES = 128
F32 = jnp.float32
BF16 = jnp.bfloat16
NN = ((1,), (0,))
NT = ((1,), (1,))
TN = ((0,), (0,))


def split(x):
    high = x.astype(BF16)
    return high, (x - high.astype(F32)).astype(BF16)


def mul(left, right, dims):
    return lax.dot_general(left, right, (dims, ((), ())), preferred_element_type=F32)


def product(left, right, dims):
    return (
        mul(left[0], right[0], dims)
        + mul(left[0], right[1], dims)
        + mul(left[1], right[0], dims)
    )


def heads(width):
    return [slice(h * HD, (h + 1) * HD) for h in range(width // HD)]


def blocks(rows):
    size = min(BLOCK, rows)
    return [slice(n * size, (n + 1) * size) for n in range(rows // size)]


def call(body, name, out_shape, flops, *operands):
    out_shape = [jax.ShapeDtypeStruct(shape, F32) for shape in out_shape]
    moved = 4 * sum(x.size for x in list(operands) + out_shape)
    return pl.pallas_call(
        body,
        out_shape=out_shape,
        name=name,
        cost_estimate=pl.CostEstimate(flops=flops, bytes_accessed=moved, transcendentals=0),
        compiler_params=pltpu.CompilerParams(vmem_limit_bytes=16 * 1024 * 1024),
    )(*operands)


def by_core(core, first, second):
    return jnp.where(core == 0, first, second)


def store_halves(core, total, mine_ref, other_ref):
    half = total.shape[0] // 2
    mine_ref[...] = by_core(core, total[:half], total[half:])
    other_ref[...] = by_core(core, total[half:], total[:half])


def key_states(core_ref, k_ref, v_ref, mine_ref, other_ref, before_ref):
    rows, width = k_ref.shape
    states = []
    for col in heads(width):
        total = None
        for n, row in enumerate(blocks(rows)):
            state = product(split(k_ref[row, col]), split(v_ref[row, col]), TN)
            total = state if total is None else total + state
            if n + 1 < len(blocks(rows)):
                before_ref[n, col, :] = total
        states.append(total)
    store_halves(core_ref[0, 0], jnp.concatenate(states, axis=0), mine_ref, other_ref)


def causal_mask(size, transposed=False):
    row = lax.broadcasted_iota(jnp.int32, (size, size), 0)
    col = lax.broadcasted_iota(jnp.int32, (size, size), 1)
    return row <= col if transposed else row >= col


def attend_local(q_ref, k_ref, v_ref, out_ref):
    rows, width = q_ref.shape
    for col in heads(width):
        for row in blocks(rows):
            scores = product(split(q_ref[row, col]), split(k_ref[row, col]), NT)
            scores = jnp.where(causal_mask(scores.shape[0]), scores, 0.0)
            out_ref[row, col] = product(split(scores), split(v_ref[row, col]), NN)


def incoming(core, keep, got, col):
    half = keep.shape[0]
    if col.start < half:
        return by_core(core, keep[col], got[col])
    col = slice(col.start - half, col.stop - half)
    return by_core(core, got[col], keep[col])


def attend_state(core_ref, q_ref, local_ref, cot_ref, gain_ref, keep_ref, got_ref, before_ref, out_ref, sums_ref):
    rows, width = q_ref.shape
    core = core_ref[0, 0]
    for col in heads(width):
        state = incoming(core, keep_ref, got_ref, col)
        for n, row in enumerate(blocks(rows)):
            here = state if n == 0 else state + before_ref[n - 1, col, :]
            out_ref[row, col] = local_ref[row, col] + product(split(q_ref[row, col]), split(here), NN)
    count = rows // LANES
    lane = lax.broadcasted_iota(jnp.int32, (LANES, LANES), 1)
    tile = jnp.zeros((LANES, LANES), F32)
    for j in range(count):
        row = slice(j * LANES, (j + 1) * LANES)
        out = out_ref[row, :]
        squares = jnp.sum(out * out, axis=1, keepdims=True)
        cross = jnp.sum(gain_ref[...] * cot_ref[row, :] * out, axis=1, keepdims=True)
        tile = jnp.where(lane == j, squares, tile)
        tile = jnp.where(lane == count + j, cross, tile)
    sums_ref[...] = tile.T[: 2 * count]


def row_factors(full_width, sums):
    count = sums.shape[0] // 2
    inverse = lax.rsqrt(sums[:count] / full_width + 1e-06)
    factor = inverse * inverse * inverse * (sums[count:] / full_width)
    both = jnp.concatenate([inverse, factor], axis=0)
    tile = jnp.concatenate([both] * (LANES // both.shape[0]), axis=0).T
    return [(tile[:, j : j + 1], tile[:, count + j : count + j + 1]) for j in range(count)]


def grad_of_block(factors, att_ref, cot_ref, gain_ref, row, col):
    parts = []
    for j in range(row.start // LANES, row.stop // LANES):
        part = slice(j * LANES, (j + 1) * LANES)
        inverse, factor = factors[j]
        parts.append(inverse * (gain_ref[:, col] * cot_ref[part, col]) - att_ref[part, col] * factor)
    return jnp.concatenate(parts, axis=0)


def grad_states(full_width, core_ref, sums_ref, q_ref, att_ref, cot_ref, gain_ref, mine_ref, other_ref, after_ref):
    rows, width = q_ref.shape
    factors = row_factors(full_width, sums_ref[...])
    states = []
    for col in heads(width):
        total = None
        for n, row in reversed(list(enumerate(blocks(rows)))):
            grad = grad_of_block(factors, att_ref, cot_ref, gain_ref, row, col)
            state = product(split(q_ref[row, col]), split(grad), TN)
            total = state if total is None else total + state
            if n > 0:
                after_ref[n - 1, col, :] = total
        states.append(total)
    store_halves(core_ref[0, 0], jnp.concatenate(states, axis=0), mine_ref, other_ref)


def grads_local(full_width, core_ref, sums_ref, q_ref, k_ref, v_ref, att_ref, cot_ref, gain_ref, keep_ref, got_ref, before_ref, gq_ref, gk_ref, gv_ref):
    rows, width = q_ref.shape
    core = core_ref[0, 0]
    factors = row_factors(full_width, sums_ref[...])
    for col in heads(width):
        state = incoming(core, keep_ref, got_ref, col)
        for n, row in enumerate(blocks(rows)):
            here = state if n == 0 else state + before_ref[n - 1, col, :]
            grad = split(grad_of_block(factors, att_ref, cot_ref, gain_ref, row, col))
            query, key, value = split(q_ref[row, col]), split(k_ref[row, col]), split(v_ref[row, col])
            size = row.stop - row.start
            lower, upper = causal_mask(size), causal_mask(size, True)
            mixing = jnp.where(lower, product(grad, value, NT), 0.0)
            gq_ref[row, col] = product(split(mixing), key, NN) + product(grad, split(here), NT)
            mixing = jnp.where(upper, product(value, grad, NT), 0.0)
            gk_ref[row, col] = product(split(mixing), query, NN)
            scores = jnp.where(upper, product(key, query, NT), 0.0)
            gv_ref[row, col] = product(split(scores), grad, NN)


def grads_state(core_ref, k_ref, v_ref, gk_local_ref, gv_local_ref, keep_ref, got_ref, after_ref, gk_ref, gv_ref):
    rows, width = k_ref.shape
    core = core_ref[0, 0]
    last = len(blocks(rows)) - 1
    for col in heads(width):
        state = incoming(core, keep_ref, got_ref, col)
        for n, row in enumerate(blocks(rows)):
            here = split(state if n == last else state + after_ref[n, col, :])
            gk_ref[row, col] = gk_local_ref[row, col] + product(split(v_ref[row, col]), here, NT)
            gv_ref[row, col] = gv_local_ref[row, col] + product(split(k_ref[row, col]), here, NN)


def swap(x, axis, distance):
    count = lax.axis_size(axis)
    return lax.ppermute(x, axis, [(i, i ^ distance) for i in range(count)])


def carried(mine, other, reverse):
    place = lax.axis_index("seq")
    core, chip = place % 2, place // 2
    chips = lax.axis_size("seq") // 2
    from_pair = swap(other, "seq", 1)
    pair = mine + from_pair
    total = jnp.zeros_like(pair)
    if chips <= 4:
        got = [(d, swap(pair, "seq", 2 * d)) for d in range(1, chips)]
        for d, part in got:
            ahead = (chip ^ d) > chip if reverse else (chip ^ d) < chip
            total = total + jnp.where(ahead, part, 0.0)
    else:
        d = 1
        while d < chips:
            part = swap(pair, "seq", 2 * d)
            ahead = (chip ^ d) > chip if reverse else (chip ^ d) < chip
            total = total + jnp.where(ahead, part, 0.0)
            pair = pair + part
            d *= 2
    far = 0 if reverse else 1
    keep = total + jnp.where(core == far, from_pair, 0.0)
    give = total + jnp.where(core == far, 0.0, mine)
    return keep, swap(give, "seq", 1)


def sum_over_heads(x):
    count = lax.axis_size("head")
    if count > 4 or count & (count - 1):
        return lax.psum(x, "head")
    return x + sum(swap(x, "head", d) for d in range(1, count))


def shards(queries, keys, values, cotangent, gain):
    rows, width = queries.shape
    full_width = width * lax.axis_size("head")
    count = len(blocks(rows))
    square = rows * width * HD * 2 * 3
    state = (width // 2, HD)
    inner = (max(count - 1, 1), width, HD)
    core = (lax.axis_index("seq") % 2).astype(jnp.int32).reshape(1, 1)
    gain = gain.reshape(1, width)

    mine, other, before = call(key_states, "key_states", [state, state, inner], square, core, keys, values)
    keep, got = carried(mine, other, False)
    local = call(attend_local, "attend_local", [queries.shape], 4 * square, queries, keys, values)[0]
    attended, sums = call(
        attend_state, "attend_state", [queries.shape, (2 * rows // LANES, LANES)], square,
        core, queries, local, cotangent, gain, keep, got, before,
    )
    sums = sum_over_heads(sums)
    mine, other, after = call(
        functools.partial(grad_states, full_width), "grad_states", [state, state, inner], square,
        core, sums, queries, attended, cotangent, gain,
    )
    keep_after, got_after = carried(mine, other, True)
    grad_q, local_k, local_v = call(
        functools.partial(grads_local, full_width), "grads_local", [queries.shape] * 3, 12 * square,
        core, sums, queries, keys, values, attended, cotangent, gain, keep, got, before,
    )
    grad_k, grad_v = call(
        grads_state, "grads_state", [queries.shape] * 2, 2 * square,
        core, keys, values, local_k, local_v, keep_after, got_after, after,
    )
    return grad_q, grad_k, grad_v


def solution(mesh):
    in_specs = (P("seq", "head"), P("seq", "head"), P("seq", "head"), P("seq", "head"), P("head"))
    out_specs = (P("seq", "head"), P("seq", "head"), P("seq", "head"))
    return jax.shard_map(shards, mesh=mesh, in_specs=in_specs, out_specs=out_specs, check_vma=False)
```

time: 120 us -> 37.6 us (0.31)
  matrix products: 30.1 us -> 0 us
  waiting for transfers between devices: 38.6 us -> 9.89 us
  between operations: 14.2 us -> 0.78 us
  starting transfers between devices: 0.08 us -> 13.2 us
  blocking collectives: 11.9 us -> 0 us
  other arithmetic: 10.2 us -> 0.1 us
  local copies, waits for them, and re-layouts: 13.9 us -> 3.81 us
  Pallas kernels: 0 us -> 9.5 us
    all_gather x2 -> x0, waiting for transfers between devices: 38.6 us -> none  [carried_in(): gathered = lax.all_gather(part, axis)]
    dot_general x12 -> x0, matrix products: 30.1 us -> none  [product(): return jnp.einsum(form, left, right, precision=lax.Precision.HIGHEST)]
    ppermute x0 -> x13, starting transfers between devices: none -> 13.2 us  [swap(): return lax.ppermute(x, axis, [(i, i ^ distance) for i in range(count)])]
    psum x1 -> x0, blocking collectives: 11.9 us -> none  [shards(): squares_sum, cross_sum = lax.psum((squares_part, cross_part), 'head')]
    ppermute x0 -> x13, waiting for transfers between devices: none -> 9.89 us  [swap(): return lax.ppermute(x, axis, [(i, i ^ distance) for i in range(count)])]
    pallas_call x0 -> x6, Pallas kernels: none -> 9.5 us  [call(): pl.pallas_call(body, out_shape=out_shape, name=name, cost_estimate=pl.Cos...]
    reshape x5 -> x0, local copies, waits for them, and re-layouts: 7.96 us -> none  [the longest x4 5.92 us: to_blocks(): array.reshape(tok_rows // block, block, width_here // HD, HD)]
    add x7, other arithmetic: 6.56 us -> 0.1 us  [the longest x2 0.05 us: carried(): give = total + jnp.where(core == far, 0.0, mine)]
  transfers between devices with their start and end apart: 2 -> 13, of which waited for: 2 -> 8; matrix products, arithmetic and copies ran while one was open for 12% -> 0% of each run, Pallas kernels for 0% -> 17%
where the time goes in v1:
time: 37.6 us; the launch traced here: 37.3 us
  starting transfers between devices  13.2 us (35%)
  waiting for transfers between devices  9.89 us (26%)
  Pallas kernels  9.5 us (25%)
  local copies, waits for them, and re-layouts  3.81 us (10%)
  between operations  0.78 us (2%)
    ppermute x13, starting transfers between devices, swap(): return lax.ppermute(x, axis, [(i, i ^ distance) for i in range(count)])  13.2 us
    ppermute x13, waiting for transfers between devices, swap(): return lax.ppermute(x, axis, [(i, i ^ distance) for i in range(count)])  9.89 us
    pallas_call x6, Pallas kernels, call(): pl.pallas_call(body, out_shape=out_shape, name=name, cost_estimate=pl.Cos...  9.5 us
    unnamed x16, local copies, waits for them, and re-layouts  3.81 us
  transfers between devices with their start and end apart: 13, of which 8 were waited for; matrix products, arithmetic and copies ran while one was open for 0% of the time, Pallas kernels for 17%

profile of v1, /device:TPU:0, one launch (start us, length us, event | category | flops | bytes accessed | tf_op | source)
XLA Modules:
  0.0 37.3 jit_solution(9420177652307352259)
XLA Ops:
  0.7 1.0 %copy-done.1 = f32[512,256]{1,0:T(8,128)S(1)} copy-done((f32[512,256]{1,0:T(8,128)S(1)}, f32[512,256]{1,0:T(8,128)}, u32[]{:S(2)}) %copy-start.1) | copy-done | bytes 524312
  1.7 1.0 %copy-done.3 = f32[512,256]{1,0:T(8,128)S(1)} copy-done((f32[512,256]{1,0:T(8,128)S(1)}, f32[512,256]{1,0:T(8,128)}, u32[]{:S(2)}) %copy-start.3) | copy-done | bytes 524312
  3.1 0.5 %collective-permute-start = (f32[128,128]{1,0:T(8,128)S(1)}, f32[128,128]{1,0:T(8,128)S(1)}, u32[]{:S(2)}, u32[]{:S(2)}) collective-permute-start(f32[128,128]{1,0:T(8,128)S(1)} %get-tuple-element.17), channel_id=1, source_target_pairs={{0,4},{4,0},{8,12},{12,8},{16,20},{20,16},{24,28},{28,24},{1,5},{5... | collective-permute-start | bytes 196616 | tf_op jit(solution)/shard_map/ppermute | solution.py:193
  3.7 0.9 %collective-permute-done = f32[128,128]{1,0:T(8,128)S(1)} collective-permute-done((f32[128,128]{1,0:T(8,128)S(1)}, f32[128,128]{1,0:T(8,128)S(1)}, u32[]{:S(2)}, u32[]{:S(2)}) %collective-permute-start) | collective-permute-done | bytes 65568 | tf_op jit(solution)/shard_map/ppermute | solution.py:193
  4.6 3.9 %collective-permute-start.3 = (f32[128,128]{1,0:T(8,128)S(1)}, f32[128,128]{1,0:T(8,128)S(1)}, u32[]{:S(2)}, u32[]{:S(2)}) collective-permute-start(f32[128,128]{1,0:T(8,128)S(1)} %add.47), channel_id=1, source_target_pairs={{0,24},{4,28},{8,16},{12,20},{16,8},{20,12},{24,0},{28,4},{1,25},{... | collective-permute-start | bytes 196616 | tf_op jit(solution)/shard_map/ppermute | solution.py:193
  8.4 0.5 %collective-permute-start.2 = (f32[128,128]{1,0:T(8,128)S(1)}, f32[128,128]{1,0:T(8,128)S(1)}, u32[]{:S(2)}, u32[]{:S(2)}) collective-permute-start(f32[128,128]{1,0:T(8,128)S(1)} %add.47), channel_id=1, source_target_pairs={{0,16},{4,20},{8,24},{12,28},{16,0},{20,4},{24,8},{28,12},{1,17},{... | collective-permute-start | bytes 196616 | tf_op jit(solution)/shard_map/ppermute | solution.py:193
  9.1 1.0 %copy-done.4 = f32[512,256]{1,0:T(8,128)S(1)} copy-done((f32[512,256]{1,0:T(8,128)S(1)}, f32[512,256]{1,0:T(8,128)}, u32[]{:S(2)}) %copy-start.4) | copy-done | bytes 524312
  10.1 1.5 %attend_local.1.local_ref = f32[512,256]{1,0:T(8,128)S(1)} custom-call(f32[512,256]{1,0:T(8,128)S(1)} %copy-done, f32[512,256]{1,0:T(8,128)S(1)} %copy-done.2, f32[512,256]{1,0:T(8,128)S(1)} %copy-done.4), custom_call_target="tpu_custom_call" | custom-call | flops 402653184 | bytes 2097152 | tf_op jit(solution)/shard_map/attend_local/pallas_call | solution.py:48
  11.6 1.1 %collective-permute-done.2 = f32[128,128]{1,0:T(8,128)S(1)} collective-permute-done((f32[128,128]{1,0:T(8,128)S(1)}, f32[128,128]{1,0:T(8,128)S(1)}, u32[]{:S(2)}, u32[]{:S(2)}) %collective-permute-start.2) | collective-permute-done | bytes 65568 | tf_op jit(solution)/shard_map/ppermute | solution.py:193
  13.3 1.2 %collective-permute-done.4.got_ref = f32[128,128]{1,0:T(8,128)S(1)} collective-permute-done((f32[128,128]{1,0:T(8,128)S(1)}, f32[128,128]{1,0:T(8,128)S(1)}, u32[]{:S(2)}, u32[]{:S(2)}) %collective-permute-start.4) | collective-permute-done | bytes 65568 | tf_op jit(solution)/shard_map/ppermute | solution.py:193
  14.6 0.7 %copy-done.7 = f32[256]{0:T(256)S(1)} copy-done((f32[256]{0:T(256)S(1)}, f32[256]{0:T(256)}, u32[]{:S(2)}) %copy-start.7) | copy-done | bytes 1048
  15.2 0.6 %attend_state.1 = (f32[512,256]{1,0:T(8,128)S(1)}, f32[8,128]{1,0:T(8,128)S(1)}) custom-call(s32[1,1]{1,0:T(1,128)} %bitcast.core_ref, f32[512,256]{1,0:T(8,128)S(1)} %copy-done, f32[512,256]{1,0:T(8,128)S(1)} %attend_local.1.local_ref, f32[512,256]{1,0:T(8,128)S(1)} %copy-done.6, f32[1,256]{1,0:T(1,128)S(1)} %bitcast.2, ...), custom_call_target="tpu_custom_call" | custom-call | flops 100663296 | bytes 2364420 | tf_op jit(solution)/shard_map/attend_state/pallas_call | solution.py:48
  15.9 3.7 %collective-permute-start.7 = (f32[8,128]{1,0:T(8,128)S(1)}, f32[8,128]{1,0:T(8,128)S(1)}, u32[]{:S(2)}, u32[]{:S(2)}) collective-permute-start(f32[8,128]{1,0:T(8,128)S(1)} %get-tuple-element.19), channel_id=1, source_target_pairs={{0,3},{1,2},{2,1},{3,0},{4,7},{5,6},{6,5},{7,4},{8,11},{9,10},{10,... | collective-permute-start | bytes 12296 | tf_op jit(solution)/shard_map/ppermute | solution.py:193
  19.5 0.8 %collective-permute-start.5 = (f32[8,128]{1,0:T(8,128)S(1)}, f32[8,128]{1,0:T(8,128)S(1)}, u32[]{:S(2)}, u32[]{:S(2)}) collective-permute-start(f32[8,128]{1,0:T(8,128)S(1)} %get-tuple-element.19), channel_id=1, source_target_pairs={{0,1},{1,0},{2,3},{3,2},{4,5},{5,4},{6,7},{7,6},{8,9},{9,8},{10,11... | collective-permute-start | bytes 12296 | tf_op jit(solution)/shard_map/ppermute | solution.py:193
  20.3 1.0 %collective-permute-done.7 = f32[8,128]{1,0:T(8,128)S(1)} collective-permute-done((f32[8,128]{1,0:T(8,128)S(1)}, f32[8,128]{1,0:T(8,128)S(1)}, u32[]{:S(2)}, u32[]{:S(2)}) %collective-permute-start.7) | collective-permute-done | bytes 4128 | tf_op jit(solution)/shard_map/ppermute | solution.py:193
  21.3 2.7 %collective-permute-done.6 = f32[8,128]{1,0:T(8,128)S(1)} collective-permute-done((f32[8,128]{1,0:T(8,128)S(1)}, f32[8,128]{1,0:T(8,128)S(1)}, u32[]{:S(2)}, u32[]{:S(2)}) %collective-permute-start.6) | collective-permute-done | bytes 4128 | tf_op jit(solution)/shard_map/ppermute | solution.py:193
  24.0 0.7 %grad_states.1 = (f32[128,128]{1,0:T(8,128)S(1)}, f32[128,128]{1,0:T(8,128)S(1)}, f32[1,256,128]{2,1,0:T(8,128)S(1)}) custom-call(s32[1,1]{1,0:T(1,128)} %bitcast.core_ref, f32[8,128]{1,0:T(8,128)S(1)} %add_add_fusion.sums_ref, f32[512,256]{1,0:T(8,128)S(1)} %copy-done, f32[512,256]{1,0:T(8,128)S(1)} %get-tuple-element.20.att_ref, f32[512,256]{1,0:T(8,128)S(1)} %copy-done.6, ...), custom_call_target="tpu_custom_call" | custom-call | flops 100663296 | bytes 1840132 | tf_op jit(solution)/shard_map/grad_states/pallas_call | solution.py:48
  24.8 1.2 %collective-permute-done.8 = f32[128,128]{1,0:T(8,128)S(1)} collective-permute-done((f32[128,128]{1,0:T(8,128)S(1)}, f32[128,128]{1,0:T(8,128)S(1)}, u32[]{:S(2)}, u32[]{:S(2)}) %collective-permute-start.8) | collective-permute-done | bytes 65568 | tf_op jit(solution)/shard_map/ppermute | solution.py:193
  26.1 1.5 %collective-permute-start.11 = (f32[128,128]{1,0:T(8,128)S(1)}, f32[128,128]{1,0:T(8,128)S(1)}, u32[]{:S(2)}, u32[]{:S(2)}) collective-permute-start(f32[128,128]{1,0:T(8,128)S(1)} %add.55), channel_id=1, source_target_pairs={{0,24},{4,28},{8,16},{12,20},{16,8},{20,12},{24,0},{28,4},{1,25},{... | collective-permute-start | bytes 196616 | tf_op jit(solution)/shard_map/ppermute | solution.py:193
  27.6 0.8 %collective-permute-start.10 = (f32[128,128]{1,0:T(8,128)S(1)}, f32[128,128]{1,0:T(8,128)S(1)}, u32[]{:S(2)}, u32[]{:S(2)}) collective-permute-start(f32[128,128]{1,0:T(8,128)S(1)} %add.55), channel_id=1, source_target_pairs={{0,16},{4,20},{8,24},{12,28},{16,0},{20,4},{24,8},{28,12},{1,17},{... | collective-permute-start | bytes 196616 | tf_op jit(solution)/shard_map/ppermute | solution.py:193
  28.4 1.3 %collective-permute-start.9 = (f32[128,128]{1,0:T(8,128)S(1)}, f32[128,128]{1,0:T(8,128)S(1)}, u32[]{:S(2)}, u32[]{:S(2)}) collective-permute-start(f32[128,128]{1,0:T(8,128)S(1)} %add.55), channel_id=1, source_target_pairs={{0,8},{4,12},{8,0},{12,4},{16,24},{20,28},{24,16},{28,20},{1,9},{5... | collective-permute-start | bytes 196616 | tf_op jit(solution)/shard_map/ppermute | solution.py:193
  29.6 4.7 %grads_local.1 = (f32[512,256]{1,0:T(8,128)}, f32[512,256]{1,0:T(8,128)S(1)}, f32[512,256]{1,0:T(8,128)S(1)}) custom-call(s32[1,1]{1,0:T(1,128)} %bitcast.core_ref, f32[8,128]{1,0:T(8,128)S(1)} %add_add_fusion.sums_ref, f32[512,256]{1,0:T(8,128)S(1)} %copy-done, f32[512,256]{1,0:T(8,128)S(1)} %copy-done.2, f32[512,256]{1,0:T(8,128)S(1)} %copy-done.5, ...), custom_call_target="tpu_custom_call" | custom-call | flops 1207959552 | bytes 4461572 | tf_op jit(solution)/shard_map/grads_local/pallas_call | solution.py:48
  34.5 1.2 %collective-permute-done.12.got_ref = f32[128,128]{1,0:T(8,128)S(1)} collective-permute-done((f32[128,128]{1,0:T(8,128)S(1)}, f32[128,128]{1,0:T(8,128)S(1)}, u32[]{:S(2)}, u32[]{:S(2)}) %collective-permute-start.12) | collective-permute-done | bytes 65568 | tf_op jit(solution)/shard_map/ppermute | solution.py:193
  35.7 1.6 %grads_state.1 = (f32[512,256]{1,0:T(8,128)}, f32[512,256]{1,0:T(8,128)}) custom-call(s32[1,1]{1,0:T(1,128)} %bitcast.core_ref, f32[512,256]{1,0:T(8,128)S(1)} %copy-done.2, f32[512,256]{1,0:T(8,128)S(1)} %copy-done.5, f32[512,256]{1,0:T(8,128)S(1)} %get-tuple-element.22.gk_local_ref, f32[512,256]{1,0:T(8,128)S(1)} %get-tuple-element.23.gv_local_ref, ...), custom_call_target="tpu_custom_call" | custom-call | flops 201326592 | bytes 3407876 | tf_op jit(solution)/shard_map/grads_state/pallas_call | solution.py:48
  (31 shorter events, 1.4 us)
Async XLA Ops:
  0.6 1.0 %copy-start.1 = (f32[512,256]{1,0:T(8,128)S(1)}, f32[512,256]{1,0:T(8,128)}, u32[]{:S(2)}) copy-start(f32[512,256]{1,0:T(8,128)} %k_ref.7) | copy-start | bytes 1572868
  1.7 1.0 %copy-start.3 = (f32[512,256]{1,0:T(8,128)S(1)}, f32[512,256]{1,0:T(8,128)}, u32[]{:S(2)}) copy-start(f32[512,256]{1,0:T(8,128)} %v_ref.7) | copy-start | bytes 1572868
  2.7 6.4 %copy-start = (f32[512,256]{1,0:T(8,128)S(1)}, f32[512,256]{1,0:T(8,128)}, u32[]{:S(2)}) copy-start(f32[512,256]{1,0:T(8,128)} %q_ref.7) | copy-start | bytes 1572868
  2.7 6.4 %copy-start.2 = (f32[512,256]{1,0:T(8,128)S(1)}, f32[512,256]{1,0:T(8,128)}, u32[]{:S(2)}) copy-start(f32[512,256]{1,0:T(8,128)} %k_ref.7) | copy-start | bytes 1572868
  3.1 1.4 %collective-permute-start = (f32[128,128]{1,0:T(8,128)S(1)}, f32[128,128]{1,0:T(8,128)S(1)}, u32[]{:S(2)}, u32[]{:S(2)}) collective-permute-start(f32[128,128]{1,0:T(8,128)S(1)} %get-tuple-element.17), channel_id=1, source_target_pairs={{0,4},{4,0},{8,12},{12,8},{16,20},{20,16},{24,28},{28,24},{1,5},{5... | collective-permute-start | bytes 196616 | tf_op jit(solution)/shard_map/ppermute | solution.py:193
  4.6 7.0 %collective-permute-start.3 = (f32[128,128]{1,0:T(8,128)S(1)}, f32[128,128]{1,0:T(8,128)S(1)}, u32[]{:S(2)}, u32[]{:S(2)}) collective-permute-start(f32[128,128]{1,0:T(8,128)S(1)} %add.47), channel_id=1, source_target_pairs={{0,24},{4,28},{8,16},{12,20},{16,8},{20,12},{24,0},{28,4},{1,25},{... | collective-permute-start | bytes 196616 | tf_op jit(solution)/shard_map/ppermute | solution.py:193
  8.4 4.3 %collective-permute-start.2 = (f32[128,128]{1,0:T(8,128)S(1)}, f32[128,128]{1,0:T(8,128)S(1)}, u32[]{:S(2)}, u32[]{:S(2)}) collective-permute-start(f32[128,128]{1,0:T(8,128)S(1)} %add.47), channel_id=1, source_target_pairs={{0,16},{4,20},{8,24},{12,28},{16,0},{20,4},{24,8},{28,12},{1,17},{... | collective-permute-start | bytes 196616 | tf_op jit(solution)/shard_map/ppermute | solution.py:193
  8.9 4.3 %collective-permute-start.1 = (f32[128,128]{1,0:T(8,128)S(1)}, f32[128,128]{1,0:T(8,128)S(1)}, u32[]{:S(2)}, u32[]{:S(2)}) collective-permute-start(f32[128,128]{1,0:T(8,128)S(1)} %add.47), channel_id=1, source_target_pairs={{0,8},{4,12},{8,0},{12,4},{16,24},{20,28},{24,16},{28,20},{1,9},{5... | collective-permute-start | bytes 196616 | tf_op jit(solution)/shard_map/ppermute | solution.py:193
  9.1 1.0 %copy-start.4 = (f32[512,256]{1,0:T(8,128)S(1)}, f32[512,256]{1,0:T(8,128)}, u32[]{:S(2)}) copy-start(f32[512,256]{1,0:T(8,128)} %v_ref.7) | copy-start | bytes 1572868
  11.6 2.9 %copy-start.6 = (f32[512,256]{1,0:T(8,128)S(1)}, f32[512,256]{1,0:T(8,128)}, u32[]{:S(2)}) copy-start(f32[512,256]{1,0:T(8,128)} %cot_ref.5) | copy-start | bytes 1572868
  13.2 1.3 %collective-permute-start.4 = (f32[128,128]{1,0:T(8,128)S(1)}, f32[128,128]{1,0:T(8,128)S(1)}, u32[]{:S(2)}, u32[]{:S(2)}) collective-permute-start(f32[128,128]{1,0:T(8,128)S(1)} %get-tuple-element.31), channel_id=1, source_target_pairs={{0,4},{4,0},{8,12},{12,8},{16,20},{20,16},{24,28},{28,24},{1,5},{5... | collective-permute-start | bytes 196616 | tf_op jit(solution)/shard_map/ppermute | solution.py:193
  14.6 0.7 %copy-start.7 = (f32[256]{0:T(256)S(1)}, f32[256]{0:T(256)}, u32[]{:S(2)}) copy-start(f32[256]{0:T(256)} %param.9) | copy-start | bytes 3076
  15.9 5.4 %collective-permute-start.7 = (f32[8,128]{1,0:T(8,128)S(1)}, f32[8,128]{1,0:T(8,128)S(1)}, u32[]{:S(2)}, u32[]{:S(2)}) collective-permute-start(f32[8,128]{1,0:T(8,128)S(1)} %get-tuple-element.19), channel_id=1, source_target_pairs={{0,3},{1,2},{2,1},{3,0},{4,7},{5,6},{6,5},{7,4},{8,11},{9,10},{10,... | collective-permute-start | bytes 12296 | tf_op jit(solution)/shard_map/ppermute | solution.py:193
  19.5 4.5 %collective-permute-start.6 = (f32[8,128]{1,0:T(8,128)S(1)}, f32[8,128]{1,0:T(8,128)S(1)}, u32[]{:S(2)}, u32[]{:S(2)}) collective-permute-start(f32[8,128]{1,0:T(8,128)S(1)} %get-tuple-element.19), channel_id=1, source_target_pairs={{0,2},{1,3},{2,0},{3,1},{4,6},{5,7},{6,4},{7,5},{8,10},{9,11},{10,... | collective-permute-start | bytes 12296 | tf_op jit(solution)/shard_map/ppermute | solution.py:193
  19.5 4.5 %collective-permute-start.5 = (f32[8,128]{1,0:T(8,128)S(1)}, f32[8,128]{1,0:T(8,128)S(1)}, u32[]{:S(2)}, u32[]{:S(2)}) collective-permute-start(f32[8,128]{1,0:T(8,128)S(1)} %get-tuple-element.19), channel_id=1, source_target_pairs={{0,1},{1,0},{2,3},{3,2},{4,5},{5,4},{6,7},{7,6},{8,9},{9,8},{10,11... | collective-permute-start | bytes 12296 | tf_op jit(solution)/shard_map/ppermute | solution.py:193
  24.0 5.6 %copy-start.5 = (f32[512,256]{1,0:T(8,128)S(1)}, f32[512,256]{1,0:T(8,128)}, u32[]{:S(2)}) copy-start(f32[512,256]{1,0:T(8,128)} %v_ref.7) | copy-start | bytes 1572868
  24.7 1.3 %collective-permute-start.8 = (f32[128,128]{1,0:T(8,128)S(1)}, f32[128,128]{1,0:T(8,128)S(1)}, u32[]{:S(2)}, u32[]{:S(2)}) collective-permute-start(f32[128,128]{1,0:T(8,128)S(1)} %get-tuple-element.25), channel_id=1, source_target_pairs={{0,4},{4,0},{8,12},{12,8},{16,20},{20,16},{24,28},{28,24},{1,5},{5... | collective-permute-start | bytes 196616 | tf_op jit(solution)/shard_map/ppermute | solution.py:193
  26.1 8.3 %collective-permute-start.11 = (f32[128,128]{1,0:T(8,128)S(1)}, f32[128,128]{1,0:T(8,128)S(1)}, u32[]{:S(2)}, u32[]{:S(2)}) collective-permute-start(f32[128,128]{1,0:T(8,128)S(1)} %add.55), channel_id=1, source_target_pairs={{0,24},{4,28},{8,16},{12,20},{16,8},{20,12},{24,0},{28,4},{1,25},{... | collective-permute-start | bytes 196616 | tf_op jit(solution)/shard_map/ppermute | solution.py:193
  27.6 6.7 %collective-permute-start.10 = (f32[128,128]{1,0:T(8,128)S(1)}, f32[128,128]{1,0:T(8,128)S(1)}, u32[]{:S(2)}, u32[]{:S(2)}) collective-permute-start(f32[128,128]{1,0:T(8,128)S(1)} %add.55), channel_id=1, source_target_pairs={{0,16},{4,20},{8,24},{12,28},{16,0},{20,4},{24,8},{28,12},{1,17},{... | collective-permute-start | bytes 196616 | tf_op jit(solution)/shard_map/ppermute | solution.py:193
  28.4 6.0 %collective-permute-start.9 = (f32[128,128]{1,0:T(8,128)S(1)}, f32[128,128]{1,0:T(8,128)S(1)}, u32[]{:S(2)}, u32[]{:S(2)}) collective-permute-start(f32[128,128]{1,0:T(8,128)S(1)} %add.55), channel_id=1, source_target_pairs={{0,8},{4,12},{8,0},{12,4},{16,24},{20,28},{24,16},{28,20},{1,9},{5... | collective-permute-start | bytes 196616 | tf_op jit(solution)/shard_map/ppermute | solution.py:193
  34.4 1.3 %collective-permute-start.12 = (f32[128,128]{1,0:T(8,128)S(1)}, f32[128,128]{1,0:T(8,128)S(1)}, u32[]{:S(2)}, u32[]{:S(2)}) collective-permute-start(f32[128,128]{1,0:T(8,128)S(1)} %get-tuple-element.29), channel_id=1, source_target_pairs={{0,4},{4,0},{8,12},{12,8},{16,20},{20,16},{24,28},{28,24},{1,5},{5... | collective-permute-start | bytes 196616 | tf_op jit(solution)/shard_map/ppermute | solution.py:193

commit v2 on v1

v2 whole, which is shorter than its diff:
```python
import functools
import jax
import jax.numpy as jnp
from jax import lax
from jax.experimental import pallas as pl
from jax.experimental.pallas import tpu as pltpu
from jax.sharding import PartitionSpec as P

HD = 128
BLOCK = 256
LANES = 128
F32 = jnp.float32
BF16 = jnp.bfloat16
NN = ((1,), (0,))
NT = ((1,), (1,))
TN = ((0,), (0,))


def split(x):
    high = x.astype(BF16)
    return high, (x - high.astype(F32)).astype(BF16)


def mul(left, right, dims):
    return lax.dot_general(left, right, (dims, ((), ())), preferred_element_type=F32)


def beside(*parts):
    return jnp.concatenate(parts, axis=1)


def product_nt(left, right):
    return mul(beside(*left), beside(right[0], right[0]), NT) + mul(left[0], right[1], NT)


def product_nn(left, right):
    size = right[0].shape[1]
    wide = mul(left[0], beside(*right), NN)
    return wide[:, :size] + wide[:, size:] + mul(left[1], right[0], NN)


def product_tn(left, right):
    rows, cols = left[0].shape[1], right[0].shape[1]
    wide = mul(beside(*left), beside(*right), TN)
    return wide[:rows, :cols] + wide[:rows, cols:] + wide[rows:, :cols]


def state_operand(state, transposed):
    high, low = split(state)
    if transposed:
        return jnp.concatenate([beside(high, high), beside(low, jnp.zeros_like(low))], axis=0)
    return jnp.concatenate([beside(high, low), beside(high, jnp.zeros_like(low))], axis=0)


def product_state(left, operand, transposed):
    wide = mul(beside(*left), operand, NT if transposed else NN)
    return wide[:, :HD] + wide[:, HD:]


def heads(width):
    return [slice(h * HD, (h + 1) * HD) for h in range(width // HD)]


def blocks(rows):
    size = min(BLOCK, rows)
    return [slice(n * size, (n + 1) * size) for n in range(rows // size)]


def call(body, name, outs, flops, operands, scratch=(), hbm_in=(), hbm_out=()):
    outs = [out if isinstance(out[0], tuple) else (out, F32) for out in outs]
    outs = [
        pltpu.HBM(*out) if i in hbm_out else jax.ShapeDtypeStruct(*out) for i, out in enumerate(outs)
    ]
    moved = sum(x.size * x.dtype.itemsize for x in operands) * 2
    operands = [
        pltpu.with_memory_space_constraint(x, pltpu.HBM) if i in hbm_in else x for i, x in enumerate(operands)
    ]
    place = lambda far: pl.BlockSpec(memory_space=pltpu.HBM if far else pltpu.VMEM)
    return pl.pallas_call(
        body,
        out_shape=outs,
        in_specs=[place(i in hbm_in) for i in range(len(operands))],
        out_specs=[place(i in hbm_out) for i in range(len(outs))],
        scratch_shapes=list(scratch),
        name=name,
        cost_estimate=pl.CostEstimate(flops=flops, bytes_accessed=moved, transcendentals=0),
        compiler_params=pltpu.CompilerParams(vmem_limit_bytes=16 * 1024 * 1024),
    )(*operands)


def on_first_core():
    return lax.axis_index("seq") % 2 == 0


def store_halves(total, mine_ref, other_ref):
    half = total.shape[0] // 2
    first = on_first_core()
    mine_ref[...] = jnp.where(first, total[:half], total[half:])
    other_ref[...] = jnp.where(first, total[half:], total[:half])


def key_states(k_hbm, v_hbm, mine_ref, other_ref, before_ref, k_ref, v_ref, sems):
    rows, width = k_ref.shape
    pieces = sems.shape[1]
    size = rows // pieces
    copies = []
    for p in range(pieces):
        row = pl.ds(p * size, size)
        copies.append([
            pltpu.make_async_copy(far.at[row], near.at[row], sems.at[i, p])
            for i, (far, near) in enumerate(((k_hbm, k_ref), (v_hbm, v_ref)))
        ])
        for copy in copies[p]:
            copy.start()
    states = {}
    for n, row in enumerate(blocks(rows)):
        for p in range(row.start // size, row.stop // size):
            for copy in copies[p]:
                copy.wait()
        for col in heads(width):
            state = product_tn(split(k_ref[row, col]), split(v_ref[row, col]))
            states[col.start] = states[col.start] + state if n > 0 else state
            if n + 1 < len(blocks(rows)):
                before_ref[n, col, :] = states[col.start]
    store_halves(jnp.concatenate([states[col.start] for col in heads(width)], axis=0), mine_ref, other_ref)


def causal_mask(size, transposed=False):
    row = lax.broadcasted_iota(jnp.int32, (size, size), 0)
    col = lax.broadcasted_iota(jnp.int32, (size, size), 1)
    return row <= col if transposed else row >= col


def attend_local(q_ref, k_ref, v_ref, cot_ref, gain_ref, out_ref, scaled_ref):
    rows, width = q_ref.shape
    for col in heads(width):
        for row in blocks(rows):
            scaled_ref[row, col] = gain_ref[:, col] * cot_ref[row, col]
            scores = product_nt(split(q_ref[row, col]), split(k_ref[row, col]))
            scores = jnp.where(causal_mask(scores.shape[0]), scores, 0.0)
            out_ref[row, col] = product_nn(split(scores), split(v_ref[row, col]))


def incoming(keep_ref, got_ref, col):
    half = keep_ref.shape[0]
    first = on_first_core()
    if col.start < half:
        return jnp.where(first, keep_ref[col, :], got_ref[col, :])
    col = slice(col.start - half, col.stop - half)
    return jnp.where(first, got_ref[col, :], keep_ref[col, :])


def attend_state(q_ref, local_ref, scaled_ref, keep_ref, got_ref, before_ref, out_ref, sums_ref):
    rows, width = q_ref.shape
    for col in heads(width):
        state = incoming(keep_ref, got_ref, col)
        for n, row in enumerate(blocks(rows)):
            here = state_operand(state if n == 0 else state + before_ref[n - 1, col, :], False)
            out_ref[row, col] = local_ref[row, col] + product_state(split(q_ref[row, col]), here, False)
    count = rows // LANES
    lane = lax.broadcasted_iota(jnp.int32, (LANES, LANES), 1)
    tile = jnp.zeros((LANES, LANES), F32)
    for j in range(count):
        row = slice(j * LANES, (j + 1) * LANES)
        out = out_ref[row, :]
        squares = jnp.sum(out * out, axis=1, keepdims=True)
        cross = jnp.sum(scaled_ref[row, :] * out, axis=1, keepdims=True)
        tile = jnp.where(lane == j, squares, tile)
        tile = jnp.where(lane == count + j, cross, tile)
    sums_ref[...] = tile.T[: 2 * count]


def row_factors(full_width, sums):
    count = sums.shape[0] // 2
    inverse = lax.rsqrt(sums[:count] / full_width + 1e-06)
    factor = inverse * inverse * inverse * (sums[count:] / full_width)
    both = jnp.concatenate([inverse, factor], axis=0)
    tile = jnp.concatenate([both] * (LANES // both.shape[0]), axis=0).T
    return [(tile[:, j : j + 1], tile[:, count + j : count + j + 1]) for j in range(count)]


def grad_of_block(factors, att_ref, scaled_ref, row, col):
    parts = []
    for j in range(row.start // LANES, row.stop // LANES):
        part = slice(j * LANES, (j + 1) * LANES)
        inverse, factor = factors[j]
        parts.append(inverse * scaled_ref[part, col] - att_ref[part, col] * factor)
    return jnp.concatenate(parts, axis=0)


def grad_states(full_width, sums_ref, q_ref, att_ref, scaled_ref, mine_ref, other_ref, after_ref, high_ref, low_ref):
    rows, width = q_ref.shape
    factors = row_factors(full_width, sums_ref[...])
    states = []
    for col in heads(width):
        total = None
        for n, row in reversed(list(enumerate(blocks(rows)))):
            grad = split(grad_of_block(factors, att_ref, scaled_ref, row, col))
            high_ref[row, col], low_ref[row, col] = grad
            state = product_tn(split(q_ref[row, col]), grad)
            total = state if total is None else total + state
            if n > 0:
                after_ref[n - 1, col, :] = total
        states.append(total)
    store_halves(jnp.concatenate(states, axis=0), mine_ref, other_ref)


def grads_local(grad_high_ref, grad_low_ref, q_ref, k_ref, v_ref, keep_ref, got_ref, before_ref, gq_hbm, gk_ref, gv_ref, gq_ref, sems):
    rows, width = q_ref.shape
    copies = []
    for col in heads(width):
        state = incoming(keep_ref, got_ref, col)
        for n, row in enumerate(blocks(rows)):
            here = state_operand(state if n == 0 else state + before_ref[n - 1, col, :], True)
            grad = grad_high_ref[row, col], grad_low_ref[row, col]
            mixing = product_nt(grad, split(v_ref[row, col]))
            mixing = jnp.where(causal_mask(row.stop - row.start), mixing, 0.0)
            gq_ref[row, col] = product_nn(split(mixing), split(k_ref[row, col])) + product_state(grad, here, True)
            copies.append(pltpu.make_async_copy(gq_ref.at[row, col], gq_hbm.at[row, col], sems.at[len(copies)]))
            copies[-1].start()
    for col in heads(width):
        for row in blocks(rows):
            grad = grad_high_ref[row, col], grad_low_ref[row, col]
            query, key, value = split(q_ref[row, col]), split(k_ref[row, col]), split(v_ref[row, col])
            mask = causal_mask(row.stop - row.start, True)
            mixing = jnp.where(mask, product_nt(value, grad), 0.0)
            gk_ref[row, col] = product_nn(split(mixing), query)
            scores = jnp.where(mask, product_nt(key, query), 0.0)
            gv_ref[row, col] = product_nn(split(scores), grad)
    for copy in copies:
        copy.wait()


def grads_state(k_ref, v_ref, gk_local_ref, gv_local_ref, keep_ref, got_ref, after_ref, gk_hbm, gv_hbm, gk_ref, gv_ref, sems):
    rows, width = k_ref.shape
    last = len(blocks(rows)) - 1
    unit = 0
    copies = []
    for col in heads(width):
        state = incoming(keep_ref, got_ref, col)
        for n, row in enumerate(blocks(rows)):
            here = state if n == last else state + after_ref[n, col, :]
            gk_ref[row, col] = gk_local_ref[row, col] + product_state(split(v_ref[row, col]), state_operand(here, True), True)
            copies.append(pltpu.make_async_copy(gk_ref.at[row, col], gk_hbm.at[row, col], sems.at[0, unit]))
            copies[-1].start()
            gv_ref[row, col] = gv_local_ref[row, col] + product_state(split(k_ref[row, col]), state_operand(here, False), False)
            copies.append(pltpu.make_async_copy(gv_ref.at[row, col], gv_hbm.at[row, col], sems.at[1, unit]))
            copies[-1].start()
            unit += 1
    for copy in copies:
        copy.wait()


def swap(x, axis, distance):
    count = lax.axis_size(axis)
    return lax.ppermute(x, axis, [(i, i ^ distance) for i in range(count)])


def carried(mine, other, reverse):
    place = lax.axis_index("seq")
    core, chip = place % 2, place // 2
    chips = lax.axis_size("seq") // 2
    from_pair = swap(other, "seq", 1)
    pair = mine + from_pair
    total = jnp.zeros_like(pair)
    if chips <= 4:
        got = [(d, swap(pair, "seq", 2 * d)) for d in range(1, chips)]
        for d, part in got:
            ahead = (chip ^ d) > chip if reverse else (chip ^ d) < chip
            total = total + jnp.where(ahead, part, 0.0)
    else:
        d = 1
        while d < chips:
            part = swap(pair, "seq", 2 * d)
            ahead = (chip ^ d) > chip if reverse else (chip ^ d) < chip
            total = total + jnp.where(ahead, part, 0.0)
            pair = pair + part
            d *= 2
    far = 0 if reverse else 1
    keep = total + jnp.where(core == far, from_pair, 0.0)
    give = total + jnp.where(core == far, 0.0, mine)
    return keep, swap(give, "seq", 1)


def sum_of_other_heads(x):
    count = lax.axis_size("head")
    if count > 4 or count & (count - 1):
        return lax.psum(x, "head") - x
    return sum(swap(x, "head", d) for d in range(1, count))


def shards(queries, keys, values, cotangent, gain):
    rows, width = queries.shape
    full_width = width * lax.axis_size("head")
    count = len(blocks(rows))
    units = count * (width // HD)
    size = rows // count
    square = rows * width * HD * 2 * 3
    whole, half = (rows, width), (width // 2, HD)
    inner = (max(count - 1, 1), width, HD)
    pieces = count

    mine, other, before, keys, values = call(
        key_states, "key_states", [half, half, inner, whole, whole], square, [keys, values],
        [pltpu.SemaphoreType.DMA((2, pieces))], hbm_in=(0, 1),
    )
    keep, got = carried(mine, other, False)
    local, scaled = call(
        attend_local, "attend_local", [whole, whole], 4 * square,
        [queries, keys, values, cotangent, gain.reshape(1, width)],
    )
    attended, own_sums = call(
        attend_state, "attend_state", [whole, (2 * rows // LANES, LANES)], square,
        [queries, local, scaled, keep, got, before],
    )
    other_sums = sum_of_other_heads(own_sums)
    sums = own_sums + other_sums
    mine, other, after, grad_high, grad_low = call(
        functools.partial(grad_states, full_width), "grad_states",
        [half, half, inner, (whole, BF16), (whole, BF16)], square,
        [sums, queries, attended, scaled],
    )
    keep_after, got_after = carried(mine, other, True)
    grad_q, local_k, local_v = call(
        grads_local, "grads_local", [whole] * 3, 13 * square,
        [grad_high, grad_low, queries, keys, values, keep, got, before],
        [pltpu.VMEM(whole, F32), pltpu.SemaphoreType.DMA((units,))], hbm_out=(0,),
    )
    grad_k, grad_v = call(
        grads_state, "grads_state", [whole] * 2, 2 * square,
        [keys, values, local_k, local_v, keep_after, got_after, after],
        [pltpu.VMEM(whole, F32), pltpu.VMEM(whole, F32), pltpu.SemaphoreType.DMA((2, units))], hbm_out=(0, 1),
    )
    return grad_q, grad_k, grad_v


def solution(mesh):
    in_specs = (P("seq", "head"), P("seq", "head"), P("seq", "head"), P("seq", "head"), P("head"))
    out_specs = (P("seq", "head"), P("seq", "head"), P("seq", "head"))
    return jax.shard_map(shards, mesh=mesh, in_specs=in_specs, out_specs=out_specs, check_vma=False)
```

time: 37.6 us -> 34.1 us (0.907)
  local copies, waits for them, and re-layouts: 3.81 us -> 0.68 us
  Pallas kernels: 9.5 us -> 8.32 us
  waiting for transfers between devices: 9.89 us -> 10.8 us
    unnamed x16 -> x6, local copies, waits for them, and re-layouts: 3.81 us -> 0.68 us
    pallas_call x6, Pallas kernels: 9.5 us -> 8.32 us  [call(): pl.pallas_call(body, out_shape=outs, in_specs=[place(i in hbm_in) for i i...]
    ppermute x13, waiting for transfers between devices: 9.89 us -> 10.8 us  [swap(): return lax.ppermute(x, axis, [(i, i ^ distance) for i in range(count)])]
  transfers between devices with their start and end apart: 13 -> 13, of which waited for: 8 -> 10; matrix products, arithmetic and copies ran while one was open for 0% -> 0% of each run, Pallas kernels for 17% -> 12%
where the time goes in v2:
time: 34.1 us; the launch traced here: 33.9 us
  starting transfers between devices  13.2 us (39%)
  waiting for transfers between devices  10.8 us (32%)
  Pallas kernels  8.32 us (24%)
  between operations  0.79 us (2%)
  local copies, waits for them, and re-layouts  0.68 us (2%)
    ppermute x13, starting transfers between devices, swap(): return lax.ppermute(x, axis, [(i, i ^ distance) for i in range(count)])  13.2 us
    ppermute x13, waiting for transfers between devices, swap(): return lax.ppermute(x, axis, [(i, i ^ distance) for i in range(count)])  10.8 us
    pallas_call x6, Pallas kernels, call(): pl.pallas_call(body, out_shape=outs, in_specs=[place(i in hbm_in) for i i...  8.32 us
  transfers between devices with their start and end apart: 13, of which 10 were waited for; matrix products, arithmetic and copies ran while one was open for 0% of the time, Pallas kernels for 12%

profile of v2, /device:TPU:0, one launch (start us, length us, event | category | flops | bytes accessed | tf_op | source)
XLA Modules:
  0.0 33.9 jit_solution(10380438179278883462)
XLA Ops:
  0.7 1.7 %key_states.1 = (f32[128,128]{1,0:T(8,128)S(1)}, f32[128,128]{1,0:T(8,128)S(1)}, f32[1,256,128]{2,1,0:T(8,128)S(1)}, f32[512,256]{1,0:T(8,128)S(1)}, f32[512,256]{1,0:T(8,128)S(1)}) custom-call(f32[512,256]{1,0:T(8,128)} %k_hbm.1, f32[512,256]{1,0:T(8,128)} %v_hbm.1), custom_call_target="tpu_custom_call" | custom-call | flops 100663296 | bytes 2097152 | tf_op jit(solution)/shard_map/key_states/pallas_call | solution.py:79
  2.4 0.5 %collective-permute-start = (f32[128,128]{1,0:T(8,128)S(1)}, f32[128,128]{1,0:T(8,128)S(1)}, u32[]{:S(2)}, u32[]{:S(2)}) collective-permute-start(f32[128,128]{1,0:T(8,128)S(1)} %get-tuple-element.27), channel_id=1, source_target_pairs={{0,4},{4,0},{8,12},{12,8},{16,20},{20,16},{24,28},{28,24},{1,5},{5... | collective-permute-start | bytes 196616 | tf_op jit(solution)/shard_map/ppermute | solution.py:256
  2.9 0.9 %collective-permute-done = f32[128,128]{1,0:T(8,128)S(1)} collective-permute-done((f32[128,128]{1,0:T(8,128)S(1)}, f32[128,128]{1,0:T(8,128)S(1)}, u32[]{:S(2)}, u32[]{:S(2)}) %collective-permute-start) | collective-permute-done | bytes 65568 | tf_op jit(solution)/shard_map/ppermute | solution.py:256
  3.8 3.9 %collective-permute-start.3 = (f32[128,128]{1,0:T(8,128)S(1)}, f32[128,128]{1,0:T(8,128)S(1)}, u32[]{:S(2)}, u32[]{:S(2)}) collective-permute-start(f32[128,128]{1,0:T(8,128)S(1)} %add.45), channel_id=1, source_target_pairs={{0,24},{4,28},{8,16},{12,20},{16,8},{20,12},{24,0},{28,4},{1,25},{... | collective-permute-start | bytes 196616 | tf_op jit(solution)/shard_map/ppermute | solution.py:256
  7.7 0.5 %collective-permute-start.2 = (f32[128,128]{1,0:T(8,128)S(1)}, f32[128,128]{1,0:T(8,128)S(1)}, u32[]{:S(2)}, u32[]{:S(2)}) collective-permute-start(f32[128,128]{1,0:T(8,128)S(1)} %add.45), channel_id=1, source_target_pairs={{0,16},{4,20},{8,24},{12,28},{16,0},{20,4},{24,8},{28,12},{1,17},{... | collective-permute-start | bytes 196616 | tf_op jit(solution)/shard_map/ppermute | solution.py:256
  8.3 0.7 %copy-done.2 = f32[256]{0:T(256)S(1)} copy-done((f32[256]{0:T(256)S(1)}, f32[256]{0:T(256)}, u32[]{:S(2)}) %copy-start.2) | copy-done | bytes 1048
  9.0 0.9 %attend_local.1 = (f32[512,256]{1,0:T(8,128)S(1)}, f32[512,256]{1,0:T(8,128)S(1)}) custom-call(f32[512,256]{1,0:T(8,128)S(1)} %copy-done, f32[512,256]{1,0:T(8,128)S(1)} %get-tuple-element.22.k_ref, f32[512,256]{1,0:T(8,128)S(1)} %get-tuple-element.23.v_ref, f32[512,256]{1,0:T(8,128)S(1)} %copy-done.1, f32[1,256]{1,0:T(1,128)S(1)} %bitcast.1), custom_call_target="tpu_custom_call" | custom-call | flops 402653184 | bytes 4196352 | tf_op jit(solution)/shard_map/attend_local/pallas_call | solution.py:79
  10.1 1.9 %collective-permute-done.2 = f32[128,128]{1,0:T(8,128)S(1)} collective-permute-done((f32[128,128]{1,0:T(8,128)S(1)}, f32[128,128]{1,0:T(8,128)S(1)}, u32[]{:S(2)}, u32[]{:S(2)}) %collective-permute-start.2) | collective-permute-done | bytes 65568 | tf_op jit(solution)/shard_map/ppermute | solution.py:256
  11.9 0.5 %collective-permute-done.1 = f32[128,128]{1,0:T(8,128)S(1)} collective-permute-done((f32[128,128]{1,0:T(8,128)S(1)}, f32[128,128]{1,0:T(8,128)S(1)}, u32[]{:S(2)}, u32[]{:S(2)}) %collective-permute-start.1) | collective-permute-done | bytes 65568 | tf_op jit(solution)/shard_map/ppermute | solution.py:256
  12.5 1.2 %collective-permute-done.4.got_ref = f32[128,128]{1,0:T(8,128)S(1)} collective-permute-done((f32[128,128]{1,0:T(8,128)S(1)}, f32[128,128]{1,0:T(8,128)S(1)}, u32[]{:S(2)}, u32[]{:S(2)}) %collective-permute-start.4) | collective-permute-done | bytes 65568 | tf_op jit(solution)/shard_map/ppermute | solution.py:256
  13.8 0.5 %attend_state.1 = (f32[512,256]{1,0:T(8,128)S(1)}, f32[8,128]{1,0:T(8,128)S(1)}) custom-call(f32[512,256]{1,0:T(8,128)S(1)} %copy-done, f32[512,256]{1,0:T(8,128)S(1)} %get-tuple-element.24.local_ref, f32[512,256]{1,0:T(8,128)S(1)} %get-tuple-element.25.scaled_ref, f32[128,128]{1,0:T(8,128)S(1)} %select_add_fusion.4.keep_ref, ...), custom_call_target="tpu_custom_call" | custom-call | flops 100663296 | bytes 3670016 | tf_op jit(solution)/shard_map/attend_state/pallas_call | solution.py:79
  14.3 3.6 %collective-permute-start.7 = (f32[8,128]{1,0:T(8,128)S(1)}, f32[8,128]{1,0:T(8,128)S(1)}, u32[]{:S(2)}, u32[]{:S(2)}) collective-permute-start(f32[8,128]{1,0:T(8,128)S(1)} %get-tuple-element.29), channel_id=1, source_target_pairs={{0,3},{1,2},{2,1},{3,0},{4,7},{5,6},{6,5},{7,4},{8,11},{9,10},{10,... | collective-permute-start | bytes 12296 | tf_op jit(solution)/shard_map/ppermute | solution.py:256
  17.9 0.8 %collective-permute-start.6 = (f32[8,128]{1,0:T(8,128)S(1)}, f32[8,128]{1,0:T(8,128)S(1)}, u32[]{:S(2)}, u32[]{:S(2)}) collective-permute-start(f32[8,128]{1,0:T(8,128)S(1)} %get-tuple-element.29), channel_id=1, source_target_pairs={{0,2},{1,3},{2,0},{3,1},{4,6},{5,7},{6,4},{7,5},{8,10},{9,11},{10,... | collective-permute-start | bytes 12296 | tf_op jit(solution)/shard_map/ppermute | solution.py:256
  18.7 1.0 %collective-permute-done.7 = f32[8,128]{1,0:T(8,128)S(1)} collective-permute-done((f32[8,128]{1,0:T(8,128)S(1)}, f32[8,128]{1,0:T(8,128)S(1)}, u32[]{:S(2)}, u32[]{:S(2)}) %collective-permute-start.7) | collective-permute-done | bytes 4128 | tf_op jit(solution)/shard_map/ppermute | solution.py:256
  19.7 1.8 %collective-permute-done.5 = f32[8,128]{1,0:T(8,128)S(1)} collective-permute-done((f32[8,128]{1,0:T(8,128)S(1)}, f32[8,128]{1,0:T(8,128)S(1)}, u32[]{:S(2)}, u32[]{:S(2)}) %collective-permute-start.5) | collective-permute-done | bytes 4128 | tf_op jit(solution)/shard_map/ppermute | solution.py:256
  21.5 0.9 %collective-permute-done.6 = f32[8,128]{1,0:T(8,128)S(1)} collective-permute-done((f32[8,128]{1,0:T(8,128)S(1)}, f32[8,128]{1,0:T(8,128)S(1)}, u32[]{:S(2)}, u32[]{:S(2)}) %collective-permute-start.6) | collective-permute-done | bytes 4128 | tf_op jit(solution)/shard_map/ppermute | solution.py:256
  22.4 0.7 %grad_states.1 = (f32[128,128]{1,0:T(8,128)S(1)}, f32[128,128]{1,0:T(8,128)S(1)}, f32[1,256,128]{2,1,0:T(8,128)S(1)}, bf16[512,256]{1,0:T(8,128)(2,1)S(1)}, bf16[512,256]{1,0:T(8,128)(2,1)S(1)}) custom-call(f32[8,128]{1,0:T(8,128)S(1)} %add_add_fusion.sums_ref, f32[512,256]{1,0:T(8,128)S(1)} %copy-done, f32[512,256]{1,0:T(8,128)S(1)} %get-tuple-element.30.att_ref, ...), custom_call_target="tpu_custom_call" | custom-call | flops 100663296 | bytes 3153920 | tf_op jit(solution)/shard_map/grad_states/pallas_call | solution.py:79
  23.2 1.2 %collective-permute-done.8 = f32[128,128]{1,0:T(8,128)S(1)} collective-permute-done((f32[128,128]{1,0:T(8,128)S(1)}, f32[128,128]{1,0:T(8,128)S(1)}, u32[]{:S(2)}, u32[]{:S(2)}) %collective-permute-start.8) | collective-permute-done | bytes 65568 | tf_op jit(solution)/shard_map/ppermute | solution.py:256
  24.5 1.6 %collective-permute-start.11 = (f32[128,128]{1,0:T(8,128)S(1)}, f32[128,128]{1,0:T(8,128)S(1)}, u32[]{:S(2)}, u32[]{:S(2)}) collective-permute-start(f32[128,128]{1,0:T(8,128)S(1)} %add.54), channel_id=1, source_target_pairs={{0,24},{4,28},{8,16},{12,20},{16,8},{20,12},{24,0},{28,4},{1,25},{... | collective-permute-start | bytes 196616 | tf_op jit(solution)/shard_map/ppermute | solution.py:256
  26.0 0.8 %collective-permute-start.10 = (f32[128,128]{1,0:T(8,128)S(1)}, f32[128,128]{1,0:T(8,128)S(1)}, u32[]{:S(2)}, u32[]{:S(2)}) collective-permute-start(f32[128,128]{1,0:T(8,128)S(1)} %add.54), channel_id=1, source_target_pairs={{0,16},{4,20},{8,24},{12,28},{16,0},{20,4},{24,8},{28,12},{1,17},{... | collective-permute-start | bytes 196616 | tf_op jit(solution)/shard_map/ppermute | solution.py:256
  26.8 1.2 %collective-permute-start.9 = (f32[128,128]{1,0:T(8,128)S(1)}, f32[128,128]{1,0:T(8,128)S(1)}, u32[]{:S(2)}, u32[]{:S(2)}) collective-permute-start(f32[128,128]{1,0:T(8,128)S(1)} %add.54), channel_id=1, source_target_pairs={{0,8},{4,12},{8,0},{12,4},{16,24},{20,28},{24,16},{28,20},{1,9},{5... | collective-permute-start | bytes 196616 | tf_op jit(solution)/shard_map/ppermute | solution.py:256
  28.0 3.2 %grads_local.1 = (f32[512,256]{1,0:T(8,128)}, f32[512,256]{1,0:T(8,128)S(1)}, f32[512,256]{1,0:T(8,128)S(1)}) custom-call(bf16[512,256]{1,0:T(8,128)(2,1)S(1)} %get-tuple-element.31.grad_high_ref, bf16[512,256]{1,0:T(8,128)(2,1)S(1)} %get-tuple-element.32.grad_low_ref, f32[512,256]{1,0:T(8,128)S(1)} %copy-done, f32[512,256]{1,0:T(8,128)S(1)} %get-tuple-element.22.k_ref, ...), custom_call_target="tpu_custom_call" | custom-call | flops 1308622848 | bytes 4718592 | tf_op jit(solution)/shard_map/grads_local/pallas_call | solution.py:79
  31.4 1.2 %collective-permute-done.12.got_ref = f32[128,128]{1,0:T(8,128)S(1)} collective-permute-done((f32[128,128]{1,0:T(8,128)S(1)}, f32[128,128]{1,0:T(8,128)S(1)}, u32[]{:S(2)}, u32[]{:S(2)}) %collective-permute-start.12) | collective-permute-done | bytes 65568 | tf_op jit(solution)/shard_map/ppermute | solution.py:256
  32.6 1.3 %grads_state.1 = (f32[512,256]{1,0:T(8,128)}, f32[512,256]{1,0:T(8,128)}) custom-call(f32[512,256]{1,0:T(8,128)S(1)} %get-tuple-element.22.k_ref, f32[512,256]{1,0:T(8,128)S(1)} %get-tuple-element.23.v_ref, f32[512,256]{1,0:T(8,128)S(1)} %get-tuple-element.34.gk_local_ref, f32[512,256]{1,0:T(8,128)S(1)} %get-tuple-element.35.gv_local_ref, ...), custom_call_target="tpu_custom_call" | custom-call | flops 201326592 | bytes 4718592 | tf_op jit(solution)/shard_map/grads_state/pallas_call | solution.py:79
  (21 shorter events, 0.6 us)
Async XLA Ops:
  0.6 7.7 %copy-start = (f32[512,256]{1,0:T(8,128)S(1)}, f32[512,256]{1,0:T(8,128)}, u32[]{:S(2)}) copy-start(f32[512,256]{1,0:T(8,128)} %q_ref.7) | copy-start | bytes 1572868
  0.6 7.7 %copy-start.1 = (f32[512,256]{1,0:T(8,128)S(1)}, f32[512,256]{1,0:T(8,128)}, u32[]{:S(2)}) copy-start(f32[512,256]{1,0:T(8,128)} %cot_ref.1) | copy-start | bytes 1572868
  2.4 1.4 %collective-permute-start = (f32[128,128]{1,0:T(8,128)S(1)}, f32[128,128]{1,0:T(8,128)S(1)}, u32[]{:S(2)}, u32[]{:S(2)}) collective-permute-start(f32[128,128]{1,0:T(8,128)S(1)} %get-tuple-element.27), channel_id=1, source_target_pairs={{0,4},{4,0},{8,12},{12,8},{16,20},{20,16},{24,28},{28,24},{1,5},{5... | collective-permute-start | bytes 196616 | tf_op jit(solution)/shard_map/ppermute | solution.py:256
  3.8 6.3 %collective-permute-start.3 = (f32[128,128]{1,0:T(8,128)S(1)}, f32[128,128]{1,0:T(8,128)S(1)}, u32[]{:S(2)}, u32[]{:S(2)}) collective-permute-start(f32[128,128]{1,0:T(8,128)S(1)} %add.45), channel_id=1, source_target_pairs={{0,24},{4,28},{8,16},{12,20},{16,8},{20,12},{24,0},{28,4},{1,25},{... | collective-permute-start | bytes 196616 | tf_op jit(solution)/shard_map/ppermute | solution.py:256
  7.7 4.3 %collective-permute-start.2 = (f32[128,128]{1,0:T(8,128)S(1)}, f32[128,128]{1,0:T(8,128)S(1)}, u32[]{:S(2)}, u32[]{:S(2)}) collective-permute-start(f32[128,128]{1,0:T(8,128)S(1)} %add.45), channel_id=1, source_target_pairs={{0,16},{4,20},{8,24},{12,28},{16,0},{20,4},{24,8},{28,12},{1,17},{... | collective-permute-start | bytes 196616 | tf_op jit(solution)/shard_map/ppermute | solution.py:256
  8.2 4.3 %collective-permute-start.1 = (f32[128,128]{1,0:T(8,128)S(1)}, f32[128,128]{1,0:T(8,128)S(1)}, u32[]{:S(2)}, u32[]{:S(2)}) collective-permute-start(f32[128,128]{1,0:T(8,128)S(1)} %add.45), channel_id=1, source_target_pairs={{0,8},{4,12},{8,0},{12,4},{16,24},{20,28},{24,16},{28,20},{1,9},{5... | collective-permute-start | bytes 196616 | tf_op jit(solution)/shard_map/ppermute | solution.py:256
  8.3 0.7 %copy-start.2 = (f32[256]{0:T(256)S(1)}, f32[256]{0:T(256)}, u32[]{:S(2)}) copy-start(f32[256]{0:T(256)} %param.9) | copy-start | bytes 3076
  12.5 1.3 %collective-permute-start.4 = (f32[128,128]{1,0:T(8,128)S(1)}, f32[128,128]{1,0:T(8,128)S(1)}, u32[]{:S(2)}, u32[]{:S(2)}) collective-permute-start(f32[128,128]{1,0:T(8,128)S(1)} %get-tuple-element.43), channel_id=1, source_target_pairs={{0,4},{4,0},{8,12},{12,8},{16,20},{20,16},{24,28},{28,24},{1,5},{5... | collective-permute-start | bytes 196616 | tf_op jit(solution)/shard_map/ppermute | solution.py:256
  14.3 5.4 %collective-permute-start.7 = (f32[8,128]{1,0:T(8,128)S(1)}, f32[8,128]{1,0:T(8,128)S(1)}, u32[]{:S(2)}, u32[]{:S(2)}) collective-permute-start(f32[8,128]{1,0:T(8,128)S(1)} %get-tuple-element.29), channel_id=1, source_target_pairs={{0,3},{1,2},{2,1},{3,0},{4,7},{5,6},{6,5},{7,4},{8,11},{9,10},{10,... | collective-permute-start | bytes 12296 | tf_op jit(solution)/shard_map/ppermute | solution.py:256
  17.9 3.6 %collective-permute-start.5 = (f32[8,128]{1,0:T(8,128)S(1)}, f32[8,128]{1,0:T(8,128)S(1)}, u32[]{:S(2)}, u32[]{:S(2)}) collective-permute-start(f32[8,128]{1,0:T(8,128)S(1)} %get-tuple-element.29), channel_id=1, source_target_pairs={{0,1},{1,0},{2,3},{3,2},{4,5},{5,4},{6,7},{7,6},{8,9},{9,8},{10,11... | collective-permute-start | bytes 12296 | tf_op jit(solution)/shard_map/ppermute | solution.py:256
  17.9 4.5 %collective-permute-start.6 = (f32[8,128]{1,0:T(8,128)S(1)}, f32[8,128]{1,0:T(8,128)S(1)}, u32[]{:S(2)}, u32[]{:S(2)}) collective-permute-start(f32[8,128]{1,0:T(8,128)S(1)} %get-tuple-element.29), channel_id=1, source_target_pairs={{0,2},{1,3},{2,0},{3,1},{4,6},{5,7},{6,4},{7,5},{8,10},{9,11},{10,... | collective-permute-start | bytes 12296 | tf_op jit(solution)/shard_map/ppermute | solution.py:256
  23.1 1.3 %collective-permute-start.8 = (f32[128,128]{1,0:T(8,128)S(1)}, f32[128,128]{1,0:T(8,128)S(1)}, u32[]{:S(2)}, u32[]{:S(2)}) collective-permute-start(f32[128,128]{1,0:T(8,128)S(1)} %get-tuple-element.37), channel_id=1, source_target_pairs={{0,4},{4,0},{8,12},{12,8},{16,20},{20,16},{24,28},{28,24},{1,5},{5... | collective-permute-start | bytes 196616 | tf_op jit(solution)/shard_map/ppermute | solution.py:256
  24.5 6.8 %collective-permute-start.11 = (f32[128,128]{1,0:T(8,128)S(1)}, f32[128,128]{1,0:T(8,128)S(1)}, u32[]{:S(2)}, u32[]{:S(2)}) collective-permute-start(f32[128,128]{1,0:T(8,128)S(1)} %add.54), channel_id=1, source_target_pairs={{0,24},{4,28},{8,16},{12,20},{16,8},{20,12},{24,0},{28,4},{1,25},{... | collective-permute-start | bytes 196616 | tf_op jit(solution)/shard_map/ppermute | solution.py:256
  26.0 5.2 %collective-permute-start.10 = (f32[128,128]{1,0:T(8,128)S(1)}, f32[128,128]{1,0:T(8,128)S(1)}, u32[]{:S(2)}, u32[]{:S(2)}) collective-permute-start(f32[128,128]{1,0:T(8,128)S(1)} %add.54), channel_id=1, source_target_pairs={{0,16},{4,20},{8,24},{12,28},{16,0},{20,4},{24,8},{28,12},{1,17},{... | collective-permute-start | bytes 196616 | tf_op jit(solution)/shard_map/ppermute | solution.py:256
  26.8 4.5 %collective-permute-start.9 = (f32[128,128]{1,0:T(8,128)S(1)}, f32[128,128]{1,0:T(8,128)S(1)}, u32[]{:S(2)}, u32[]{:S(2)}) collective-permute-start(f32[128,128]{1,0:T(8,128)S(1)} %add.54), channel_id=1, source_target_pairs={{0,8},{4,12},{8,0},{12,4},{16,24},{20,28},{24,16},{28,20},{1,9},{5... | collective-permute-start | bytes 196616 | tf_op jit(solution)/shard_map/ppermute | solution.py:256
  31.3 1.3 %collective-permute-start.12 = (f32[128,128]{1,0:T(8,128)S(1)}, f32[128,128]{1,0:T(8,128)S(1)}, u32[]{:S(2)}, u32[]{:S(2)}) collective-permute-start(f32[128,128]{1,0:T(8,128)S(1)} %get-tuple-element.41), channel_id=1, source_target_pairs={{0,4},{4,0},{8,12},{12,8},{16,20},{20,16},{24,28},{28,24},{1,5},{5... | collective-permute-start | bytes 196616 | tf_op jit(solution)/shard_map/ppermute | solution.py:256

commit v3 on v0

v3 whole, which is shorter than its diff:
```python
import functools
import jax
import jax.numpy as jnp
from jax import lax
from jax.experimental import pallas as pl
from jax.experimental.pallas import tpu as pltpu
from jax.sharding import PartitionSpec as P

HD = 128
BLOCK = 256
LANES = 128
F32 = jnp.float32
BF16 = jnp.bfloat16
NN = ((1,), (0,))
NT = ((1,), (1,))
TN = ((0,), (0,))


def split(x):
    high = x.astype(BF16)
    return high, (x - high.astype(F32)).astype(BF16)


def mul(left, right, dims):
    return lax.dot_general(left, right, (dims, ((), ())), preferred_element_type=F32)


def beside(*parts):
    return jnp.concatenate(parts, axis=1)


def product_nt(left, right):
    return mul(beside(*left), beside(right[0], right[0]), NT) + mul(left[0], right[1], NT)


def product_nn(left, right):
    size = right[0].shape[1]
    wide = mul(left[0], beside(*right), NN)
    return wide[:, :size] + wide[:, size:] + mul(left[1], right[0], NN)


def product_tn(left, right):
    rows, cols = left[0].shape[1], right[0].shape[1]
    wide = mul(beside(*left), beside(*right), TN)
    return wide[:rows, :cols] + wide[:rows, cols:] + wide[rows:, :cols]


def state_operand(state, transposed):
    high, low = split(state)
    if transposed:
        return jnp.concatenate([beside(high, high), beside(low, jnp.zeros_like(low))], axis=0)
    return jnp.concatenate([beside(high, low), beside(high, jnp.zeros_like(low))], axis=0)


def product_state(left, operand, transposed):
    wide = mul(beside(*left), operand, NT if transposed else NN)
    return wide[:, :HD] + wide[:, HD:]


def heads(width):
    return [slice(h * HD, (h + 1) * HD) for h in range(width // HD)]


def blocks(rows):
    size = min(BLOCK, rows)
    return [slice(n * size, (n + 1) * size) for n in range(rows // size)]


def call(body, name, outs, flops, operands, scratch=(), hbm_in=(), hbm_out=(), aliases=None):
    outs = [out if isinstance(out[0], tuple) else (out, F32) for out in outs]
    outs = [
        pltpu.HBM(*out) if i in hbm_out else jax.ShapeDtypeStruct(*out) for i, out in enumerate(outs)
    ]
    moved = 2 * sum(x.size * x.dtype.itemsize for x in operands)
    operands = [
        pltpu.with_memory_space_constraint(x, pltpu.HBM) if i in hbm_in else x for i, x in enumerate(operands)
    ]
    place = lambda far: pl.BlockSpec(memory_space=pltpu.HBM if far else pltpu.VMEM)
    return pl.pallas_call(
        body,
        out_shape=outs,
        in_specs=[place(i in hbm_in) for i in range(len(operands))],
        out_specs=[place(i in hbm_out) for i in range(len(outs))],
        scratch_shapes=list(scratch),
        input_output_aliases=aliases or {},
        name=name,
        cost_estimate=pl.CostEstimate(flops=flops, bytes_accessed=moved, transcendentals=0),
        compiler_params=pltpu.CompilerParams(vmem_limit_bytes=16 * 1024 * 1024),
    )(*operands)


def my_core():
    return lax.axis_index("seq") % 2


def half_cols(half, mine, start=0, size=None):
    which = my_core() if mine else 1 - my_core()
    return pl.ds(pl.multiple_of(which * half + start, LANES), size or half)


def causal_mask(size, transposed=False):
    row = lax.broadcasted_iota(jnp.int32, (size, size), 0)
    col = lax.broadcasted_iota(jnp.int32, (size, size), 1)
    return row <= col if transposed else row >= col


def block_states(k_ref, v_ref, mine, total_ref, before_ref, ready=None):
    rows, width = k_ref.shape
    half = width // 2
    count = len(blocks(rows))
    for n, row in enumerate(blocks(rows)):
        if ready:
            ready(n)
        for head in heads(half):
            col = half_cols(half, mine, head.start, HD)
            state = product_tn(split(k_ref[row, col]), split(v_ref[row, col]))
            if n > 0:
                state = state + before_ref[n - 1, head, :]
            if n + 1 < count:
                before_ref[n, head, :] = state
            else:
                total_ref[head, :] = state


def key_states_other(k_hbm, v_hbm, gain_hbm, total_ref, before_ref, k_ref, v_ref, gain_ref, sems, gain_sem):
    gain_copy = pltpu.make_async_copy(gain_hbm, gain_ref, gain_sem)
    copies = []
    for n, row in enumerate(blocks(k_ref.shape[0])):
        copies.append([
            pltpu.make_async_copy(far.at[row], near.at[row], sems.at[i, n])
            for i, (far, near) in enumerate(((k_hbm, k_ref), (v_hbm, v_ref)))
        ])
        for copy in copies[n]:
            copy.start()
    gain_copy.start()

    def ready(n):
        for copy in copies[n]:
            copy.wait()

    block_states(k_ref, v_ref, False, total_ref, before_ref, ready)
    gain_copy.wait()


def key_states_mine(k_ref, v_ref, q_ref, cot_ref, gain_ref, total_ref, before_ref, mine_ref, other_ref):
    half = k_ref.shape[1] // 2
    block_states(k_ref, v_ref, True, total_ref, before_ref)
    for mine, pack_ref in ((True, mine_ref), (False, other_ref)):
        col = half_cols(half, mine)
        pack_ref[:, :half] = q_ref[:, col]
        pack_ref[:, half:] = gain_ref[:, col] * cot_ref[:, col]


def attend_local(pack_mine_ref, pack_other_ref, k_ref, v_ref, before_mine_ref, before_other_ref, mine_ref, other_ref):
    rows, width = k_ref.shape
    half = width // 2
    parts = ((False, pack_other_ref, before_other_ref, other_ref), (True, pack_mine_ref, before_mine_ref, mine_ref))
    for mine, pack_ref, before_ref, out_ref in parts:
        for head in heads(half):
            col = half_cols(half, mine, head.start, HD)
            for n, row in enumerate(blocks(rows)):
                query = split(pack_ref[row, head])
                scores = product_nt(query, split(k_ref[row, col]))
                scores = jnp.where(causal_mask(scores.shape[0]), scores, 0.0)
                out = product_nn(split(scores), split(v_ref[row, col]))
                if n > 0:
                    out = out + product_state(query, state_operand(before_ref[n - 1, head, :], False), False)
                out_ref[row, head] = out


def attend_state(own_ref, own_local_ref, sib_ref, sib_local_ref, keep_ref, give_ref, own_out_ref, sib_out_ref, sums_ref):
    rows, width = own_ref.shape
    half = width // 2
    count = rows // LANES
    lane = lax.broadcasted_iota(jnp.int32, (LANES, LANES), 1)
    for core, pack_ref, local_ref, state_ref, out_ref in (
        (my_core(), own_ref, own_local_ref, keep_ref, own_out_ref),
        (1 - my_core(), sib_ref, sib_local_ref, give_ref, sib_out_ref),
    ):
        tile = jnp.zeros((LANES, LANES), F32)
        states = [state_operand(state_ref[head, :], False) for head in heads(half)]
        for n, row in enumerate(blocks(rows)):
            for head, state in zip(heads(half), states):
                out_ref[row, head] = local_ref[row, head] + product_state(split(pack_ref[row, head]), state, False)
        for j in range(count):
            row = slice(j * LANES, (j + 1) * LANES)
            out = out_ref[row, :]
            squares = jnp.sum(out * out, axis=1, keepdims=True)
            cross = jnp.sum(pack_ref[row, half:] * out, axis=1, keepdims=True)
            tile = jnp.where(lane == j, squares, tile)
            tile = jnp.where(lane == count + j, cross, tile)
        sums_ref[pl.ds(pl.multiple_of(core * 2 * count, 2 * count), 2 * count), :] = tile.T[: 2 * count]


def row_factors(full_width, rows, given_ref, got_ref, own):
    count = rows // LANES
    core = my_core() if own else 1 - my_core()
    place = pl.ds(pl.multiple_of(core * 2 * count, 2 * count), 2 * count)
    sums = given_ref[place, :] + got_ref[place, :]
    inverse = lax.rsqrt(sums[:count] / full_width + 1e-06)
    factor = inverse * inverse * inverse * (sums[count:] / full_width)
    both = jnp.concatenate([inverse, factor], axis=0)
    tile = jnp.concatenate([both] * (LANES // both.shape[0]), axis=0).T
    return [(tile[:, j : j + 1], tile[:, count + j : count + j + 1]) for j in range(count)]


def grad_of_block(factors, scaled, attended, row):
    parts = []
    for i in range((row.stop - row.start) // LANES):
        part = slice(i * LANES, (i + 1) * LANES)
        inverse, factor = factors[row.start // LANES + i]
        parts.append(inverse * scaled[part] - attended[part] * factor)
    return jnp.concatenate(parts, axis=0)


def grad_states(full_width, given_ref, got_ref, own_ref, sib_ref, own_att_ref, sib_att_ref, pair_ref, own_total_ref, sib_total_ref, after_ref, high_ref, low_ref):
    rows, width = own_ref.shape
    half = width // 2
    for own, pack_ref, att_ref, total_ref in ((False, sib_ref, sib_att_ref, sib_total_ref), (True, own_ref, own_att_ref, own_total_ref)):
        factors = row_factors(full_width, rows, given_ref, got_ref, own)
        for head in heads(half):
            total = None
            for n, row in reversed(list(enumerate(blocks(rows)))):
                scaled = pack_ref[row, half + head.start : half + head.stop]
                grad = split(grad_of_block(factors, scaled, att_ref[row, head], row))
                if own:
                    high_ref[row, head], low_ref[row, head] = grad
                state = product_tn(split(pack_ref[row, head]), grad)
                total = state if total is None else total + state
                if own and n > 0:
                    after_ref[n - 1, head, :] = total
            total_ref[head, :] = total
    pair_ref[...] = own_total_ref[...] + sib_total_ref[...]


def grads_local(full_width, given_ref, got_ref, high_ref, low_ref, local_ref, pack_mine_ref, pack_other_ref, k_ref, v_ref, keep_ref, before_mine_ref, before_other_ref, total_ref, gq_hbm, gk_ref, gv_ref, after_ref, same_total_ref, gq_ref, other_high, other_low, sems):
    rows, width = k_ref.shape
    half = width // 2
    sums_rows = 4 * rows // LANES
    same_total_ref[...] = total_ref[...]
    factors = row_factors(full_width, rows, given_ref, got_ref, True)
    copies = []
    for mine in (True, False):
        pack_ref, before_ref = (pack_mine_ref, before_mine_ref) if mine else (pack_other_ref, before_other_ref)
        for head in heads(half):
            col = half_cols(half, mine, head.start, HD)
            if mine:
                state = keep_ref[head, :]
            else:
                state = got_ref[sums_rows + head.start : sums_rows + head.stop, :]
                operand = state_operand(state, False)
                total = None
            for n, row in reversed(list(enumerate(blocks(rows)))):
                if mine:
                    grad = high_ref[row, head], low_ref[row, head]
                else:
                    query = split(pack_ref[row, head])
                    attended = local_ref[row, head] + product_state(query, operand, False)
                    scaled = pack_ref[row, half + head.start : half + head.stop]
                    grad = split(grad_of_block(factors, scaled, attended, row))
                    other_high[row, head], other_low[row, head] = grad
                    if n > 0:
                        more = product_tn(query, grad)
                        total = more if total is None else total + more
                        after_ref[n - 1, head, :] = total
                here = state_operand(state if n == 0 else state + before_ref[n - 1, head, :], True)
                mixing = product_nt(grad, split(v_ref[row, col]))
                mixing = jnp.where(causal_mask(row.stop - row.start), mixing, 0.0)
                gq_ref[row, col] = product_nn(split(mixing), split(k_ref[row, col])) + product_state(grad, here, True)
                copies.append(pltpu.make_async_copy(gq_ref.at[row, col], gq_hbm.at[row, col], sems.at[len(copies)]))
                copies[-1].start()
    for mine in (True, False):
        pack_ref = pack_mine_ref if mine else pack_other_ref
        for head in heads(half):
            col = half_cols(half, mine, head.start, HD)
            place = head if mine else slice(half + head.start, half + head.stop)
            for row in blocks(rows):
                grad = (high_ref[row, head], low_ref[row, head]) if mine else (other_high[row, head], other_low[row, head])
                query, key, value = split(pack_ref[row, head]), split(k_ref[row, col]), split(v_ref[row, col])
                mask = causal_mask(row.stop - row.start, True)
                mixing = jnp.where(mask, product_nt(value, grad), 0.0)
                gk_ref[row, place] = product_nn(split(mixing), query)
                scores = jnp.where(mask, product_nt(key, query), 0.0)
                gv_ref[row, place] = product_nn(split(scores), grad)
    for copy in copies:
        copy.wait()


def grads_state(mine, k_ref, v_ref, gk_local_ref, gv_local_ref, state_ref, after_ref, *refs):
    gk_hbm, gv_hbm, gk_ref, gv_ref, sems = refs[-5:]
    rows, width = k_ref.shape
    half = width // 2
    last = len(blocks(rows)) - 1
    copies = []

    def leave(near, far, row, head, col):
        copies.append(pltpu.make_async_copy(near.at[row, head], far.at[row, col], sems.at[len(copies)]))
        copies[-1].start()

    for head in heads(half):
        col = half_cols(half, mine, head.start, HD)
        place = head if mine else slice(half + head.start, half + head.stop)
        for n, row in enumerate(blocks(rows)):
            here = state_ref[head, :] if n == last else state_ref[head, :] + after_ref[n, head, :]
            gk_ref[row, head] = gk_local_ref[row, place] + product_state(split(v_ref[row, col]), state_operand(here, True), True)
            leave(gk_ref, gk_hbm, row, head, col)
            gv_ref[row, head] = gv_local_ref[row, place] + product_state(split(k_ref[row, col]), state_operand(here, False), False)
            leave(gv_ref, gv_hbm, row, head, col)
    for copy in copies:
        copy.wait()


def swap(x, axis, distance):
    count = lax.axis_size(axis)
    return lax.ppermute(x, axis, [(i, i ^ distance) for i in range(count)])


def from_other_chips(pair, reverse):
    chip = lax.axis_index("seq") // 2
    chips = lax.axis_size("seq") // 2
    total = jnp.zeros_like(pair)
    ahead = lambda d: (chip ^ d) > chip if reverse else (chip ^ d) < chip
    if chips <= 4:
        got = [(d, swap(pair, "seq", 2 * d)) for d in reversed(range(1, chips))]
        for d, part in got:
            total = total + jnp.where(ahead(d), part, 0.0)
        return total
    d = 1
    while d < chips:
        part = swap(pair, "seq", 2 * d)
        total = total + jnp.where(ahead(d), part, 0.0)
        pair = pair + part
        d *= 2
    return total


def sum_over_heads(x):
    count = lax.axis_size("head")
    if count > 4 or count & (count - 1):
        return lax.psum(x, "head")
    parts = [swap(x, "head", d) for d in reversed(range(1, count))]
    for part in parts:
        x = x + part
    return x


def shards(queries, keys, values, cotangent, gain):
    rows, width = queries.shape
    full_width = width * lax.axis_size("head")
    half = width // 2
    count = len(blocks(rows))
    units = count * (width // HD)
    square = rows * width * HD * 2 * 3
    whole, halves, state = (rows, width), (rows, half), (half, HD)
    inner = (max(count - 1, 1), half, HD)
    first = lax.axis_index("seq") % 2 == 0
    gain = gain.reshape(1, width)

    other, before_other, near_keys, near_values, gain = call(
        key_states_other, "key_states_other", [state, inner, whole, whole, (1, width)], square // 2,
        [keys, values, gain], [pltpu.SemaphoreType.DMA((2, count)), pltpu.SemaphoreType.DMA], hbm_in=(0, 1, 2),
    )
    from_pair = swap(other, "seq", 1)
    mine, before_mine, pack_mine, pack_other = call(
        key_states_mine, "key_states_mine", [state, inner, whole, whole], square // 2,
        [near_keys, near_values, queries, cotangent, gain],
    )
    sibling = swap(pack_other, "seq", 1)
    earlier = from_other_chips(mine + from_pair, False)
    keep = earlier + jnp.where(first, 0.0, from_pair)
    give = earlier + jnp.where(first, mine, 0.0)
    local_mine, local_other = call(
        attend_local, "attend_local", [halves, halves], 5 * square,
        [pack_mine, pack_other, near_keys, near_values, before_mine, before_other],
    )
    sibling_local = swap(local_other, "seq", 1)
    attended, sibling_attended, sums = call(
        attend_state, "attend_state", [halves, halves, (4 * rows // LANES, LANES)], square,
        [pack_mine, local_mine, sibling, sibling_local, keep, give],
    )
    given = jnp.concatenate([sum_over_heads(sums), give], axis=0)
    got = swap(given, "seq", 1)
    pair, own_grad, sibling_grad, after_mine, high, low = call(
        functools.partial(grad_states, full_width), "grad_states",
        [state, state, state, inner, (halves, BF16), (halves, BF16)], square,
        [given, got, pack_mine, sibling, attended, sibling_attended],
    )
    later = from_other_chips(pair, True)
    grad_q, local_k, local_v, after_other, own_grad = call(
        functools.partial(grads_local, full_width), "grads_local", [whole, whole, whole, inner, state], 14 * square,
        [given, got, high, low, local_other, pack_mine, pack_other, keys, values, keep, before_mine, before_other, own_grad],
        [pltpu.VMEM(whole, F32), pltpu.VMEM(halves, BF16), pltpu.VMEM(halves, BF16), pltpu.SemaphoreType.DMA((units,))],
        hbm_out=(0,),
    )
    keep_later = later + jnp.where(first, sibling_grad, 0.0)
    got_later = swap(later + jnp.where(first, 0.0, own_grad), "seq", 1)
    scratch = [pltpu.VMEM(halves, F32), pltpu.VMEM(halves, F32), pltpu.SemaphoreType.DMA((units,))]
    grad_k, grad_v = call(
        functools.partial(grads_state, True), "grads_state_mine", [whole] * 2, square,
        [keys, values, local_k, local_v, keep_later, after_mine], scratch, hbm_out=(0, 1),
    )
    grad_k, grad_v = call(
        functools.partial(grads_state, False), "grads_state_other", [whole] * 2, square,
        [keys, values, local_k, local_v, got_later, after_other, grad_k, grad_v], scratch,
        hbm_in=(6, 7), hbm_out=(0, 1), aliases={6: 0, 7: 1},
    )
    return grad_q, grad_k, grad_v


def solution(mesh):
    in_specs = (P("seq", "head"), P("seq", "head"), P("seq", "head"), P("seq", "head"), P("head"))
    out_specs = (P("seq", "head"), P("seq", "head"), P("seq", "head"))
    return jax.shard_map(shards, mesh=mesh, in_specs=in_specs, out_specs=out_specs, check_vma=False)
```

time: 120 us -> 33.2 us (0.28)
  waiting for transfers between devices: 38.6 us -> 8.18 us
  matrix products: 30.1 us -> 0 us
  local copies, waits for them, and re-layouts: 13.9 us -> 0.02 us
  starting transfers between devices: 0.08 us -> 13.7 us
  between operations: 14.2 us -> 0.81 us
  blocking collectives: 11.9 us -> 0 us
  Pallas kernels: 0 us -> 10.2 us
  other arithmetic: 10.2 us -> 0.09 us
    all_gather x2 -> x0, waiting for transfers between devices: 38.6 us -> none  [carried_in(): gathered = lax.all_gather(part, axis)]
    dot_general x12 -> x0, matrix products: 30.1 us -> none  [product(): return jnp.einsum(form, left, right, precision=lax.Precision.HIGHEST)]
    ppermute x0 -> x14, starting transfers between devices: none -> 13.7 us  [swap(): return lax.ppermute(x, axis, [(i, i ^ distance) for i in range(count)])]
    psum x1 -> x0, blocking collectives: 11.9 us -> none  [shards(): squares_sum, cross_sum = lax.psum((squares_part, cross_part), 'head')]
    pallas_call x0 -> x8, Pallas kernels: none -> 10.2 us  [call(): pl.pallas_call(body, out_shape=outs, in_specs=[place(i in hbm_in) for i i...]
    ppermute x0 -> x14, waiting for transfers between devices: none -> 8.18 us  [swap(): return lax.ppermute(x, axis, [(i, i ^ distance) for i in range(count)])]
    reshape x5 -> x0, local copies, waits for them, and re-layouts: 7.96 us -> none  [the longest x4 5.92 us: to_blocks(): array.reshape(tok_rows // block, block, width_here // HD, HD)]
    add x7 -> x6, other arithmetic: 6.56 us -> 0.08 us  [the longest x1 0.03 us: shards(): keep_later = later + jnp.where(first, sibling_grad, 0.0)]
  transfers between devices with their start and end apart: 2 -> 14, of which waited for: 2 -> 8; matrix products, arithmetic and copies ran while one was open for 12% -> 0% of each run, Pallas kernels for 0% -> 19%
where the time goes in v3:
time: 33.2 us; the launch traced here: 33.1 us
  starting transfers between devices  13.7 us (41%)
  Pallas kernels  10.2 us (31%)
  waiting for transfers between devices  8.18 us (25%)
  between operations  0.81 us (2%)
    ppermute x14, starting transfers between devices, swap(): return lax.ppermute(x, axis, [(i, i ^ distance) for i in range(count)])  13.7 us
    pallas_call x8, Pallas kernels, call(): pl.pallas_call(body, out_shape=outs, in_specs=[place(i in hbm_in) for i i...  10.2 us
    ppermute x14, waiting for transfers between devices, swap(): return lax.ppermute(x, axis, [(i, i ^ distance) for i in range(count)])  8.18 us
  transfers between devices with their start and end apart: 14, of which 8 were waited for; matrix products, arithmetic and copies ran while one was open for 0% of the time, Pallas kernels for 19%

profile of v3, /device:TPU:0, one launch (start us, length us, event | category | flops | bytes accessed | tf_op | source)
XLA Modules:
  0.0 33.1 jit_solution(3406694783875781672)
XLA Ops:
  0.7 1.6 %key_states_other.1 = (f32[128,128]{1,0:T(8,128)S(1)}, f32[1,128,128]{2,1,0:T(8,128)S(1)}, f32[512,256]{1,0:T(8,128)S(1)}, f32[512,256]{1,0:T(8,128)S(1)}, f32[1,256]{1,0:T(1,128)S(1)}) custom-call(f32[512,256]{1,0:T(8,128)} %k_ref.5, f32[512,256]{1,0:T(8,128)} %v_ref.5, f32[1,256]{1,0:T(1,128)} %bitcast.1), custom_call_target="tpu_custom_call" | custom-call | flops 50331648 | bytes 2099200 | tf_op jit(solution)/shard_map/key_states_other/pallas_call | solution.py:79
  2.3 0.5 %collective-permute-start.2 = (f32[128,128]{1,0:T(8,128)S(1)}, f32[128,128]{1,0:T(8,128)S(1)}, u32[]{:S(2)}, u32[]{:S(2)}) collective-permute-start(f32[128,128]{1,0:T(8,128)S(1)} %get-tuple-element.42), channel_id=1, source_target_pairs={{0,4},{4,0},{8,12},{12,8},{16,20},{20,16},{24,28},{28,24},{1,5},{5... | collective-permute-start | bytes 196616 | tf_op jit(solution)/shard_map/ppermute | solution.py:315
  2.8 0.3 %key_states_mine.1 = (f32[128,128]{1,0:T(8,128)S(1)}, f32[1,128,128]{2,1,0:T(8,128)S(1)}, f32[512,256]{1,0:T(8,128)S(1)}, f32[512,256]{1,0:T(8,128)S(1)}) custom-call(f32[512,256]{1,0:T(8,128)S(1)} %get-tuple-element.32.k_ref, f32[512,256]{1,0:T(8,128)S(1)} %get-tuple-element.33.v_ref, f32[512,256]{1,0:T(8,128)S(1)} %copy-done.2, f32[512,256]{1,0:T(8,128)S(1)} %copy-done.3, ...), custom_call_target="tpu_custom_call" | custom-call | flops 50331648 | bytes 4196352 | tf_op jit(solution)/shard_map/key_states_mine/pallas_call | solution.py:79
  3.2 0.6 %collective-permute-done.2 = f32[128,128]{1,0:T(8,128)S(1)} collective-permute-done((f32[128,128]{1,0:T(8,128)S(1)}, f32[128,128]{1,0:T(8,128)S(1)}, u32[]{:S(2)}, u32[]{:S(2)}) %collective-permute-start.2) | collective-permute-done | bytes 65568 | tf_op jit(solution)/shard_map/ppermute | solution.py:315
  3.7 3.9 %collective-permute-start.3 = (f32[128,128]{1,0:T(8,128)S(1)}, f32[128,128]{1,0:T(8,128)S(1)}, u32[]{:S(2)}, u32[]{:S(2)}) collective-permute-start(f32[128,128]{1,0:T(8,128)S(1)} %add.41), channel_id=1, source_target_pairs={{0,24},{4,28},{8,16},{12,20},{16,8},{20,12},{24,0},{28,4},{1,25},{... | collective-permute-start | bytes 196616 | tf_op jit(solution)/shard_map/ppermute | solution.py:315
  7.6 0.5 %collective-permute-start.4 = (f32[128,128]{1,0:T(8,128)S(1)}, f32[128,128]{1,0:T(8,128)S(1)}, u32[]{:S(2)}, u32[]{:S(2)}) collective-permute-start(f32[128,128]{1,0:T(8,128)S(1)} %add.41), channel_id=1, source_target_pairs={{0,16},{4,20},{8,24},{12,28},{16,0},{20,4},{24,8},{28,12},{1,17},{... | collective-permute-start | bytes 196616 | tf_op jit(solution)/shard_map/ppermute | solution.py:315
  8.2 1.1 %attend_local.1 = (f32[512,128]{1,0:T(8,128)S(1)}, f32[512,128]{1,0:T(8,128)S(1)}) custom-call(f32[512,256]{1,0:T(8,128)S(1)} %get-tuple-element.35.pack_mine_ref.own_ref, f32[512,256]{1,0:T(8,128)S(1)} %get-tuple-element.36.pack_other_ref, f32[512,256]{1,0:T(8,128)S(1)} %get-tuple-element.32.k_ref, f32[512,256]{1,0:T(8,128)S(1)} %get-tuple-element.33.v_ref, ...), custom_call_target="tpu_custom_call" | custom-call | flops 503316480 | bytes 4456448 | tf_op jit(solution)/shard_map/attend_local/pallas_call | solution.py:79
  9.3 0.6 %collective-permute-start.1 = (f32[512,128]{1,0:T(8,128)S(1)}, f32[512,128]{1,0:T(8,128)S(1)}, u32[]{:S(2)}, u32[]{:S(2)}) collective-permute-start(f32[512,128]{1,0:T(8,128)S(1)} %get-tuple-element.40.local_ref), channel_id=1, source_target_pairs={{0,4},{4,0},{8,12},{12,8},{16,20},{20,16},{24,28},{28,24},{1,5},{5... | collective-permute-start | bytes 786440 | tf_op jit(solution)/shard_map/ppermute | solution.py:315
  10.0 1.9 %collective-permute-done.4 = f32[128,128]{1,0:T(8,128)S(1)} collective-permute-done((f32[128,128]{1,0:T(8,128)S(1)}, f32[128,128]{1,0:T(8,128)S(1)}, u32[]{:S(2)}, u32[]{:S(2)}) %collective-permute-start.4) | collective-permute-done | bytes 65568 | tf_op jit(solution)/shard_map/ppermute | solution.py:315
  11.9 0.5 %collective-permute-done.5 = f32[128,128]{1,0:T(8,128)S(1)} collective-permute-done((f32[128,128]{1,0:T(8,128)S(1)}, f32[128,128]{1,0:T(8,128)S(1)}, u32[]{:S(2)}, u32[]{:S(2)}) %collective-permute-start.5) | collective-permute-done | bytes 65568 | tf_op jit(solution)/shard_map/ppermute | solution.py:315
  12.4 0.6 %attend_state.1 = (f32[512,128]{1,0:T(8,128)S(1)}, f32[512,128]{1,0:T(8,128)S(1)}, f32[16,128]{1,0:T(8,128)S(1)}) custom-call(f32[512,256]{1,0:T(8,128)S(1)} %get-tuple-element.35.pack_mine_ref.own_ref, f32[512,128]{1,0:T(8,128)S(1)} %get-tuple-element.39.own_local_ref, f32[512,256]{1,0:T(8,128)S(1)} %collective-permute-done.sib_ref, ...), custom_call_target="tpu_custom_call" | custom-call | flops 100663296 | bytes 3407872 | tf_op jit(solution)/shard_map/attend_state/pallas_call | solution.py:79
  13.0 3.6 %collective-permute-start.6 = (f32[16,128]{1,0:T(8,128)S(1)}, f32[16,128]{1,0:T(8,128)S(1)}, u32[]{:S(2)}, u32[]{:S(2)}) collective-permute-start(f32[16,128]{1,0:T(8,128)S(1)} %get-tuple-element.43), channel_id=1, source_target_pairs={{0,3},{1,2},{2,1},{3,0},{4,7},{5,6},{6,5},{7,4},{8,11},{9,10},{10,... | collective-permute-start | bytes 24584 | tf_op jit(solution)/shard_map/ppermute | solution.py:315
  16.7 0.8 %collective-permute-start.8 = (f32[16,128]{1,0:T(8,128)S(1)}, f32[16,128]{1,0:T(8,128)S(1)}, u32[]{:S(2)}, u32[]{:S(2)}) collective-permute-start(f32[16,128]{1,0:T(8,128)S(1)} %get-tuple-element.43), channel_id=1, source_target_pairs={{0,1},{1,0},{2,3},{3,2},{4,5},{5,4},{6,7},{7,6},{8,9},{9,8},{10,11... | collective-permute-start | bytes 24584 | tf_op jit(solution)/shard_map/ppermute | solution.py:315
  17.5 1.1 %collective-permute-done.6 = f32[16,128]{1,0:T(8,128)S(1)} collective-permute-done((f32[16,128]{1,0:T(8,128)S(1)}, f32[16,128]{1,0:T(8,128)S(1)}, u32[]{:S(2)}, u32[]{:S(2)}) %collective-permute-start.6) | collective-permute-done | bytes 8224 | tf_op jit(solution)/shard_map/ppermute | solution.py:315
  18.6 2.6 %collective-permute-done.7 = f32[16,128]{1,0:T(8,128)S(1)} collective-permute-done((f32[16,128]{1,0:T(8,128)S(1)}, f32[16,128]{1,0:T(8,128)S(1)}, u32[]{:S(2)}, u32[]{:S(2)}) %collective-permute-start.7) | collective-permute-done | bytes 8224 | tf_op jit(solution)/shard_map/ppermute | solution.py:315
  21.3 1.2 %collective-permute-done.9.got_ref = f32[144,128]{1,0:T(8,128)S(1)} collective-permute-done((f32[144,128]{1,0:T(8,128)S(1)}, f32[144,128]{1,0:T(8,128)S(1)}, u32[]{:S(2)}, u32[]{:S(2)}) %collective-permute-start.9) | collective-permute-done | bytes 73760 | tf_op jit(solution)/shard_map/ppermute | solution.py:315
  22.6 0.8 %grad_states.1 = (f32[128,128]{1,0:T(8,128)S(1)}, f32[128,128]{1,0:T(8,128)S(1)}, f32[128,128]{1,0:T(8,128)S(1)}, f32[1,128,128]{2,1,0:T(8,128)S(1)}, bf16[512,1...) custom-call(f32[144,128]{1,0:T(8,128)S(1)} %pad_maximum_fusion.given_ref, ...), custom_call_target="tpu_custom_call" | custom-call | flops 100663296 | bytes 3440640 | tf_op jit(solution)/shard_map/grad_states/pallas_call | solution.py:79
  23.4 1.6 %collective-permute-start.10 = (f32[128,128]{1,0:T(8,128)S(1)}, f32[128,128]{1,0:T(8,128)S(1)}, u32[]{:S(2)}, u32[]{:S(2)}) collective-permute-start(f32[128,128]{1,0:T(8,128)S(1)} %get-tuple-element.52), channel_id=1, source_target_pairs={{0,24},{4,28},{8,16},{12,20},{16,8},{20,12},{24,0},{28,4},{1,25},{... | collective-permute-start | bytes 196616 | tf_op jit(solution)/shard_map/ppermute | solution.py:315
  24.9 0.7 %collective-permute-start.11 = (f32[128,128]{1,0:T(8,128)S(1)}, f32[128,128]{1,0:T(8,128)S(1)}, u32[]{:S(2)}, u32[]{:S(2)}) collective-permute-start(f32[128,128]{1,0:T(8,128)S(1)} %get-tuple-element.52), channel_id=1, source_target_pairs={{0,16},{4,20},{8,24},{12,28},{16,0},{20,4},{24,8},{28,12},{1,17},{... | collective-permute-start | bytes 196616 | tf_op jit(solution)/shard_map/ppermute | solution.py:315
  25.7 1.2 %collective-permute-start.12 = (f32[128,128]{1,0:T(8,128)S(1)}, f32[128,128]{1,0:T(8,128)S(1)}, u32[]{:S(2)}, u32[]{:S(2)}) collective-permute-start(f32[128,128]{1,0:T(8,128)S(1)} %get-tuple-element.52), channel_id=1, source_target_pairs={{0,8},{4,12},{8,0},{12,4},{16,24},{20,28},{24,16},{28,20},{1,9},{5... | collective-permute-start | bytes 196616 | tf_op jit(solution)/shard_map/ppermute | solution.py:315
  26.9 3.6 %grads_local.1 = (f32[512,256]{1,0:T(8,128)}, f32[512,256]{1,0:T(8,128)S(1)}, f32[512,256]{1,0:T(8,128)S(1)}, f32[1,128,128]{2,1,0:T(8,128)S(1)}, f32[128,128]{1,0:T(8,128)S(1)}) custom-call(f32[144,128]{1,0:T(8,128)S(1)} %pad_maximum_fusion.given_ref, f32[144,128]{1,0:T(8,128)S(1)} %collective-permute-done.9.got_ref, ...), custom_call_target="tpu_custom_call" | custom-call | flops 1409286144 | bytes 6062080 | tf_op jit(solution)/shard_map/grads_local/pallas_call | solution.py:79
  30.7 1.1 %grads_state_mine.1 = (f32[512,256]{1,0:T(8,128)}, f32[512,256]{1,0:T(8,128)}) custom-call(f32[512,256]{1,0:T(8,128)S(1)} %copy-done, f32[512,256]{1,0:T(8,128)S(1)} %copy-done.1, f32[512,256]{1,0:T(8,128)S(1)} %get-tuple-element.50.gk_local_ref, f32[512,256]{1,0:T(8,128)S(1)} %get-tuple-element.51.gv_local_ref, f32[128,128]{1,0:T(8,128)S(1)} %get-tuple-element.61.state_ref, ...), custom_call_target="tpu_custom_call" | custom-call | flops 100663296 | bytes 4456448 | tf_op jit(solution)/shard_map/grads_state_mine/pallas_call | solution.py:79
  31.8 0.1 collective-permute-done.13.state_ref
  32.0 1.1 %grads_state_other.1 = (f32[512,256]{1,0:T(8,128)}, f32[512,256]{1,0:T(8,128)}) custom-call(f32[512,256]{1,0:T(8,128)S(1)} %copy-done, f32[512,256]{1,0:T(8,128)S(1)} %copy-done.1, f32[512,256]{1,0:T(8,128)S(1)} %get-tuple-element.50.gk_local_ref, f32[512,256]{1,0:T(8,128)S(1)} %get-tuple-element.51.gv_local_ref, ...), custom_call_target="tpu_custom_call", output_to_operand_aliasing={{0}: (6, {}), {1}: (7, {})} | custom-call | flops 100663296 | bytes 6553600 | tf_op jit(solution)/shard_map/grads_state_other/pallas_call | solution.py:79
  (27 shorter events, 0.5 us)
Async XLA Ops:
  0.6 2.2 %copy-start.2 = (f32[512,256]{1,0:T(8,128)S(1)}, f32[512,256]{1,0:T(8,128)}, u32[]{:S(2)}) copy-start(f32[512,256]{1,0:T(8,128)} %q_ref.1) | copy-start | bytes 1572868
  0.6 2.2 %copy-start.3 = (f32[512,256]{1,0:T(8,128)S(1)}, f32[512,256]{1,0:T(8,128)}, u32[]{:S(2)}) copy-start(f32[512,256]{1,0:T(8,128)} %cot_ref.1) | copy-start | bytes 1572868
  2.3 1.4 %collective-permute-start.2 = (f32[128,128]{1,0:T(8,128)S(1)}, f32[128,128]{1,0:T(8,128)S(1)}, u32[]{:S(2)}, u32[]{:S(2)}) collective-permute-start(f32[128,128]{1,0:T(8,128)S(1)} %get-tuple-element.42), channel_id=1, source_target_pairs={{0,4},{4,0},{8,12},{12,8},{16,20},{20,16},{24,28},{28,24},{1,5},{5... | collective-permute-start | bytes 196616 | tf_op jit(solution)/shard_map/ppermute | solution.py:315
  3.7 6.3 %collective-permute-start.3 = (f32[128,128]{1,0:T(8,128)S(1)}, f32[128,128]{1,0:T(8,128)S(1)}, u32[]{:S(2)}, u32[]{:S(2)}) collective-permute-start(f32[128,128]{1,0:T(8,128)S(1)} %add.41), channel_id=1, source_target_pairs={{0,24},{4,28},{8,16},{12,20},{16,8},{20,12},{24,0},{28,4},{1,25},{... | collective-permute-start | bytes 196616 | tf_op jit(solution)/shard_map/ppermute | solution.py:315
  7.6 4.3 %collective-permute-start.4 = (f32[128,128]{1,0:T(8,128)S(1)}, f32[128,128]{1,0:T(8,128)S(1)}, u32[]{:S(2)}, u32[]{:S(2)}) collective-permute-start(f32[128,128]{1,0:T(8,128)S(1)} %add.41), channel_id=1, source_target_pairs={{0,16},{4,20},{8,24},{12,28},{16,0},{20,4},{24,8},{28,12},{1,17},{... | collective-permute-start | bytes 196616 | tf_op jit(solution)/shard_map/ppermute | solution.py:315
  8.1 4.3 %collective-permute-start.5 = (f32[128,128]{1,0:T(8,128)S(1)}, f32[128,128]{1,0:T(8,128)S(1)}, u32[]{:S(2)}, u32[]{:S(2)}) collective-permute-start(f32[128,128]{1,0:T(8,128)S(1)} %add.41), channel_id=1, source_target_pairs={{0,8},{4,12},{8,0},{12,4},{16,24},{20,28},{24,16},{28,20},{1,9},{5... | collective-permute-start | bytes 196616 | tf_op jit(solution)/shard_map/ppermute | solution.py:315
  8.2 4.2 %collective-permute-start = (f32[512,256]{1,0:T(8,128)S(1)}, f32[512,256]{1,0:T(8,128)S(1)}, u32[]{:S(2)}, u32[]{:S(2)}) collective-permute-start(f32[512,256]{1,0:T(8,128)S(1)} %get-tuple-element.36.pack_other_ref), channel_id=1, source_target_pairs={{0,4},{4,0},{8,12},{12,8},{16,20},{20,16},{24,28},{28,24},{1,5},{5... | collective-permute-start | bytes 1572872 | tf_op jit(solution)/shard_map/ppermute | solution.py:315
  9.3 3.1 %collective-permute-start.1 = (f32[512,128]{1,0:T(8,128)S(1)}, f32[512,128]{1,0:T(8,128)S(1)}, u32[]{:S(2)}, u32[]{:S(2)}) collective-permute-start(f32[512,128]{1,0:T(8,128)S(1)} %get-tuple-element.40.local_ref), channel_id=1, source_target_pairs={{0,4},{4,0},{8,12},{12,8},{16,20},{20,16},{24,28},{28,24},{1,5},{5... | collective-permute-start | bytes 786440 | tf_op jit(solution)/shard_map/ppermute | solution.py:315
  13.0 5.5 %collective-permute-start.6 = (f32[16,128]{1,0:T(8,128)S(1)}, f32[16,128]{1,0:T(8,128)S(1)}, u32[]{:S(2)}, u32[]{:S(2)}) collective-permute-start(f32[16,128]{1,0:T(8,128)S(1)} %get-tuple-element.43), channel_id=1, source_target_pairs={{0,3},{1,2},{2,1},{3,0},{4,7},{5,6},{6,5},{7,4},{8,11},{9,10},{10,... | collective-permute-start | bytes 24584 | tf_op jit(solution)/shard_map/ppermute | solution.py:315
  16.7 4.5 %collective-permute-start.7 = (f32[16,128]{1,0:T(8,128)S(1)}, f32[16,128]{1,0:T(8,128)S(1)}, u32[]{:S(2)}, u32[]{:S(2)}) collective-permute-start(f32[16,128]{1,0:T(8,128)S(1)} %get-tuple-element.43), channel_id=1, source_target_pairs={{0,2},{1,3},{2,0},{3,1},{4,6},{5,7},{6,4},{7,5},{8,10},{9,11},{10,... | collective-permute-start | bytes 24584 | tf_op jit(solution)/shard_map/ppermute | solution.py:315
  16.7 4.5 %collective-permute-start.8 = (f32[16,128]{1,0:T(8,128)S(1)}, f32[16,128]{1,0:T(8,128)S(1)}, u32[]{:S(2)}, u32[]{:S(2)}) collective-permute-start(f32[16,128]{1,0:T(8,128)S(1)} %get-tuple-element.43), channel_id=1, source_target_pairs={{0,1},{1,0},{2,3},{3,2},{4,5},{5,4},{6,7},{7,6},{8,9},{9,8},{10,11... | collective-permute-start | bytes 24584 | tf_op jit(solution)/shard_map/ppermute | solution.py:315
  21.3 1.3 %collective-permute-start.9 = (f32[144,128]{1,0:T(8,128)S(1)}, f32[144,128]{1,0:T(8,128)S(1)}, u32[]{:S(2)}, u32[]{:S(2)}) collective-permute-start(f32[144,128]{1,0:T(8,128)S(1)} %pad_maximum_fusion.given_ref), channel_id=1, source_target_pairs={{0,4},{4,0},{8,12},{12,8},{16,20},{20,16},{24,28},{28,24},{1,5},{5... | collective-permute-start | bytes 221192 | tf_op jit(solution)/shard_map/ppermute | solution.py:315
  22.6 4.3 %copy-start = (f32[512,256]{1,0:T(8,128)S(1)}, f32[512,256]{1,0:T(8,128)}, u32[]{:S(2)}) copy-start(f32[512,256]{1,0:T(8,128)} %k_ref.5) | copy-start | bytes 1572868
  22.6 4.3 %copy-start.1 = (f32[512,256]{1,0:T(8,128)S(1)}, f32[512,256]{1,0:T(8,128)}, u32[]{:S(2)}) copy-start(f32[512,256]{1,0:T(8,128)} %v_ref.5) | copy-start | bytes 1572868
  23.4 7.2 %collective-permute-start.10 = (f32[128,128]{1,0:T(8,128)S(1)}, f32[128,128]{1,0:T(8,128)S(1)}, u32[]{:S(2)}, u32[]{:S(2)}) collective-permute-start(f32[128,128]{1,0:T(8,128)S(1)} %get-tuple-element.52), channel_id=1, source_target_pairs={{0,24},{4,28},{8,16},{12,20},{16,8},{20,12},{24,0},{28,4},{1,25},{... | collective-permute-start | bytes 196616 | tf_op jit(solution)/shard_map/ppermute | solution.py:315
  24.9 5.6 %collective-permute-start.11 = (f32[128,128]{1,0:T(8,128)S(1)}, f32[128,128]{1,0:T(8,128)S(1)}, u32[]{:S(2)}, u32[]{:S(2)}) collective-permute-start(f32[128,128]{1,0:T(8,128)S(1)} %get-tuple-element.52), channel_id=1, source_target_pairs={{0,16},{4,20},{8,24},{12,28},{16,0},{20,4},{24,8},{28,12},{1,17},{... | collective-permute-start | bytes 196616 | tf_op jit(solution)/shard_map/ppermute | solution.py:315
  25.7 4.9 %collective-permute-start.12 = (f32[128,128]{1,0:T(8,128)S(1)}, f32[128,128]{1,0:T(8,128)S(1)}, u32[]{:S(2)}, u32[]{:S(2)}) collective-permute-start(f32[128,128]{1,0:T(8,128)S(1)} %get-tuple-element.52), channel_id=1, source_target_pairs={{0,8},{4,12},{8,0},{12,4},{16,24},{20,28},{24,16},{28,20},{1,9},{5... | collective-permute-start | bytes 196616 | tf_op jit(solution)/shard_map/ppermute | solution.py:315
  30.7 1.3 %collective-permute-start.13 = (f32[128,128]{1,0:T(8,128)S(1)}, f32[128,128]{1,0:T(8,128)S(1)}, u32[]{:S(2)}, u32[]{:S(2)}) collective-permute-start(f32[128,128]{1,0:T(8,128)S(1)} %select_add_fusion.1), channel_id=1, source_target_pairs={{0,4},{4,0},{8,12},{12,8},{16,20},{20,16},{24,28},{28,24},{1,5},{5... | collective-permute-start | bytes 196616 | tf_op jit(solution)/shard_map/ppermute | solution.py:315

commit v4 on v3

--- a/solution.py
+++ b/solution.py
@@ -93,8 +93,17 @@
     return lax.axis_index("seq") % 2
 
 
+def on_grid():
+    return lax.axis_size("seq") == 8
+
+
+def my_half():
+    place = lax.axis_index("seq")
+    return (place + place // 2) % 2 if on_grid() else place % 2
+
+
 def half_cols(half, mine, start=0, size=None):
-    which = my_core() if mine else 1 - my_core()
+    which = my_half() if mine else 1 - my_half()
     return pl.ds(pl.multiple_of(which * half + start, LANES), size or half)
 
 
@@ -192,11 +201,20 @@
         sums_ref[pl.ds(pl.multiple_of(core * 2 * count, 2 * count), 2 * count), :] = tile.T[: 2 * count]
 
 
-def row_factors(full_width, rows, given_ref, got_ref, own):
+def attend_other(pair_sums_ref, got_ref, pack_ref, local_ref, out_ref, same_sums_ref):
+    same_sums_ref[...] = pair_sums_ref[...]
+    start = pair_sums_ref.shape[0]
+    rows, half = local_ref.shape
+    for head in heads(half):
+        operand = state_operand(got_ref[start + head.start : start + head.stop, :], False)
+        for row in blocks(rows):
+            out_ref[row, head] = local_ref[row, head] + product_state(split(pack_ref[row, head]), operand, False)
+
+
+def row_factors(full_width, rows, sums_ref, own):
     count = rows // LANES
     core = my_core() if own else 1 - my_core()
-    place = pl.ds(pl.multiple_of(core * 2 * count, 2 * count), 2 * count)
-    sums = given_ref[place, :] + got_ref[place, :]
+    sums = sums_ref[pl.ds(pl.multiple_of(core * 2 * count, 2 * count), 2 * count), :]
     inverse = lax.rsqrt(sums[:count] / full_width + 1e-06)
     factor = inverse * inverse * inverse * (sums[count:] / full_width)
     both = jnp.concatenate([inverse, factor], axis=0)
@@ -213,11 +231,11 @@
     return jnp.concatenate(parts, axis=0)
 
 
-def grad_states(full_width, given_ref, got_ref, own_ref, sib_ref, own_att_ref, sib_att_ref, pair_ref, own_total_ref, sib_total_ref, after_ref, high_ref, low_ref):
+def grad_states(full_width, sums_ref, own_ref, sib_ref, own_att_ref, sib_att_ref, pair_ref, own_total_ref, sib_total_ref, after_ref, high_ref, low_ref):
     rows, width = own_ref.shape
     half = width // 2
     for own, pack_ref, att_ref, total_ref in ((False, sib_ref, sib_att_ref, sib_total_ref), (True, own_ref, own_att_ref, own_total_ref)):
-        factors = row_factors(full_width, rows, given_ref, got_ref, own)
+        factors = row_factors(full_width, rows, sums_ref, own)
         for head in heads(half):
             total = None
             for n, row in reversed(list(enumerate(blocks(rows)))):
@@ -233,12 +251,12 @@
     pair_ref[...] = own_total_ref[...] + sib_total_ref[...]
 
 
-def grads_local(full_width, given_ref, got_ref, high_ref, low_ref, local_ref, pack_mine_ref, pack_other_ref, k_ref, v_ref, keep_ref, before_mine_ref, before_other_ref, total_ref, gq_hbm, gk_ref, gv_ref, after_ref, same_total_ref, gq_ref, other_high, other_low, sems):
+def grads_local(full_width, sums_ref, got_ref, high_ref, low_ref, att_other_ref, pack_mine_ref, pack_other_ref, k_ref, v_ref, keep_ref, before_mine_ref, before_other_ref, total_ref, gq_hbm, gk_ref, gv_ref, after_ref, same_total_ref, gq_ref, other_high, other_low, sems):
     rows, width = k_ref.shape
     half = width // 2
     sums_rows = 4 * rows // LANES
     same_total_ref[...] = total_ref[...]
-    factors = row_factors(full_width, rows, given_ref, got_ref, True)
+    factors = row_factors(full_width, rows, sums_ref, True)
     copies = []
     for mine in (True, False):
         pack_ref, before_ref = (pack_mine_ref, before_mine_ref) if mine else (pack_other_ref, before_other_ref)
@@ -248,25 +266,23 @@
                 state = keep_ref[head, :]
             else:
                 state = got_ref[sums_rows + head.start : sums_rows + head.stop, :]
-                operand = state_operand(state, False)
                 total = None
             for n, row in reversed(list(enumerate(blocks(rows)))):
                 if mine:
                     grad = high_ref[row, head], low_ref[row, head]
                 else:
-                    query = split(pack_ref[row, head])
-                    attended = local_ref[row, head] + product_state(query, operand, False)
                     scaled = pack_ref[row, half + head.start : half + head.stop]
-                    grad = split(grad_of_block(factors, scaled, attended, row))
+                    grad = split(grad_of_block(factors, scaled, att_other_ref[row, head], row))
                     other_high[row, head], other_low[row, head] = grad
                     if n > 0:
-                        more = product_tn(query, grad)
+                        more = product_tn(split(pack_ref[row, head]), grad)
                         total = more if total is None else total + more
                         after_ref[n - 1, head, :] = total
                 here = state_operand(state if n == 0 else state + before_ref[n - 1, head, :], True)
                 mixing = product_nt(grad, split(v_ref[row, col]))
                 mixing = jnp.where(causal_mask(row.stop - row.start), mixing, 0.0)
-                gq_ref[row, col] = product_nn(split(mixing), split(k_ref[row, col])) + product_state(grad, here, True)
+                gq_ref[row, col] = product_state(grad, here, True)
+                gq_ref[row, col] += product_nn(split(mixing), split(k_ref[row, col]))
                 copies.append(pltpu.make_async_copy(gq_ref.at[row, col], gq_hbm.at[row, col], sems.at[len(copies)]))
                 copies[-1].start()
     for mine in (True, False):
@@ -316,17 +332,17 @@
 
 
 def from_other_chips(pair, reverse):
-    chip = lax.axis_index("seq") // 2
-    chips = lax.axis_size("seq") // 2
+    place = lax.axis_index("seq")
+    chip = place // 2
+    ahead = lambda d: (chip ^ d) > chip if reverse else (chip ^ d) < chip
     total = jnp.zeros_like(pair)
-    ahead = lambda d: (chip ^ d) > chip if reverse else (chip ^ d) < chip
-    if chips <= 4:
-        got = [(d, swap(pair, "seq", 2 * d)) for d in reversed(range(1, chips))]
+    if on_grid():
+        got = [(d, swap(pair, "seq", 2 * d + d % 2)) for d in (3, 2, 1)]
         for d, part in got:
             total = total + jnp.where(ahead(d), part, 0.0)
         return total
     d = 1
-    while d < chips:
+    while d < lax.axis_size("seq") // 2:
         part = swap(pair, "seq", 2 * d)
         total = total + jnp.where(ahead(d), part, 0.0)
         pair = pair + part
@@ -334,14 +350,18 @@
     return total
 
 
-def sum_over_heads(x):
+def sum_over_heads(x, same_x):
     count = lax.axis_size("head")
     if count > 4 or count & (count - 1):
-        return lax.psum(x, "head")
-    parts = [swap(x, "head", d) for d in reversed(range(1, count))]
+        return lax.psum(same_x, "head")
+    parts = []
+    seqs = range(lax.axis_size("seq"))
+    for d in reversed(range(1, count)):
+        pairs = [(i * count + z, (i ^ 1) * count + (z ^ d)) for i in seqs for z in range(count)]
+        parts.append(lax.ppermute(x, ("seq", "head"), pairs))
     for part in parts:
-        x = x + part
-    return x
+        same_x = same_x + part
+    return same_x
 
 
 def shards(queries, keys, values, cotangent, gain):
@@ -378,17 +398,22 @@
         attend_state, "attend_state", [halves, halves, (4 * rows // LANES, LANES)], square,
         [pack_mine, local_mine, sibling, sibling_local, keep, give],
     )
-    given = jnp.concatenate([sum_over_heads(sums), give], axis=0)
+    given = jnp.concatenate([sums, give], axis=0)
     got = swap(given, "seq", 1)
+    pair_sums = given[: sums.shape[0]] + got[: sums.shape[0]]
+    attended_other, same_pair_sums = call(
+        attend_other, "attend_other", [halves, sums.shape], square // 2, [pair_sums, got, pack_other, local_other]
+    )
+    sums = sum_over_heads(pair_sums, same_pair_sums)
     pair, own_grad, sibling_grad, after_mine, high, low = call(
         functools.partial(grad_states, full_width), "grad_states",
         [state, state, state, inner, (halves, BF16), (halves, BF16)], square,
-        [given, got, pack_mine, sibling, attended, sibling_attended],
+        [sums, pack_mine, sibling, attended, sibling_attended],
     )
     later = from_other_chips(pair, True)
     grad_q, local_k, local_v, after_other, own_grad = call(
         functools.partial(grads_local, full_width), "grads_local", [whole, whole, whole, inner, state], 14 * square,
-        [given, got, high, low, local_other, pack_mine, pack_other, keys, values, keep, before_mine, before_other, own_grad],
+        [sums, got, high, low, attended_other, pack_mine, pack_other, keys, values, keep, before_mine, before_other, own_grad],
         [pltpu.VMEM(whole, F32), pltpu.VMEM(halves, BF16), pltpu.VMEM(halves, BF16), pltpu.SemaphoreType.DMA((units,))],
         hbm_out=(0,),
     )

time: 33.2 us -> 31.9 us (0.961)
  starting transfers between devices: 13.7 us -> 12.4 us
    ppermute x14 -> x11, starting transfers between devices: 13.7 us -> 8.55 us  [swap(): return lax.ppermute(x, axis, [(i, i ^ distance) for i in range(count)])]
    ppermute x0 -> x3, starting transfers between devices: none -> 3.89 us  [sum_over_heads(): parts.append(lax.ppermute(x, ('seq', 'head'), pairs))]
    ppermute x0 -> x3, waiting for transfers between devices: none -> 3.21 us  [sum_over_heads(): parts.append(lax.ppermute(x, ('seq', 'head'), pairs))]
    ppermute x14 -> x11, waiting for transfers between devices: 8.18 us -> 5.18 us  [swap(): return lax.ppermute(x, axis, [(i, i ^ distance) for i in range(count)])]
    pallas_call x8 -> x9, Pallas kernels: 10.2 us -> 10 us  [call(): pl.pallas_call(body, out_shape=outs, in_specs=[place(i in hbm_in) for i i...]
  transfers between devices with their start and end apart: 14 -> 14, of which waited for: 8 -> 9; matrix products, arithmetic and copies ran while one was open for 0% -> 0% of each run, Pallas kernels for 19% -> 19%
where the time goes in v4:
time: 31.9 us; the launch traced here: 31.8 us
  starting transfers between devices  12.4 us (39%)
  Pallas kernels  10 us (31%)
  waiting for transfers between devices  8.4 us (26%)
  between operations  0.8 us (3%)
    pallas_call x9, Pallas kernels, call(): pl.pallas_call(body, out_shape=outs, in_specs=[place(i in hbm_in) for i i...  10 us
    ppermute x11, starting transfers between devices, swap(): return lax.ppermute(x, axis, [(i, i ^ distance) for i in range(count)])  8.55 us
    ppermute x11, waiting for transfers between devices, swap(): return lax.ppermute(x, axis, [(i, i ^ distance) for i in range(count)])  5.18 us
    ppermute x3, starting transfers between devices, sum_over_heads(): parts.append(lax.ppermute(x, ('seq', 'head'), pairs))  3.89 us
    ppermute x3, waiting for transfers between devices, sum_over_heads(): parts.append(lax.ppermute(x, ('seq', 'head'), pairs))  3.21 us
  transfers between devices with their start and end apart: 14, of which 9 were waited for; matrix products, arithmetic and copies ran while one was open for 0% of the time, Pallas kernels for 19%

profile of v4, /device:TPU:0, one launch (start us, length us, event | category | flops | bytes accessed | tf_op | source)
XLA Modules:
  0.0 31.8 jit_solution(9456620949613720830)
XLA Ops:
  0.7 1.6 %key_states_other.1 = (f32[128,128]{1,0:T(8,128)S(1)}, f32[1,128,128]{2,1,0:T(8,128)S(1)}, f32[512,256]{1,0:T(8,128)S(1)}, f32[512,256]{1,0:T(8,128)S(1)}, f32[1,256]{1,0:T(1,128)S(1)}) custom-call(f32[512,256]{1,0:T(8,128)} %k_ref.5, f32[512,256]{1,0:T(8,128)} %v_ref.5, f32[1,256]{1,0:T(1,128)} %bitcast.1), custom_call_target="tpu_custom_call" | custom-call | flops 50331648 | bytes 2099200 | tf_op jit(solution)/shard_map/key_states_other/pallas_call | solution.py:79
  2.3 0.5 %collective-permute-start.2 = (f32[128,128]{1,0:T(8,128)S(1)}, f32[128,128]{1,0:T(8,128)S(1)}, u32[]{:S(2)}, u32[]{:S(2)}) collective-permute-start(f32[128,128]{1,0:T(8,128)S(1)} %get-tuple-element.44), channel_id=1, source_target_pairs={{0,4},{4,0},{8,12},{12,8},{16,20},{20,16},{24,28},{28,24},{1,5},{5... | collective-permute-start | bytes 196616 | tf_op jit(solution)/shard_map/ppermute | solution.py:331
  2.8 0.3 %key_states_mine.1 = (f32[128,128]{1,0:T(8,128)S(1)}, f32[1,128,128]{2,1,0:T(8,128)S(1)}, f32[512,256]{1,0:T(8,128)S(1)}, f32[512,256]{1,0:T(8,128)S(1)}) custom-call(f32[512,256]{1,0:T(8,128)S(1)} %get-tuple-element.34.k_ref, f32[512,256]{1,0:T(8,128)S(1)} %get-tuple-element.35.v_ref, f32[512,256]{1,0:T(8,128)S(1)} %copy-done.2, f32[512,256]{1,0:T(8,128)S(1)} %copy-done.3, ...), custom_call_target="tpu_custom_call" | custom-call | flops 50331648 | bytes 4196352 | tf_op jit(solution)/shard_map/key_states_mine/pallas_call | solution.py:79
  3.2 0.6 %collective-permute-done.2 = f32[128,128]{1,0:T(8,128)S(1)} collective-permute-done((f32[128,128]{1,0:T(8,128)S(1)}, f32[128,128]{1,0:T(8,128)S(1)}, u32[]{:S(2)}, u32[]{:S(2)}) %collective-permute-start.2) | collective-permute-done | bytes 65568 | tf_op jit(solution)/shard_map/ppermute | solution.py:331
  3.7 3.6 %collective-permute-start.3 = (f32[128,128]{1,0:T(8,128)S(1)}, f32[128,128]{1,0:T(8,128)S(1)}, u32[]{:S(2)}, u32[]{:S(2)}) collective-permute-start(f32[128,128]{1,0:T(8,128)S(1)} %add.44), channel_id=1, source_target_pairs={{0,28},{4,24},{8,20},{12,16},{16,12},{20,8},{24,4},{28,0},{1,29},{... | collective-permute-start | bytes 196616 | tf_op jit(solution)/shard_map/ppermute | solution.py:331
  7.4 0.5 %collective-permute-start.4 = (f32[128,128]{1,0:T(8,128)S(1)}, f32[128,128]{1,0:T(8,128)S(1)}, u32[]{:S(2)}, u32[]{:S(2)}) collective-permute-start(f32[128,128]{1,0:T(8,128)S(1)} %add.44), channel_id=1, source_target_pairs={{0,16},{4,20},{8,24},{12,28},{16,0},{20,4},{24,8},{28,12},{1,17},{... | collective-permute-start | bytes 196616 | tf_op jit(solution)/shard_map/ppermute | solution.py:331
  7.9 0.5 %collective-permute-start = (f32[512,256]{1,0:T(8,128)S(1)}, f32[512,256]{1,0:T(8,128)S(1)}, u32[]{:S(2)}, u32[]{:S(2)}) collective-permute-start(f32[512,256]{1,0:T(8,128)S(1)} %get-tuple-element.38.pack_other_ref.pack_ref), channel_id=1, source_target_pairs={{0,4},{4,0},{8,12},{12,8},{16,20},{20,16},{24,28},{28,24},{1,5},{5... | collective-permute-start | bytes 1572872 | tf_op jit(solution)/shard_map/ppermute | solution.py:331
  8.4 1.1 %attend_local.1 = (f32[512,128]{1,0:T(8,128)S(1)}, f32[512,128]{1,0:T(8,128)S(1)}) custom-call(f32[512,256]{1,0:T(8,128)S(1)} %get-tuple-element.37.pack_mine_ref.own_ref, f32[512,256]{1,0:T(8,128)S(1)} %get-tuple-element.38.pack_other_ref.pack_ref, f32[512,256]{1,0:T(8,128)S(1)} %get-tuple-element.34.k_ref, f32[512,256]{1,0:T(8,128)S(1)} %get-tuple-element.35.v_ref, ...), custom_call_target="tpu_custom_call" | custom-call | flops 503316480 | bytes 4456448 | tf_op jit(solution)/shard_map/attend_local/pallas_call | solution.py:79
  9.6 0.3 %collective-permute-done.3 = f32[128,128]{1,0:T(8,128)S(1)} collective-permute-done((f32[128,128]{1,0:T(8,128)S(1)}, f32[128,128]{1,0:T(8,128)S(1)}, u32[]{:S(2)}, u32[]{:S(2)}) %collective-permute-start.3) | collective-permute-done | bytes 65568 | tf_op jit(solution)/shard_map/ppermute | solution.py:331
  9.9 1.8 %collective-permute-done.4 = f32[128,128]{1,0:T(8,128)S(1)} collective-permute-done((f32[128,128]{1,0:T(8,128)S(1)}, f32[128,128]{1,0:T(8,128)S(1)}, u32[]{:S(2)}, u32[]{:S(2)}) %collective-permute-start.4) | collective-permute-done | bytes 65568 | tf_op jit(solution)/shard_map/ppermute | solution.py:331
  12.1 0.6 %attend_state.1 = (f32[512,128]{1,0:T(8,128)S(1)}, f32[512,128]{1,0:T(8,128)S(1)}, f32[16,128]{1,0:T(8,128)S(1)}) custom-call(f32[512,256]{1,0:T(8,128)S(1)} %get-tuple-element.37.pack_mine_ref.own_ref, f32[512,128]{1,0:T(8,128)S(1)} %get-tuple-element.41.own_local_ref, f32[512,256]{1,0:T(8,128)S(1)} %collective-permute-done.sib_ref, ...), custom_call_target="tpu_custom_call" | custom-call | flops 100663296 | bytes 3407872 | tf_op jit(solution)/shard_map/attend_state/pallas_call | solution.py:79
  12.8 1.2 %collective-permute-done.6.got_ref = f32[144,128]{1,0:T(8,128)S(1)} collective-permute-done((f32[144,128]{1,0:T(8,128)S(1)}, f32[144,128]{1,0:T(8,128)S(1)}, u32[]{:S(2)}, u32[]{:S(2)}) %collective-permute-start.6) | collective-permute-done | bytes 73760 | tf_op jit(solution)/shard_map/ppermute | solution.py:331
  14.0 3.4 %collective-permute-start.7 = (f32[16,128]{1,0:T(8,128)S(1)}, f32[16,128]{1,0:T(8,128)S(1)}, u32[]{:S(2)}, u32[]{:S(2)}) collective-permute-start(f32[16,128]{1,0:T(8,128)S(1)} %slice_add_fusion.pair_sums_ref), channel_id=1, source_target_pairs={{0,7},{1,6},{2,5},{3,4},{4,3},{5,2},{6,1},{7,0},{8,15},{9,14},{10,... | collective-permute-start | bytes 24584 | tf_op jit(solution)/shard_map/ppermute | solution.py:361
  17.4 0.5 %collective-permute-start.9 = (f32[16,128]{1,0:T(8,128)S(1)}, f32[16,128]{1,0:T(8,128)S(1)}, u32[]{:S(2)}, u32[]{:S(2)}) collective-permute-start(f32[16,128]{1,0:T(8,128)S(1)} %slice_add_fusion.pair_sums_ref), channel_id=1, source_target_pairs={{0,5},{1,4},{2,7},{3,6},{4,1},{5,0},{6,3},{7,2},{8,13},{9,12},{10,... | collective-permute-start | bytes 24584 | tf_op jit(solution)/shard_map/ppermute | solution.py:361
  18.1 0.7 %collective-permute-done.7 = f32[16,128]{1,0:T(8,128)S(1)} collective-permute-done((f32[16,128]{1,0:T(8,128)S(1)}, f32[16,128]{1,0:T(8,128)S(1)}, u32[]{:S(2)}, u32[]{:S(2)}) %collective-permute-start.7) | collective-permute-done | bytes 8224 | tf_op jit(solution)/shard_map/ppermute | solution.py:361
  18.9 2.5 %collective-permute-done.8 = f32[16,128]{1,0:T(8,128)S(1)} collective-permute-done((f32[16,128]{1,0:T(8,128)S(1)}, f32[16,128]{1,0:T(8,128)S(1)}, u32[]{:S(2)}, u32[]{:S(2)}) %collective-permute-start.8) | collective-permute-done | bytes 8224 | tf_op jit(solution)/shard_map/ppermute | solution.py:361
  21.4 0.8 %grad_states.1 = (f32[128,128]{1,0:T(8,128)S(1)}, f32[128,128]{1,0:T(8,128)S(1)}, f32[128,128]{1,0:T(8,128)S(1)}, f32[1,128,128]{2,1,0:T(8,128)S(1)}, bf16[512,1...) custom-call(f32[16,128]{1,0:T(8,128)S(1)} %add_add_fusion.sums_ref, ...), custom_call_target="tpu_custom_call" | custom-call | flops 100663296 | bytes 3162112 | tf_op jit(solution)/shard_map/grad_states/pallas_call | solution.py:79
  22.1 1.6 %collective-permute-start.10 = (f32[128,128]{1,0:T(8,128)S(1)}, f32[128,128]{1,0:T(8,128)S(1)}, u32[]{:S(2)}, u32[]{:S(2)}) collective-permute-start(f32[128,128]{1,0:T(8,128)S(1)} %get-tuple-element.56), channel_id=1, source_target_pairs={{0,28},{4,24},{8,20},{12,16},{16,12},{20,8},{24,4},{28,0},{1,29},{... | collective-permute-start | bytes 196616 | tf_op jit(solution)/shard_map/ppermute | solution.py:331
  23.8 1.2 %collective-permute-start.11 = (f32[128,128]{1,0:T(8,128)S(1)}, f32[128,128]{1,0:T(8,128)S(1)}, u32[]{:S(2)}, u32[]{:S(2)}) collective-permute-start(f32[128,128]{1,0:T(8,128)S(1)} %get-tuple-element.56), channel_id=1, source_target_pairs={{0,16},{4,20},{8,24},{12,28},{16,0},{20,4},{24,8},{28,12},{1,17},{... | collective-permute-start | bytes 196616 | tf_op jit(solution)/shard_map/ppermute | solution.py:331
  25.1 3.2 %grads_local.1 = (f32[512,256]{1,0:T(8,128)}, f32[512,256]{1,0:T(8,128)S(1)}, f32[512,256]{1,0:T(8,128)S(1)}, f32[1,128,128]{2,1,0:T(8,128)S(1)}, f32[128,128]{1,0:T(8,128)S(1)}) custom-call(f32[16,128]{1,0:T(8,128)S(1)} %add_add_fusion.sums_ref, f32[144,128]{1,0:T(8,128)S(1)} %collective-permute-done.6.got_ref, ...), custom_call_target="tpu_custom_call" | custom-call | flops 1409286144 | bytes 5931008 | tf_op jit(solution)/shard_map/grads_local/pallas_call | solution.py:79
  28.3 0.6 %collective-permute-done.11 = f32[128,128]{1,0:T(8,128)S(1)} collective-permute-done((f32[128,128]{1,0:T(8,128)S(1)}, f32[128,128]{1,0:T(8,128)S(1)}, u32[]{:S(2)}, u32[]{:S(2)}) %collective-permute-start.11) | collective-permute-done | bytes 65568 | tf_op jit(solution)/shard_map/ppermute | solution.py:331
  28.9 0.4 %collective-permute-done.12 = f32[128,128]{1,0:T(8,128)S(1)} collective-permute-done((f32[128,128]{1,0:T(8,128)S(1)}, f32[128,128]{1,0:T(8,128)S(1)}, u32[]{:S(2)}, u32[]{:S(2)}) %collective-permute-start.12) | collective-permute-done | bytes 65568 | tf_op jit(solution)/shard_map/ppermute | solution.py:331
  29.5 1.1 %grads_state_mine.1 = (f32[512,256]{1,0:T(8,128)}, f32[512,256]{1,0:T(8,128)}) custom-call(f32[512,256]{1,0:T(8,128)S(1)} %copy-done, f32[512,256]{1,0:T(8,128)S(1)} %copy-done.1, f32[512,256]{1,0:T(8,128)S(1)} %get-tuple-element.54.gk_local_ref, f32[512,256]{1,0:T(8,128)S(1)} %get-tuple-element.55.gv_local_ref, f32[128,128]{1,0:T(8,128)S(1)} %get-tuple-element.65.state_ref, ...), custom_call_target="tpu_custom_call" | custom-call | flops 100663296 | bytes 4456448 | tf_op jit(solution)/shard_map/grads_state_mine/pallas_call | solution.py:79
  30.7 1.1 %grads_state_other.1 = (f32[512,256]{1,0:T(8,128)}, f32[512,256]{1,0:T(8,128)}) custom-call(f32[512,256]{1,0:T(8,128)S(1)} %copy-done, f32[512,256]{1,0:T(8,128)S(1)} %copy-done.1, f32[512,256]{1,0:T(8,128)S(1)} %get-tuple-element.54.gk_local_ref, f32[512,256]{1,0:T(8,128)S(1)} %get-tuple-element.55.gv_local_ref, ...), custom_call_target="tpu_custom_call", output_to_operand_aliasing={{0}: (6, {}), {1}: (7, {})} | custom-call | flops 100663296 | bytes 6553600 | tf_op jit(solution)/shard_map/grads_state_other/pallas_call | solution.py:79
  (29 shorter events, 1.3 us)
Async XLA Ops:
  0.6 2.2 %copy-start.2 = (f32[512,256]{1,0:T(8,128)S(1)}, f32[512,256]{1,0:T(8,128)}, u32[]{:S(2)}) copy-start(f32[512,256]{1,0:T(8,128)} %q_ref.1) | copy-start | bytes 1572868
  0.6 2.2 %copy-start.3 = (f32[512,256]{1,0:T(8,128)S(1)}, f32[512,256]{1,0:T(8,128)}, u32[]{:S(2)}) copy-start(f32[512,256]{1,0:T(8,128)} %cot_ref.1) | copy-start | bytes 1572868
  2.3 1.4 %collective-permute-start.2 = (f32[128,128]{1,0:T(8,128)S(1)}, f32[128,128]{1,0:T(8,128)S(1)}, u32[]{:S(2)}, u32[]{:S(2)}) collective-permute-start(f32[128,128]{1,0:T(8,128)S(1)} %get-tuple-element.44), channel_id=1, source_target_pairs={{0,4},{4,0},{8,12},{12,8},{16,20},{20,16},{24,28},{28,24},{1,5},{5... | collective-permute-start | bytes 196616 | tf_op jit(solution)/shard_map/ppermute | solution.py:331
  3.7 6.2 %collective-permute-start.3 = (f32[128,128]{1,0:T(8,128)S(1)}, f32[128,128]{1,0:T(8,128)S(1)}, u32[]{:S(2)}, u32[]{:S(2)}) collective-permute-start(f32[128,128]{1,0:T(8,128)S(1)} %add.44), channel_id=1, source_target_pairs={{0,28},{4,24},{8,20},{12,16},{16,12},{20,8},{24,4},{28,0},{1,29},{... | collective-permute-start | bytes 196616 | tf_op jit(solution)/shard_map/ppermute | solution.py:331
  7.4 4.4 %collective-permute-start.4 = (f32[128,128]{1,0:T(8,128)S(1)}, f32[128,128]{1,0:T(8,128)S(1)}, u32[]{:S(2)}, u32[]{:S(2)}) collective-permute-start(f32[128,128]{1,0:T(8,128)S(1)} %add.44), channel_id=1, source_target_pairs={{0,16},{4,20},{8,24},{12,28},{16,0},{20,4},{24,8},{28,12},{1,17},{... | collective-permute-start | bytes 196616 | tf_op jit(solution)/shard_map/ppermute | solution.py:331
  7.9 4.1 %collective-permute-start.5 = (f32[128,128]{1,0:T(8,128)S(1)}, f32[128,128]{1,0:T(8,128)S(1)}, u32[]{:S(2)}, u32[]{:S(2)}) collective-permute-start(f32[128,128]{1,0:T(8,128)S(1)} %add.44), channel_id=1, source_target_pairs={{0,12},{4,8},{8,4},{12,0},{16,28},{20,24},{24,20},{28,16},{1,13},{... | collective-permute-start | bytes 196616 | tf_op jit(solution)/shard_map/ppermute | solution.py:331
  7.9 4.2 %collective-permute-start = (f32[512,256]{1,0:T(8,128)S(1)}, f32[512,256]{1,0:T(8,128)S(1)}, u32[]{:S(2)}, u32[]{:S(2)}) collective-permute-start(f32[512,256]{1,0:T(8,128)S(1)} %get-tuple-element.38.pack_other_ref.pack_ref), channel_id=1, source_target_pairs={{0,4},{4,0},{8,12},{12,8},{16,20},{20,16},{24,28},{28,24},{1,5},{5... | collective-permute-start | bytes 1572872 | tf_op jit(solution)/shard_map/ppermute | solution.py:331
  9.4 2.6 %collective-permute-start.1 = (f32[512,128]{1,0:T(8,128)S(1)}, f32[512,128]{1,0:T(8,128)S(1)}, u32[]{:S(2)}, u32[]{:S(2)}) collective-permute-start(f32[512,128]{1,0:T(8,128)S(1)} %get-tuple-element.42.local_ref), channel_id=1, source_target_pairs={{0,4},{4,0},{8,12},{12,8},{16,20},{20,16},{24,28},{28,24},{1,5},{5... | collective-permute-start | bytes 786440 | tf_op jit(solution)/shard_map/ppermute | solution.py:331
  12.7 1.3 %collective-permute-start.6 = (f32[144,128]{1,0:T(8,128)S(1)}, f32[144,128]{1,0:T(8,128)S(1)}, u32[]{:S(2)}, u32[]{:S(2)}) collective-permute-start(f32[144,128]{1,0:T(8,128)S(1)} %pad_maximum_fusion), channel_id=1, source_target_pairs={{0,4},{4,0},{8,12},{12,8},{16,20},{20,16},{24,28},{28,24},{1,5},{5... | collective-permute-start | bytes 221192 | tf_op jit(solution)/shard_map/ppermute | solution.py:331
  14.0 4.9 %collective-permute-start.7 = (f32[16,128]{1,0:T(8,128)S(1)}, f32[16,128]{1,0:T(8,128)S(1)}, u32[]{:S(2)}, u32[]{:S(2)}) collective-permute-start(f32[16,128]{1,0:T(8,128)S(1)} %slice_add_fusion.pair_sums_ref), channel_id=1, source_target_pairs={{0,7},{1,6},{2,5},{3,4},{4,3},{5,2},{6,1},{7,0},{8,15},{9,14},{10,... | collective-permute-start | bytes 24584 | tf_op jit(solution)/shard_map/ppermute | solution.py:361
  17.3 4.0 %collective-permute-start.8 = (f32[16,128]{1,0:T(8,128)S(1)}, f32[16,128]{1,0:T(8,128)S(1)}, u32[]{:S(2)}, u32[]{:S(2)}) collective-permute-start(f32[16,128]{1,0:T(8,128)S(1)} %slice_add_fusion.pair_sums_ref), channel_id=1, source_target_pairs={{0,6},{1,7},{2,4},{3,5},{4,2},{5,3},{6,0},{7,1},{8,14},{9,15},{10,... | collective-permute-start | bytes 24584 | tf_op jit(solution)/shard_map/ppermute | solution.py:361
  17.4 4.0 %collective-permute-start.9 = (f32[16,128]{1,0:T(8,128)S(1)}, f32[16,128]{1,0:T(8,128)S(1)}, u32[]{:S(2)}, u32[]{:S(2)}) collective-permute-start(f32[16,128]{1,0:T(8,128)S(1)} %slice_add_fusion.pair_sums_ref), channel_id=1, source_target_pairs={{0,5},{1,4},{2,7},{3,6},{4,1},{5,0},{6,3},{7,2},{8,13},{9,12},{10,... | collective-permute-start | bytes 24584 | tf_op jit(solution)/shard_map/ppermute | solution.py:361
  21.3 3.8 %copy-start = (f32[512,256]{1,0:T(8,128)S(1)}, f32[512,256]{1,0:T(8,128)}, u32[]{:S(2)}) copy-start(f32[512,256]{1,0:T(8,128)} %k_ref.5) | copy-start | bytes 1572868
  21.3 3.8 %copy-start.1 = (f32[512,256]{1,0:T(8,128)S(1)}, f32[512,256]{1,0:T(8,128)}, u32[]{:S(2)}) copy-start(f32[512,256]{1,0:T(8,128)} %v_ref.5) | copy-start | bytes 1572868
  22.1 6.2 %collective-permute-start.10 = (f32[128,128]{1,0:T(8,128)S(1)}, f32[128,128]{1,0:T(8,128)S(1)}, u32[]{:S(2)}, u32[]{:S(2)}) collective-permute-start(f32[128,128]{1,0:T(8,128)S(1)} %get-tuple-element.56), channel_id=1, source_target_pairs={{0,28},{4,24},{8,20},{12,16},{16,12},{20,8},{24,4},{28,0},{1,29},{... | collective-permute-start | bytes 196616 | tf_op jit(solution)/shard_map/ppermute | solution.py:331
  23.8 5.1 %collective-permute-start.11 = (f32[128,128]{1,0:T(8,128)S(1)}, f32[128,128]{1,0:T(8,128)S(1)}, u32[]{:S(2)}, u32[]{:S(2)}) collective-permute-start(f32[128,128]{1,0:T(8,128)S(1)} %get-tuple-element.56), channel_id=1, source_target_pairs={{0,16},{4,20},{8,24},{12,28},{16,0},{20,4},{24,8},{28,12},{1,17},{... | collective-permute-start | bytes 196616 | tf_op jit(solution)/shard_map/ppermute | solution.py:331
  25.0 4.3 %collective-permute-start.12 = (f32[128,128]{1,0:T(8,128)S(1)}, f32[128,128]{1,0:T(8,128)S(1)}, u32[]{:S(2)}, u32[]{:S(2)}) collective-permute-start(f32[128,128]{1,0:T(8,128)S(1)} %get-tuple-element.56), channel_id=1, source_target_pairs={{0,12},{4,8},{8,4},{12,0},{16,28},{20,24},{24,20},{28,16},{1,13},{... | collective-permute-start | bytes 196616 | tf_op jit(solution)/shard_map/ppermute | solution.py:331
  29.4 1.3 %collective-permute-start.13 = (f32[128,128]{1,0:T(8,128)S(1)}, f32[128,128]{1,0:T(8,128)S(1)}, u32[]{:S(2)}, u32[]{:S(2)}) collective-permute-start(f32[128,128]{1,0:T(8,128)S(1)} %select_add_fusion.1), channel_id=1, source_target_pairs={{0,4},{4,0},{8,12},{12,8},{16,20},{20,16},{24,28},{28,24},{1,5},{5... | collective-permute-start | bytes 196616 | tf_op jit(solution)/shard_map/ppermute | solution.py:331

commit v5 on v4

--- a/solution.py
+++ b/solution.py
@@ -156,8 +156,20 @@
     block_states(k_ref, v_ref, True, total_ref, before_ref)
     for mine, pack_ref in ((True, mine_ref), (False, other_ref)):
         col = half_cols(half, mine)
-        pack_ref[:, :half] = q_ref[:, col]
-        pack_ref[:, half:] = gain_ref[:, col] * cot_ref[:, col]
+        pack_ref[:half, :] = q_ref[:, col].T
+        pack_ref[half:, :] = (gain_ref[:, col] * cot_ref[:, col]).T
+
+
+def state_times(state, query):
+    left = split(state.T)
+    twice = jnp.concatenate([query[0], query[0]], axis=0)
+    return mul(beside(*left), twice, NN) + mul(left[0], query[1], NN)
+
+
+def over_steps(left, right):
+    rows, cols = left[0].shape[0], right[0].shape[0]
+    wide = mul(jnp.concatenate(left, axis=0), jnp.concatenate(right, axis=0), NT)
+    return wide[:rows, :cols] + wide[:rows, cols:] + wide[rows:, :cols]
 
 
 def attend_local(pack_mine_ref, pack_other_ref, k_ref, v_ref, before_mine_ref, before_other_ref, mine_ref, other_ref):
@@ -168,120 +180,124 @@
         for head in heads(half):
             col = half_cols(half, mine, head.start, HD)
             for n, row in enumerate(blocks(rows)):
-                query = split(pack_ref[row, head])
-                scores = product_nt(query, split(k_ref[row, col]))
-                scores = jnp.where(causal_mask(scores.shape[0]), scores, 0.0)
-                out = product_nn(split(scores), split(v_ref[row, col]))
+                query = split(pack_ref[head, row])
+                key = split(k_ref[row, col])
+                twice = jnp.concatenate([query[0], query[0]], axis=0)
+                scores = mul(beside(*key), twice, NN) + mul(key[0], query[1], NN)
+                scores = split(jnp.where(causal_mask(scores.shape[0], True), scores, 0.0))
+                value = split(v_ref[row, col].T)
+                out = mul(value[0], scores[0], NN) + mul(value[0], scores[1], NN) + mul(value[1], scores[0], NN)
                 if n > 0:
-                    out = out + product_state(query, state_operand(before_ref[n - 1, head, :], False), False)
-                out_ref[row, head] = out
+                    out = out + state_times(before_ref[n - 1, head, :], query)
+                out_ref[head, row] = out
+
+
+def lane_rows(x):
+    return [x[:, start : start + LANES] for start in range(0, x.shape[1], LANES)]
 
 
 def attend_state(own_ref, own_local_ref, sib_ref, sib_local_ref, keep_ref, give_ref, own_out_ref, sib_out_ref, sums_ref):
-    rows, width = own_ref.shape
-    half = width // 2
+    half, rows = own_local_ref.shape
     count = rows // LANES
-    lane = lax.broadcasted_iota(jnp.int32, (LANES, LANES), 1)
     for core, pack_ref, local_ref, state_ref, out_ref in (
         (my_core(), own_ref, own_local_ref, keep_ref, own_out_ref),
         (1 - my_core(), sib_ref, sib_local_ref, give_ref, sib_out_ref),
     ):
-        tile = jnp.zeros((LANES, LANES), F32)
-        states = [state_operand(state_ref[head, :], False) for head in heads(half)]
-        for n, row in enumerate(blocks(rows)):
-            for head, state in zip(heads(half), states):
-                out_ref[row, head] = local_ref[row, head] + product_state(split(pack_ref[row, head]), state, False)
-        for j in range(count):
-            row = slice(j * LANES, (j + 1) * LANES)
-            out = out_ref[row, :]
-            squares = jnp.sum(out * out, axis=1, keepdims=True)
-            cross = jnp.sum(pack_ref[row, half:] * out, axis=1, keepdims=True)
-            tile = jnp.where(lane == j, squares, tile)
-            tile = jnp.where(lane == count + j, cross, tile)
-        sums_ref[pl.ds(pl.multiple_of(core * 2 * count, 2 * count), 2 * count), :] = tile.T[: 2 * count]
+        squares, cross = jnp.zeros((1, rows), F32), jnp.zeros((1, rows), F32)
+        for head in heads(half):
+            out = local_ref[head, :] + state_times(state_ref[head, :], split(pack_ref[head, :]))
+            out_ref[head, :] = out
+            scaled = pack_ref[half + head.start : half + head.stop, :]
+            squares = squares + jnp.sum(out * out, axis=0, keepdims=True)
+            cross = cross + jnp.sum(scaled * out, axis=0, keepdims=True)
+        place = pl.ds(pl.multiple_of(core * 2 * count, 2 * count), 2 * count)
+        sums_ref[place, :] = jnp.concatenate(lane_rows(squares) + lane_rows(cross), axis=0)
 
 
 def attend_other(pair_sums_ref, got_ref, pack_ref, local_ref, out_ref, same_sums_ref):
     same_sums_ref[...] = pair_sums_ref[...]
     start = pair_sums_ref.shape[0]
-    rows, half = local_ref.shape
-    for head in heads(half):
-        operand = state_operand(got_ref[start + head.start : start + head.stop, :], False)
-        for row in blocks(rows):
-            out_ref[row, head] = local_ref[row, head] + product_state(split(pack_ref[row, head]), operand, False)
-
-
-def row_factors(full_width, rows, sums_ref, own):
+    for head in heads(local_ref.shape[0]):
+        state = got_ref[start + head.start : start + head.stop, :]
+        out_ref[head, :] = local_ref[head, :] + state_times(state, split(pack_ref[head, :]))
+
+
+def step_factors(full_width, rows, sums_ref, own):
     count = rows // LANES
     core = my_core() if own else 1 - my_core()
     sums = sums_ref[pl.ds(pl.multiple_of(core * 2 * count, 2 * count), 2 * count), :]
     inverse = lax.rsqrt(sums[:count] / full_width + 1e-06)
     factor = inverse * inverse * inverse * (sums[count:] / full_width)
-    both = jnp.concatenate([inverse, factor], axis=0)
-    tile = jnp.concatenate([both] * (LANES // both.shape[0]), axis=0).T
-    return [(tile[:, j : j + 1], tile[:, count + j : count + j + 1]) for j in range(count)]
-
-
-def grad_of_block(factors, scaled, attended, row):
-    parts = []
-    for i in range((row.stop - row.start) // LANES):
-        part = slice(i * LANES, (i + 1) * LANES)
-        inverse, factor = factors[row.start // LANES + i]
-        parts.append(inverse * scaled[part] - attended[part] * factor)
-    return jnp.concatenate(parts, axis=0)
+    return [beside(*[x[j : j + 1, :] for j in range(count)]) for x in (inverse, factor)]
+
+
+def gradient(factors, pack_ref, att_ref, head):
+    half = att_ref.shape[0]
+    scaled = pack_ref[half + head.start : half + head.stop, :]
+    return split(factors[0] * scaled - factors[1] * att_ref[head, :])
+
+
+def steps(parts, row):
+    return [part[:, row] for part in parts]
 
 
 def grad_states(full_width, sums_ref, own_ref, sib_ref, own_att_ref, sib_att_ref, pair_ref, own_total_ref, sib_total_ref, after_ref, high_ref, low_ref):
-    rows, width = own_ref.shape
-    half = width // 2
+    half, rows = own_att_ref.shape
     for own, pack_ref, att_ref, total_ref in ((False, sib_ref, sib_att_ref, sib_total_ref), (True, own_ref, own_att_ref, own_total_ref)):
-        factors = row_factors(full_width, rows, sums_ref, own)
-        for head in heads(half):
+        factors = step_factors(full_width, rows, sums_ref, own)
+        for head in heads(half):
+            grad = gradient(factors, pack_ref, att_ref, head)
+            query = split(pack_ref[head, :])
             total = None
             for n, row in reversed(list(enumerate(blocks(rows)))):
-                scaled = pack_ref[row, half + head.start : half + head.stop]
-                grad = split(grad_of_block(factors, scaled, att_ref[row, head], row))
-                if own:
-                    high_ref[row, head], low_ref[row, head] = grad
-                state = product_tn(split(pack_ref[row, head]), grad)
+                state = over_steps(steps(grad, row), steps(query, row))
                 total = state if total is None else total + state
                 if own and n > 0:
                     after_ref[n - 1, head, :] = total
+            if own:
+                high_ref[head, :], low_ref[head, :] = grad
             total_ref[head, :] = total
     pair_ref[...] = own_total_ref[...] + sib_total_ref[...]
 
 
-def grads_local(full_width, sums_ref, got_ref, high_ref, low_ref, att_other_ref, pack_mine_ref, pack_other_ref, k_ref, v_ref, keep_ref, before_mine_ref, before_other_ref, total_ref, gq_hbm, gk_ref, gv_ref, after_ref, same_total_ref, gq_ref, other_high, other_low, sems):
+def grads_local(full_width, sums_ref, got_ref, high_ref, low_ref, att_other_ref, pack_mine_ref, pack_other_ref, k_ref, v_ref, keep_ref, before_mine_ref, before_other_ref, total_ref, gq_hbm, gk_ref, gv_ref, after_ref, same_total_ref, gq_ref, grad_high, grad_low, sems):
     rows, width = k_ref.shape
     half = width // 2
     sums_rows = 4 * rows // LANES
     same_total_ref[...] = total_ref[...]
-    factors = row_factors(full_width, rows, sums_ref, True)
+    factors = step_factors(full_width, rows, sums_ref, True)
     copies = []
     for mine in (True, False):
         pack_ref, before_ref = (pack_mine_ref, before_mine_ref) if mine else (pack_other_ref, before_other_ref)
         for head in heads(half):
             col = half_cols(half, mine, head.start, HD)
+            place = head if mine else slice(half + head.start, half + head.stop)
             if mine:
                 state = keep_ref[head, :]
+                grad = high_ref[head, :], low_ref[head, :]
             else:
                 state = got_ref[sums_rows + head.start : sums_rows + head.stop, :]
+                grad = gradient(factors, pack_ref, att_other_ref, head)
+                query = split(pack_ref[head, :])
                 total = None
             for n, row in reversed(list(enumerate(blocks(rows)))):
-                if mine:
-                    grad = high_ref[row, head], low_ref[row, head]
-                else:
-                    scaled = pack_ref[row, half + head.start : half + head.stop]
-                    grad = split(grad_of_block(factors, scaled, att_other_ref[row, head], row))
-                    other_high[row, head], other_low[row, head] = grad
-                    if n > 0:
-                        more = product_tn(split(pack_ref[row, head]), grad)
-                        total = more if total is None else total + more
-                        after_ref[n - 1, head, :] = total
+                part = steps(grad, row)
+                if not mine and n > 0:
+                    more = over_steps(part, steps(query, row))
+                    total = more if total is None else total + more
+                    after_ref[n - 1, head, :] = total
+                part = [x.T for x in part]
+                grad_high[row, place], grad_low[row, place] = part
                 here = state_operand(state if n == 0 else state + before_ref[n - 1, head, :], True)
+                gq_ref[row, col] = product_state(part, here, True)
+    for mine in (True, False):
+        for head in heads(half):
+            col = half_cols(half, mine, head.start, HD)
+            place = head if mine else slice(half + head.start, half + head.stop)
+            for row in blocks(rows):
+                grad = grad_high[row, place], grad_low[row, place]
                 mixing = product_nt(grad, split(v_ref[row, col]))
                 mixing = jnp.where(causal_mask(row.stop - row.start), mixing, 0.0)
-                gq_ref[row, col] = product_state(grad, here, True)
                 gq_ref[row, col] += product_nn(split(mixing), split(k_ref[row, col]))
                 copies.append(pltpu.make_async_copy(gq_ref.at[row, col], gq_hbm.at[row, col], sems.at[len(copies)]))
                 copies[-1].start()
@@ -291,8 +307,8 @@
             col = half_cols(half, mine, head.start, HD)
             place = head if mine else slice(half + head.start, half + head.stop)
             for row in blocks(rows):
-                grad = (high_ref[row, head], low_ref[row, head]) if mine else (other_high[row, head], other_low[row, head])
-                query, key, value = split(pack_ref[row, head]), split(k_ref[row, col]), split(v_ref[row, col])
+                grad = grad_high[row, place], grad_low[row, place]
+                query, key, value = split(pack_ref[head, row].T), split(k_ref[row, col]), split(v_ref[row, col])
                 mask = causal_mask(row.stop - row.start, True)
                 mixing = jnp.where(mask, product_nt(value, grad), 0.0)
                 gk_ref[row, place] = product_nn(split(mixing), query)
@@ -318,9 +334,9 @@
         place = head if mine else slice(half + head.start, half + head.stop)
         for n, row in enumerate(blocks(rows)):
             here = state_ref[head, :] if n == last else state_ref[head, :] + after_ref[n, head, :]
-            gk_ref[row, head] = gk_local_ref[row, place] + product_state(split(v_ref[row, col]), state_operand(here, True), True)
+            gk_ref[row, head] = gk_local_ref[row, place] + product_state(split(v_ref[row, col]), state_operand(here, False), False)
             leave(gk_ref, gk_hbm, row, head, col)
-            gv_ref[row, head] = gv_local_ref[row, place] + product_state(split(k_ref[row, col]), state_operand(here, False), False)
+            gv_ref[row, head] = gv_local_ref[row, place] + product_state(split(k_ref[row, col]), state_operand(here, True), True)
             leave(gv_ref, gv_hbm, row, head, col)
     for copy in copies:
         copy.wait()
@@ -372,6 +388,7 @@
     units = count * (width // HD)
     square = rows * width * HD * 2 * 3
     whole, halves, state = (rows, width), (rows, half), (half, HD)
+    packed, across = (2 * half, rows), (half, rows)
     inner = (max(count - 1, 1), half, HD)
     first = lax.axis_index("seq") % 2 == 0
     gain = gain.reshape(1, width)
@@ -382,7 +399,7 @@
     )
     from_pair = swap(other, "seq", 1)
     mine, before_mine, pack_mine, pack_other = call(
-        key_states_mine, "key_states_mine", [state, inner, whole, whole], square // 2,
+        key_states_mine, "key_states_mine", [state, inner, packed, packed], square // 2,
         [near_keys, near_values, queries, cotangent, gain],
     )
     sibling = swap(pack_other, "seq", 1)
@@ -390,31 +407,31 @@
     keep = earlier + jnp.where(first, 0.0, from_pair)
     give = earlier + jnp.where(first, mine, 0.0)
     local_mine, local_other = call(
-        attend_local, "attend_local", [halves, halves], 5 * square,
+        attend_local, "attend_local", [across, across], 5 * square,
         [pack_mine, pack_other, near_keys, near_values, before_mine, before_other],
     )
     sibling_local = swap(local_other, "seq", 1)
     attended, sibling_attended, sums = call(
-        attend_state, "attend_state", [halves, halves, (4 * rows // LANES, LANES)], square,
+        attend_state, "attend_state", [across, across, (4 * rows // LANES, LANES)], square,
         [pack_mine, local_mine, sibling, sibling_local, keep, give],
     )
     given = jnp.concatenate([sums, give], axis=0)
     got = swap(given, "seq", 1)
     pair_sums = given[: sums.shape[0]] + got[: sums.shape[0]]
     attended_other, same_pair_sums = call(
-        attend_other, "attend_other", [halves, sums.shape], square // 2, [pair_sums, got, pack_other, local_other]
+        attend_other, "attend_other", [across, sums.shape], square // 2, [pair_sums, got, pack_other, local_other]
     )
     sums = sum_over_heads(pair_sums, same_pair_sums)
     pair, own_grad, sibling_grad, after_mine, high, low = call(
         functools.partial(grad_states, full_width), "grad_states",
-        [state, state, state, inner, (halves, BF16), (halves, BF16)], square,
+        [state, state, state, inner, (across, BF16), (across, BF16)], square,
         [sums, pack_mine, sibling, attended, sibling_attended],
     )
     later = from_other_chips(pair, True)
     grad_q, local_k, local_v, after_other, own_grad = call(
         functools.partial(grads_local, full_width), "grads_local", [whole, whole, whole, inner, state], 14 * square,
         [sums, got, high, low, attended_other, pack_mine, pack_other, keys, values, keep, before_mine, before_other, own_grad],
-        [pltpu.VMEM(whole, F32), pltpu.VMEM(halves, BF16), pltpu.VMEM(halves, BF16), pltpu.SemaphoreType.DMA((units,))],
+        [pltpu.VMEM(whole, F32), pltpu.VMEM(whole, BF16), pltpu.VMEM(whole, BF16), pltpu.SemaphoreType.DMA((units,))],
         hbm_out=(0,),
     )
     keep_later = later + jnp.where(first, sibling_grad, 0.0)

time: 31.9 us -> 31.3 us (0.981)
  Pallas kernels: 10 us -> 9.11 us
    pallas_call x9, Pallas kernels: 10 us -> 9.11 us  [call(): pl.pallas_call(body, out_shape=outs, in_specs=[place(i in hbm_in) for i i...]
  transfers between devices with their start and end apart: 14 -> 14, of which waited for: 9 -> 10; matrix products, arithmetic and copies ran while one was open for 0% -> 0% of each run, Pallas kernels for 19% -> 18%
where the time goes in v5:
time: 31.3 us; the launch traced here: 31.1 us
  starting transfers between devices  12.5 us (40%)
  Pallas kernels  9.11 us (29%)
  waiting for transfers between devices  8.61 us (28%)
  between operations  0.81 us (3%)
    pallas_call x9, Pallas kernels, call(): pl.pallas_call(body, out_shape=outs, in_specs=[place(i in hbm_in) for i i...  9.11 us
    ppermute x11, starting transfers between devices, swap(): return lax.ppermute(x, axis, [(i, i ^ distance) for i in range(count)])  8.58 us
    ppermute x11, waiting for transfers between devices, swap(): return lax.ppermute(x, axis, [(i, i ^ distance) for i in range(count)])  5.44 us
    ppermute x3, starting transfers between devices, sum_over_heads(): parts.append(lax.ppermute(x, ('seq', 'head'), pairs))  3.89 us
    ppermute x3, waiting for transfers between devices, sum_over_heads(): parts.append(lax.ppermute(x, ('seq', 'head'), pairs))  3.17 us
  transfers between devices with their start and end apart: 14, of which 10 were waited for; matrix products, arithmetic and copies ran while one was open for 0% of the time, Pallas kernels for 18%

profile of v5, /device:TPU:0, one launch (start us, length us, event | category | flops | bytes accessed | tf_op | source)
XLA Modules:
  0.0 31.1 jit_solution(3218017933497445003)
XLA Ops:
  0.7 1.6 %key_states_other.1 = (f32[128,128]{1,0:T(8,128)S(1)}, f32[1,128,128]{2,1,0:T(8,128)S(1)}, f32[512,256]{1,0:T(8,128)S(1)}, f32[512,256]{1,0:T(8,128)S(1)}, f32[1,256]{1,0:T(1,128)S(1)}) custom-call(f32[512,256]{1,0:T(8,128)} %k_ref.5, f32[512,256]{1,0:T(8,128)} %v_ref.5, f32[1,256]{1,0:T(1,128)} %bitcast.1), custom_call_target="tpu_custom_call" | custom-call | flops 50331648 | bytes 2099200 | tf_op jit(solution)/shard_map/key_states_other/pallas_call | solution.py:79
  2.3 0.5 %collective-permute-start.2 = (f32[128,128]{1,0:T(8,128)S(1)}, f32[128,128]{1,0:T(8,128)S(1)}, u32[]{:S(2)}, u32[]{:S(2)}) collective-permute-start(f32[128,128]{1,0:T(8,128)S(1)} %get-tuple-element.44), channel_id=1, source_target_pairs={{0,4},{4,0},{8,12},{12,8},{16,20},{20,16},{24,28},{28,24},{1,5},{5... | collective-permute-start | bytes 196616 | tf_op jit(solution)/shard_map/ppermute | solution.py:347
  2.8 0.4 %key_states_mine.1 = (f32[128,128]{1,0:T(8,128)S(1)}, f32[1,128,128]{2,1,0:T(8,128)S(1)}, f32[256,512]{1,0:T(8,128)S(1)}, f32[256,512]{1,0:T(8,128)S(1)}) custom-call(f32[512,256]{1,0:T(8,128)S(1)} %get-tuple-element.34.k_ref, f32[512,256]{1,0:T(8,128)S(1)} %get-tuple-element.35.v_ref, f32[512,256]{1,0:T(8,128)S(1)} %copy-done.2, f32[512,256]{1,0:T(8,128)S(1)} %copy-done.3, ...), custom_call_target="tpu_custom_call" | custom-call | flops 50331648 | bytes 4196352 | tf_op jit(solution)/shard_map/key_states_mine/pallas_call | solution.py:79
  3.3 0.5 %collective-permute-done.2 = f32[128,128]{1,0:T(8,128)S(1)} collective-permute-done((f32[128,128]{1,0:T(8,128)S(1)}, f32[128,128]{1,0:T(8,128)S(1)}, u32[]{:S(2)}, u32[]{:S(2)}) %collective-permute-start.2) | collective-permute-done | bytes 65568 | tf_op jit(solution)/shard_map/ppermute | solution.py:347
  3.7 3.6 %collective-permute-start.3 = (f32[128,128]{1,0:T(8,128)S(1)}, f32[128,128]{1,0:T(8,128)S(1)}, u32[]{:S(2)}, u32[]{:S(2)}) collective-permute-start(f32[128,128]{1,0:T(8,128)S(1)} %add.44), channel_id=1, source_target_pairs={{0,28},{4,24},{8,20},{12,16},{16,12},{20,8},{24,4},{28,0},{1,29},{... | collective-permute-start | bytes 196616 | tf_op jit(solution)/shard_map/ppermute | solution.py:347
  7.4 0.5 %collective-permute-start.4 = (f32[128,128]{1,0:T(8,128)S(1)}, f32[128,128]{1,0:T(8,128)S(1)}, u32[]{:S(2)}, u32[]{:S(2)}) collective-permute-start(f32[128,128]{1,0:T(8,128)S(1)} %add.44), channel_id=1, source_target_pairs={{0,16},{4,20},{8,24},{12,28},{16,0},{20,4},{24,8},{28,12},{1,17},{... | collective-permute-start | bytes 196616 | tf_op jit(solution)/shard_map/ppermute | solution.py:347
  7.9 0.5 %collective-permute-start = (f32[256,512]{1,0:T(8,128)S(1)}, f32[256,512]{1,0:T(8,128)S(1)}, u32[]{:S(2)}, u32[]{:S(2)}) collective-permute-start(f32[256,512]{1,0:T(8,128)S(1)} %get-tuple-element.38.pack_other_ref.pack_ref), channel_id=1, source_target_pairs={{0,4},{4,0},{8,12},{12,8},{16,20},{20,16},{24,28},{28,24},{1,5},{5... | collective-permute-start | bytes 1572872 | tf_op jit(solution)/shard_map/ppermute | solution.py:347
  8.4 1.2 %attend_local.1 = (f32[128,512]{1,0:T(8,128)S(1)}, f32[128,512]{1,0:T(8,128)S(1)}) custom-call(f32[256,512]{1,0:T(8,128)S(1)} %get-tuple-element.37.pack_mine_ref.own_ref, f32[256,512]{1,0:T(8,128)S(1)} %get-tuple-element.38.pack_other_ref.pack_ref, f32[512,256]{1,0:T(8,128)S(1)} %get-tuple-element.34.k_ref, f32[512,256]{1,0:T(8,128)S(1)} %get-tuple-element.35.v_ref, ...), custom_call_target="tpu_custom_call" | custom-call | flops 503316480 | bytes 4456448 | tf_op jit(solution)/shard_map/attend_local/pallas_call | solution.py:79
  9.9 1.8 %collective-permute-done.4 = f32[128,128]{1,0:T(8,128)S(1)} collective-permute-done((f32[128,128]{1,0:T(8,128)S(1)}, f32[128,128]{1,0:T(8,128)S(1)}, u32[]{:S(2)}, u32[]{:S(2)}) %collective-permute-start.4) | collective-permute-done | bytes 65568 | tf_op jit(solution)/shard_map/ppermute | solution.py:347
  11.7 0.3 collective-permute-done.5
  12.1 0.4 %attend_state.1 = (f32[128,512]{1,0:T(8,128)S(1)}, f32[128,512]{1,0:T(8,128)S(1)}, f32[16,128]{1,0:T(8,128)S(1)}) custom-call(f32[256,512]{1,0:T(8,128)S(1)} %get-tuple-element.37.pack_mine_ref.own_ref, f32[128,512]{1,0:T(8,128)S(1)} %get-tuple-element.41.own_local_ref, f32[256,512]{1,0:T(8,128)S(1)} %collective-permute-done.sib_ref, ...), custom_call_target="tpu_custom_call" | custom-call | flops 100663296 | bytes 3407872 | tf_op jit(solution)/shard_map/attend_state/pallas_call | solution.py:79
  12.6 1.2 %collective-permute-done.6.got_ref = f32[144,128]{1,0:T(8,128)S(1)} collective-permute-done((f32[144,128]{1,0:T(8,128)S(1)}, f32[144,128]{1,0:T(8,128)S(1)}, u32[]{:S(2)}, u32[]{:S(2)}) %collective-permute-start.6) | collective-permute-done | bytes 73760 | tf_op jit(solution)/shard_map/ppermute | solution.py:347
  13.8 3.4 %collective-permute-start.7 = (f32[16,128]{1,0:T(8,128)S(1)}, f32[16,128]{1,0:T(8,128)S(1)}, u32[]{:S(2)}, u32[]{:S(2)}) collective-permute-start(f32[16,128]{1,0:T(8,128)S(1)} %slice_add_fusion.pair_sums_ref), channel_id=1, source_target_pairs={{0,7},{1,6},{2,5},{3,4},{4,3},{5,2},{6,1},{7,0},{8,15},{9,14},{10,... | collective-permute-start | bytes 24584 | tf_op jit(solution)/shard_map/ppermute | solution.py:377
  17.2 0.5 %collective-permute-start.9 = (f32[16,128]{1,0:T(8,128)S(1)}, f32[16,128]{1,0:T(8,128)S(1)}, u32[]{:S(2)}, u32[]{:S(2)}) collective-permute-start(f32[16,128]{1,0:T(8,128)S(1)} %slice_add_fusion.pair_sums_ref), channel_id=1, source_target_pairs={{0,5},{1,4},{2,7},{3,6},{4,1},{5,0},{6,3},{7,2},{8,13},{9,12},{10,... | collective-permute-start | bytes 24584 | tf_op jit(solution)/shard_map/ppermute | solution.py:377
  18.0 0.7 %collective-permute-done.7 = f32[16,128]{1,0:T(8,128)S(1)} collective-permute-done((f32[16,128]{1,0:T(8,128)S(1)}, f32[16,128]{1,0:T(8,128)S(1)}, u32[]{:S(2)}, u32[]{:S(2)}) %collective-permute-start.7) | collective-permute-done | bytes 8224 | tf_op jit(solution)/shard_map/ppermute | solution.py:377
  18.7 2.5 %collective-permute-done.8 = f32[16,128]{1,0:T(8,128)S(1)} collective-permute-done((f32[16,128]{1,0:T(8,128)S(1)}, f32[16,128]{1,0:T(8,128)S(1)}, u32[]{:S(2)}, u32[]{:S(2)}) %collective-permute-start.8) | collective-permute-done | bytes 8224 | tf_op jit(solution)/shard_map/ppermute | solution.py:377
  21.2 0.4 %grad_states.1 = (f32[128,128]{1,0:T(8,128)S(1)}, f32[128,128]{1,0:T(8,128)S(1)}, f32[128,128]{1,0:T(8,128)S(1)}, f32[1,128,128]{2,1,0:T(8,128)S(1)}, bf16[128,5...) custom-call(f32[16,128]{1,0:T(8,128)S(1)} %add_add_fusion.sums_ref, ...), custom_call_target="tpu_custom_call" | custom-call | flops 100663296 | bytes 3162112 | tf_op jit(solution)/shard_map/grad_states/pallas_call | solution.py:79
  21.5 1.7 %collective-permute-start.10 = (f32[128,128]{1,0:T(8,128)S(1)}, f32[128,128]{1,0:T(8,128)S(1)}, u32[]{:S(2)}, u32[]{:S(2)}) collective-permute-start(f32[128,128]{1,0:T(8,128)S(1)} %get-tuple-element.56), channel_id=1, source_target_pairs={{0,28},{4,24},{8,20},{12,16},{16,12},{20,8},{24,4},{28,0},{1,29},{... | collective-permute-start | bytes 196616 | tf_op jit(solution)/shard_map/ppermute | solution.py:347
  23.3 1.1 %collective-permute-start.11 = (f32[128,128]{1,0:T(8,128)S(1)}, f32[128,128]{1,0:T(8,128)S(1)}, u32[]{:S(2)}, u32[]{:S(2)}) collective-permute-start(f32[128,128]{1,0:T(8,128)S(1)} %get-tuple-element.56), channel_id=1, source_target_pairs={{0,16},{4,20},{8,24},{12,28},{16,0},{20,4},{24,8},{28,12},{1,17},{... | collective-permute-start | bytes 196616 | tf_op jit(solution)/shard_map/ppermute | solution.py:347
  24.5 2.8 %grads_local.1 = (f32[512,256]{1,0:T(8,128)}, f32[512,256]{1,0:T(8,128)S(1)}, f32[512,256]{1,0:T(8,128)S(1)}, f32[1,128,128]{2,1,0:T(8,128)S(1)}, f32[128,128]{1,0:T(8,128)S(1)}) custom-call(f32[16,128]{1,0:T(8,128)S(1)} %add_add_fusion.sums_ref, f32[144,128]{1,0:T(8,128)S(1)} %collective-permute-done.6.got_ref, ...), custom_call_target="tpu_custom_call" | custom-call | flops 1409286144 | bytes 5931008 | tf_op jit(solution)/shard_map/grads_local/pallas_call | solution.py:79
  27.3 1.0 %collective-permute-done.11 = f32[128,128]{1,0:T(8,128)S(1)} collective-permute-done((f32[128,128]{1,0:T(8,128)S(1)}, f32[128,128]{1,0:T(8,128)S(1)}, u32[]{:S(2)}, u32[]{:S(2)}) %collective-permute-start.11) | collective-permute-done | bytes 65568 | tf_op jit(solution)/shard_map/ppermute | solution.py:347
  28.3 0.4 %collective-permute-done.12 = f32[128,128]{1,0:T(8,128)S(1)} collective-permute-done((f32[128,128]{1,0:T(8,128)S(1)}, f32[128,128]{1,0:T(8,128)S(1)}, u32[]{:S(2)}, u32[]{:S(2)}) %collective-permute-start.12) | collective-permute-done | bytes 65568 | tf_op jit(solution)/shard_map/ppermute | solution.py:347
  28.9 1.1 %grads_state_mine.1 = (f32[512,256]{1,0:T(8,128)}, f32[512,256]{1,0:T(8,128)}) custom-call(f32[512,256]{1,0:T(8,128)S(1)} %copy-done, f32[512,256]{1,0:T(8,128)S(1)} %copy-done.1, f32[512,256]{1,0:T(8,128)S(1)} %get-tuple-element.54.gk_local_ref, f32[512,256]{1,0:T(8,128)S(1)} %get-tuple-element.55.gv_local_ref, f32[128,128]{1,0:T(8,128)S(1)} %get-tuple-element.65.state_ref, ...), custom_call_target="tpu_custom_call" | custom-call | flops 100663296 | bytes 4456448 | tf_op jit(solution)/shard_map/grads_state_mine/pallas_call | solution.py:79
  30.1 1.1 %grads_state_other.1 = (f32[512,256]{1,0:T(8,128)}, f32[512,256]{1,0:T(8,128)}) custom-call(f32[512,256]{1,0:T(8,128)S(1)} %copy-done, f32[512,256]{1,0:T(8,128)S(1)} %copy-done.1, f32[512,256]{1,0:T(8,128)S(1)} %get-tuple-element.54.gk_local_ref, f32[512,256]{1,0:T(8,128)S(1)} %get-tuple-element.55.gv_local_ref, ...), custom_call_target="tpu_custom_call", output_to_operand_aliasing={{0}: (6, {}), {1}: (7, {})} | custom-call | flops 100663296 | bytes 6553600 | tf_op jit(solution)/shard_map/grads_state_other/pallas_call | solution.py:79
  (29 shorter events, 1.3 us)
Async XLA Ops:
  0.6 2.2 %copy-start.2 = (f32[512,256]{1,0:T(8,128)S(1)}, f32[512,256]{1,0:T(8,128)}, u32[]{:S(2)}) copy-start(f32[512,256]{1,0:T(8,128)} %q_ref.1) | copy-start | bytes 1572868
  0.6 2.2 %copy-start.3 = (f32[512,256]{1,0:T(8,128)S(1)}, f32[512,256]{1,0:T(8,128)}, u32[]{:S(2)}) copy-start(f32[512,256]{1,0:T(8,128)} %cot_ref.1) | copy-start | bytes 1572868
  2.3 1.4 %collective-permute-start.2 = (f32[128,128]{1,0:T(8,128)S(1)}, f32[128,128]{1,0:T(8,128)S(1)}, u32[]{:S(2)}, u32[]{:S(2)}) collective-permute-start(f32[128,128]{1,0:T(8,128)S(1)} %get-tuple-element.44), channel_id=1, source_target_pairs={{0,4},{4,0},{8,12},{12,8},{16,20},{20,16},{24,28},{28,24},{1,5},{5... | collective-permute-start | bytes 196616 | tf_op jit(solution)/shard_map/ppermute | solution.py:347
  3.7 6.2 %collective-permute-start.3 = (f32[128,128]{1,0:T(8,128)S(1)}, f32[128,128]{1,0:T(8,128)S(1)}, u32[]{:S(2)}, u32[]{:S(2)}) collective-permute-start(f32[128,128]{1,0:T(8,128)S(1)} %add.44), channel_id=1, source_target_pairs={{0,28},{4,24},{8,20},{12,16},{16,12},{20,8},{24,4},{28,0},{1,29},{... | collective-permute-start | bytes 196616 | tf_op jit(solution)/shard_map/ppermute | solution.py:347
  7.4 4.4 %collective-permute-start.4 = (f32[128,128]{1,0:T(8,128)S(1)}, f32[128,128]{1,0:T(8,128)S(1)}, u32[]{:S(2)}, u32[]{:S(2)}) collective-permute-start(f32[128,128]{1,0:T(8,128)S(1)} %add.44), channel_id=1, source_target_pairs={{0,16},{4,20},{8,24},{12,28},{16,0},{20,4},{24,8},{28,12},{1,17},{... | collective-permute-start | bytes 196616 | tf_op jit(solution)/shard_map/ppermute | solution.py:347
  7.9 4.1 %collective-permute-start.5 = (f32[128,128]{1,0:T(8,128)S(1)}, f32[128,128]{1,0:T(8,128)S(1)}, u32[]{:S(2)}, u32[]{:S(2)}) collective-permute-start(f32[128,128]{1,0:T(8,128)S(1)} %add.44), channel_id=1, source_target_pairs={{0,12},{4,8},{8,4},{12,0},{16,28},{20,24},{24,20},{28,16},{1,13},{... | collective-permute-start | bytes 196616 | tf_op jit(solution)/shard_map/ppermute | solution.py:347
  7.9 4.2 %collective-permute-start = (f32[256,512]{1,0:T(8,128)S(1)}, f32[256,512]{1,0:T(8,128)S(1)}, u32[]{:S(2)}, u32[]{:S(2)}) collective-permute-start(f32[256,512]{1,0:T(8,128)S(1)} %get-tuple-element.38.pack_other_ref.pack_ref), channel_id=1, source_target_pairs={{0,4},{4,0},{8,12},{12,8},{16,20},{20,16},{24,28},{28,24},{1,5},{5... | collective-permute-start | bytes 1572872 | tf_op jit(solution)/shard_map/ppermute | solution.py:347
  9.5 2.5 %collective-permute-start.1 = (f32[128,512]{1,0:T(8,128)S(1)}, f32[128,512]{1,0:T(8,128)S(1)}, u32[]{:S(2)}, u32[]{:S(2)}) collective-permute-start(f32[128,512]{1,0:T(8,128)S(1)} %get-tuple-element.42.local_ref), channel_id=1, source_target_pairs={{0,4},{4,0},{8,12},{12,8},{16,20},{20,16},{24,28},{28,24},{1,5},{5... | collective-permute-start | bytes 786440 | tf_op jit(solution)/shard_map/ppermute | solution.py:347
  12.5 1.3 %collective-permute-start.6 = (f32[144,128]{1,0:T(8,128)S(1)}, f32[144,128]{1,0:T(8,128)S(1)}, u32[]{:S(2)}, u32[]{:S(2)}) collective-permute-start(f32[144,128]{1,0:T(8,128)S(1)} %pad_maximum_fusion), channel_id=1, source_target_pairs={{0,4},{4,0},{8,12},{12,8},{16,20},{20,16},{24,28},{28,24},{1,5},{5... | collective-permute-start | bytes 221192 | tf_op jit(solution)/shard_map/ppermute | solution.py:347
  13.8 4.9 %collective-permute-start.7 = (f32[16,128]{1,0:T(8,128)S(1)}, f32[16,128]{1,0:T(8,128)S(1)}, u32[]{:S(2)}, u32[]{:S(2)}) collective-permute-start(f32[16,128]{1,0:T(8,128)S(1)} %slice_add_fusion.pair_sums_ref), channel_id=1, source_target_pairs={{0,7},{1,6},{2,5},{3,4},{4,3},{5,2},{6,1},{7,0},{8,15},{9,14},{10,... | collective-permute-start | bytes 24584 | tf_op jit(solution)/shard_map/ppermute | solution.py:377
  17.2 4.0 %collective-permute-start.8 = (f32[16,128]{1,0:T(8,128)S(1)}, f32[16,128]{1,0:T(8,128)S(1)}, u32[]{:S(2)}, u32[]{:S(2)}) collective-permute-start(f32[16,128]{1,0:T(8,128)S(1)} %slice_add_fusion.pair_sums_ref), channel_id=1, source_target_pairs={{0,6},{1,7},{2,4},{3,5},{4,2},{5,3},{6,0},{7,1},{8,14},{9,15},{10,... | collective-permute-start | bytes 24584 | tf_op jit(solution)/shard_map/ppermute | solution.py:377
  17.2 4.0 %collective-permute-start.9 = (f32[16,128]{1,0:T(8,128)S(1)}, f32[16,128]{1,0:T(8,128)S(1)}, u32[]{:S(2)}, u32[]{:S(2)}) collective-permute-start(f32[16,128]{1,0:T(8,128)S(1)} %slice_add_fusion.pair_sums_ref), channel_id=1, source_target_pairs={{0,5},{1,4},{2,7},{3,6},{4,1},{5,0},{6,3},{7,2},{8,13},{9,12},{10,... | collective-permute-start | bytes 24584 | tf_op jit(solution)/shard_map/ppermute | solution.py:377
  21.1 3.4 %copy-start = (f32[512,256]{1,0:T(8,128)S(1)}, f32[512,256]{1,0:T(8,128)}, u32[]{:S(2)}) copy-start(f32[512,256]{1,0:T(8,128)} %k_ref.5) | copy-start | bytes 1572868
  21.2 3.4 %copy-start.1 = (f32[512,256]{1,0:T(8,128)S(1)}, f32[512,256]{1,0:T(8,128)}, u32[]{:S(2)}) copy-start(f32[512,256]{1,0:T(8,128)} %v_ref.5) | copy-start | bytes 1572868
  21.5 5.8 %collective-permute-start.10 = (f32[128,128]{1,0:T(8,128)S(1)}, f32[128,128]{1,0:T(8,128)S(1)}, u32[]{:S(2)}, u32[]{:S(2)}) collective-permute-start(f32[128,128]{1,0:T(8,128)S(1)} %get-tuple-element.56), channel_id=1, source_target_pairs={{0,28},{4,24},{8,20},{12,16},{16,12},{20,8},{24,4},{28,0},{1,29},{... | collective-permute-start | bytes 196616 | tf_op jit(solution)/shard_map/ppermute | solution.py:347
  23.3 5.0 %collective-permute-start.11 = (f32[128,128]{1,0:T(8,128)S(1)}, f32[128,128]{1,0:T(8,128)S(1)}, u32[]{:S(2)}, u32[]{:S(2)}) collective-permute-start(f32[128,128]{1,0:T(8,128)S(1)} %get-tuple-element.56), channel_id=1, source_target_pairs={{0,16},{4,20},{8,24},{12,28},{16,0},{20,4},{24,8},{28,12},{1,17},{... | collective-permute-start | bytes 196616 | tf_op jit(solution)/shard_map/ppermute | solution.py:347
  24.4 4.3 %collective-permute-start.12 = (f32[128,128]{1,0:T(8,128)S(1)}, f32[128,128]{1,0:T(8,128)S(1)}, u32[]{:S(2)}, u32[]{:S(2)}) collective-permute-start(f32[128,128]{1,0:T(8,128)S(1)} %get-tuple-element.56), channel_id=1, source_target_pairs={{0,12},{4,8},{8,4},{12,0},{16,28},{20,24},{24,20},{28,16},{1,13},{... | collective-permute-start | bytes 196616 | tf_op jit(solution)/shard_map/ppermute | solution.py:347
  28.7 1.3 %collective-permute-start.13 = (f32[128,128]{1,0:T(8,128)S(1)}, f32[128,128]{1,0:T(8,128)S(1)}, u32[]{:S(2)}, u32[]{:S(2)}) collective-permute-start(f32[128,128]{1,0:T(8,128)S(1)} %select_add_fusion.1), channel_id=1, source_target_pairs={{0,4},{4,0},{8,12},{12,8},{16,20},{20,16},{24,28},{28,24},{1,5},{5... | collective-permute-start | bytes 196616 | tf_op jit(solution)/shard_map/ppermute | solution.py:347

commit v6 on v5

--- a/solution.py
+++ b/solution.py
@@ -353,7 +353,7 @@
     ahead = lambda d: (chip ^ d) > chip if reverse else (chip ^ d) < chip
     total = jnp.zeros_like(pair)
     if on_grid():
-        got = [(d, swap(pair, "seq", 2 * d + d % 2)) for d in (3, 2, 1)]
+        got = [(d, swap(pair, "seq", 2 * d + d % 2)) for d in (3, 1, 2)]
         for d, part in got:
             total = total + jnp.where(ahead(d), part, 0.0)
         return total
@@ -372,7 +372,7 @@
         return lax.psum(same_x, "head")
     parts = []
     seqs = range(lax.axis_size("seq"))
-    for d in reversed(range(1, count)):
+    for d in sorted(range(1, count), key=lambda d: (d != count // 2, -d)):
         pairs = [(i * count + z, (i ^ 1) * count + (z ^ d)) for i in seqs for z in range(count)]
         parts.append(lax.ppermute(x, ("seq", "head"), pairs))
     for part in parts:

time: 31.3 us -> 31 us (level)
  waiting for transfers between devices: 8.61 us -> 8.1 us
    ppermute x11, waiting for transfers between devices: 5.44 us -> 5.04 us  [swap(): return lax.ppermute(x, axis, [(i, i ^ distance) for i in range(count)])]
  transfers between devices with their start and end apart: 14 -> 14, of which waited for: 10 -> 9; matrix products, arithmetic and copies ran while one was open for 0% -> 0% of each run, Pallas kernels for 18% -> 18%
where the time goes in v6:
time: 31 us; the launch traced here: 30.8 us
  starting transfers between devices  12.7 us (41%)
  Pallas kernels  9.12 us (29%)
  waiting for transfers between devices  8.1 us (26%)
  between operations  0.82 us (3%)
    pallas_call x9, Pallas kernels, call(): pl.pallas_call(body, out_shape=outs, in_specs=[place(i in hbm_in) for i i...  9.12 us
    ppermute x11, starting transfers between devices, swap(): return lax.ppermute(x, axis, [(i, i ^ distance) for i in range(count)])  8.78 us
    ppermute x11, waiting for transfers between devices, swap(): return lax.ppermute(x, axis, [(i, i ^ distance) for i in range(count)])  5.04 us
    ppermute x3, starting transfers between devices, sum_over_heads(): parts.append(lax.ppermute(x, ('seq', 'head'), pairs))  3.89 us
    ppermute x3, waiting for transfers between devices, sum_over_heads(): parts.append(lax.ppermute(x, ('seq', 'head'), pairs))  3.06 us
  transfers between devices with their start and end apart: 14, of which 9 were waited for; matrix products, arithmetic and copies ran while one was open for 0% of the time, Pallas kernels for 18%

profile of v6, /device:TPU:0, one launch (start us, length us, event | category | flops | bytes accessed | tf_op | source)
XLA Modules:
  0.0 30.8 jit_solution(5624334228733425326)
XLA Ops:
  0.7 1.6 %key_states_other.1 = (f32[128,128]{1,0:T(8,128)S(1)}, f32[1,128,128]{2,1,0:T(8,128)S(1)}, f32[512,256]{1,0:T(8,128)S(1)}, f32[512,256]{1,0:T(8,128)S(1)}, f32[1,256]{1,0:T(1,128)S(1)}) custom-call(f32[512,256]{1,0:T(8,128)} %k_ref.5, f32[512,256]{1,0:T(8,128)} %v_ref.5, f32[1,256]{1,0:T(1,128)} %bitcast.1), custom_call_target="tpu_custom_call" | custom-call | flops 50331648 | bytes 2099200 | tf_op jit(solution)/shard_map/key_states_other/pallas_call | solution.py:79
  2.3 0.5 %collective-permute-start.2 = (f32[128,128]{1,0:T(8,128)S(1)}, f32[128,128]{1,0:T(8,128)S(1)}, u32[]{:S(2)}, u32[]{:S(2)}) collective-permute-start(f32[128,128]{1,0:T(8,128)S(1)} %get-tuple-element.44), channel_id=1, source_target_pairs={{0,4},{4,0},{8,12},{12,8},{16,20},{20,16},{24,28},{28,24},{1,5},{5... | collective-permute-start | bytes 196616 | tf_op jit(solution)/shard_map/ppermute | solution.py:347
  2.8 0.4 %key_states_mine.1 = (f32[128,128]{1,0:T(8,128)S(1)}, f32[1,128,128]{2,1,0:T(8,128)S(1)}, f32[256,512]{1,0:T(8,128)S(1)}, f32[256,512]{1,0:T(8,128)S(1)}) custom-call(f32[512,256]{1,0:T(8,128)S(1)} %get-tuple-element.34.k_ref, f32[512,256]{1,0:T(8,128)S(1)} %get-tuple-element.35.v_ref, f32[512,256]{1,0:T(8,128)S(1)} %copy-done.2, f32[512,256]{1,0:T(8,128)S(1)} %copy-done.3, ...), custom_call_target="tpu_custom_call" | custom-call | flops 50331648 | bytes 4196352 | tf_op jit(solution)/shard_map/key_states_mine/pallas_call | solution.py:79
  3.3 0.5 %collective-permute-done.2 = f32[128,128]{1,0:T(8,128)S(1)} collective-permute-done((f32[128,128]{1,0:T(8,128)S(1)}, f32[128,128]{1,0:T(8,128)S(1)}, u32[]{:S(2)}, u32[]{:S(2)}) %collective-permute-start.2) | collective-permute-done | bytes 65568 | tf_op jit(solution)/shard_map/ppermute | solution.py:347
  3.7 3.6 %collective-permute-start.3 = (f32[128,128]{1,0:T(8,128)S(1)}, f32[128,128]{1,0:T(8,128)S(1)}, u32[]{:S(2)}, u32[]{:S(2)}) collective-permute-start(f32[128,128]{1,0:T(8,128)S(1)} %add.44), channel_id=1, source_target_pairs={{0,28},{4,24},{8,20},{12,16},{16,12},{20,8},{24,4},{28,0},{1,29},{... | collective-permute-start | bytes 196616 | tf_op jit(solution)/shard_map/ppermute | solution.py:347
  7.4 0.5 %collective-permute-start.4 = (f32[128,128]{1,0:T(8,128)S(1)}, f32[128,128]{1,0:T(8,128)S(1)}, u32[]{:S(2)}, u32[]{:S(2)}) collective-permute-start(f32[128,128]{1,0:T(8,128)S(1)} %add.44), channel_id=1, source_target_pairs={{0,12},{4,8},{8,4},{12,0},{16,28},{20,24},{24,20},{28,16},{1,13},{... | collective-permute-start | bytes 196616 | tf_op jit(solution)/shard_map/ppermute | solution.py:347
  8.1 1.2 %attend_local.1 = (f32[128,512]{1,0:T(8,128)S(1)}, f32[128,512]{1,0:T(8,128)S(1)}) custom-call(f32[256,512]{1,0:T(8,128)S(1)} %get-tuple-element.37.pack_mine_ref.own_ref, f32[256,512]{1,0:T(8,128)S(1)} %get-tuple-element.38.pack_other_ref.pack_ref, f32[512,256]{1,0:T(8,128)S(1)} %get-tuple-element.34.k_ref, f32[512,256]{1,0:T(8,128)S(1)} %get-tuple-element.35.v_ref, ...), custom_call_target="tpu_custom_call" | custom-call | flops 503316480 | bytes 4456448 | tf_op jit(solution)/shard_map/attend_local/pallas_call | solution.py:79
  9.3 0.5 %collective-permute-start.1 = (f32[128,512]{1,0:T(8,128)S(1)}, f32[128,512]{1,0:T(8,128)S(1)}, u32[]{:S(2)}, u32[]{:S(2)}) collective-permute-start(f32[128,512]{1,0:T(8,128)S(1)} %get-tuple-element.42.local_ref), channel_id=1, source_target_pairs={{0,4},{4,0},{8,12},{12,8},{16,20},{20,16},{24,28},{28,24},{1,5},{5... | collective-permute-start | bytes 786440 | tf_op jit(solution)/shard_map/ppermute | solution.py:347
  9.8 1.7 %collective-permute-done.4 = f32[128,128]{1,0:T(8,128)S(1)} collective-permute-done((f32[128,128]{1,0:T(8,128)S(1)}, f32[128,128]{1,0:T(8,128)S(1)}, u32[]{:S(2)}, u32[]{:S(2)}) %collective-permute-start.4) | collective-permute-done | bytes 65568 | tf_op jit(solution)/shard_map/ppermute | solution.py:347
  11.6 0.5 %collective-permute-done.5 = f32[128,128]{1,0:T(8,128)S(1)} collective-permute-done((f32[128,128]{1,0:T(8,128)S(1)}, f32[128,128]{1,0:T(8,128)S(1)}, u32[]{:S(2)}, u32[]{:S(2)}) %collective-permute-start.5) | collective-permute-done | bytes 65568 | tf_op jit(solution)/shard_map/ppermute | solution.py:347
  12.2 0.4 %attend_state.1 = (f32[128,512]{1,0:T(8,128)S(1)}, f32[128,512]{1,0:T(8,128)S(1)}, f32[16,128]{1,0:T(8,128)S(1)}) custom-call(f32[256,512]{1,0:T(8,128)S(1)} %get-tuple-element.37.pack_mine_ref.own_ref, f32[128,512]{1,0:T(8,128)S(1)} %get-tuple-element.41.own_local_ref, f32[256,512]{1,0:T(8,128)S(1)} %collective-permute-done.sib_ref, ...), custom_call_target="tpu_custom_call" | custom-call | flops 100663296 | bytes 3407872 | tf_op jit(solution)/shard_map/attend_state/pallas_call | solution.py:79
  12.7 1.3 %collective-permute-done.6.got_ref = f32[144,128]{1,0:T(8,128)S(1)} collective-permute-done((f32[144,128]{1,0:T(8,128)S(1)}, f32[144,128]{1,0:T(8,128)S(1)}, u32[]{:S(2)}, u32[]{:S(2)}) %collective-permute-start.6) | collective-permute-done | bytes 73760 | tf_op jit(solution)/shard_map/ppermute | solution.py:347
  13.9 2.4 %collective-permute-start.7 = (f32[16,128]{1,0:T(8,128)S(1)}, f32[16,128]{1,0:T(8,128)S(1)}, u32[]{:S(2)}, u32[]{:S(2)}) collective-permute-start(f32[16,128]{1,0:T(8,128)S(1)} %slice_add_fusion.pair_sums_ref), channel_id=1, source_target_pairs={{0,6},{1,7},{2,4},{3,5},{4,2},{5,3},{6,0},{7,1},{8,14},{9,15},{10,... | collective-permute-start | bytes 24584 | tf_op jit(solution)/shard_map/ppermute | solution.py:377
  16.3 1.3 %collective-permute-start.8 = (f32[16,128]{1,0:T(8,128)S(1)}, f32[16,128]{1,0:T(8,128)S(1)}, u32[]{:S(2)}, u32[]{:S(2)}) collective-permute-start(f32[16,128]{1,0:T(8,128)S(1)} %slice_add_fusion.pair_sums_ref), channel_id=1, source_target_pairs={{0,7},{1,6},{2,5},{3,4},{4,3},{5,2},{6,1},{7,0},{8,15},{9,14},{10,... | collective-permute-start | bytes 24584 | tf_op jit(solution)/shard_map/ppermute | solution.py:377
  17.8 0.3 attend_other.1
  18.1 3.1 %collective-permute-done.8 = f32[16,128]{1,0:T(8,128)S(1)} collective-permute-done((f32[16,128]{1,0:T(8,128)S(1)}, f32[16,128]{1,0:T(8,128)S(1)}, u32[]{:S(2)}, u32[]{:S(2)}) %collective-permute-start.8) | collective-permute-done | bytes 8224 | tf_op jit(solution)/shard_map/ppermute | solution.py:377
  21.2 0.4 %grad_states.1 = (f32[128,128]{1,0:T(8,128)S(1)}, f32[128,128]{1,0:T(8,128)S(1)}, f32[128,128]{1,0:T(8,128)S(1)}, f32[1,128,128]{2,1,0:T(8,128)S(1)}, bf16[128,5...) custom-call(f32[16,128]{1,0:T(8,128)S(1)} %add_add_fusion.sums_ref, ...), custom_call_target="tpu_custom_call" | custom-call | flops 100663296 | bytes 3162112 | tf_op jit(solution)/shard_map/grad_states/pallas_call | solution.py:79
  21.5 2.2 %collective-permute-start.10 = (f32[128,128]{1,0:T(8,128)S(1)}, f32[128,128]{1,0:T(8,128)S(1)}, u32[]{:S(2)}, u32[]{:S(2)}) collective-permute-start(f32[128,128]{1,0:T(8,128)S(1)} %get-tuple-element.56), channel_id=1, source_target_pairs={{0,28},{4,24},{8,20},{12,16},{16,12},{20,8},{24,4},{28,0},{1,29},{... | collective-permute-start | bytes 196616 | tf_op jit(solution)/shard_map/ppermute | solution.py:347
  23.7 0.3 collective-permute-start.11
  24.0 0.8 %collective-permute-start.12 = (f32[128,128]{1,0:T(8,128)S(1)}, f32[128,128]{1,0:T(8,128)S(1)}, u32[]{:S(2)}, u32[]{:S(2)}) collective-permute-start(f32[128,128]{1,0:T(8,128)S(1)} %get-tuple-element.56), channel_id=1, source_target_pairs={{0,16},{4,20},{8,24},{12,28},{16,0},{20,4},{24,8},{28,12},{1,17},{... | collective-permute-start | bytes 196616 | tf_op jit(solution)/shard_map/ppermute | solution.py:347
  24.8 2.8 %grads_local.1 = (f32[512,256]{1,0:T(8,128)}, f32[512,256]{1,0:T(8,128)S(1)}, f32[512,256]{1,0:T(8,128)S(1)}, f32[1,128,128]{2,1,0:T(8,128)S(1)}, f32[128,128]{1,0:T(8,128)S(1)}) custom-call(f32[16,128]{1,0:T(8,128)S(1)} %add_add_fusion.sums_ref, f32[144,128]{1,0:T(8,128)S(1)} %collective-permute-done.6.got_ref, ...), custom_call_target="tpu_custom_call" | custom-call | flops 1409286144 | bytes 5931008 | tf_op jit(solution)/shard_map/grads_local/pallas_call | solution.py:79
  27.8 0.6 %collective-permute-done.12 = f32[128,128]{1,0:T(8,128)S(1)} collective-permute-done((f32[128,128]{1,0:T(8,128)S(1)}, f32[128,128]{1,0:T(8,128)S(1)}, u32[]{:S(2)}, u32[]{:S(2)}) %collective-permute-start.12) | collective-permute-done | bytes 65568 | tf_op jit(solution)/shard_map/ppermute | solution.py:347
  28.5 1.1 %grads_state_mine.1 = (f32[512,256]{1,0:T(8,128)}, f32[512,256]{1,0:T(8,128)}) custom-call(f32[512,256]{1,0:T(8,128)S(1)} %copy-done, f32[512,256]{1,0:T(8,128)S(1)} %copy-done.1, f32[512,256]{1,0:T(8,128)S(1)} %get-tuple-element.54.gk_local_ref, f32[512,256]{1,0:T(8,128)S(1)} %get-tuple-element.55.gv_local_ref, f32[128,128]{1,0:T(8,128)S(1)} %get-tuple-element.65.state_ref, ...), custom_call_target="tpu_custom_call" | custom-call | flops 100663296 | bytes 4456448 | tf_op jit(solution)/shard_map/grads_state_mine/pallas_call | solution.py:79
  29.8 1.1 %grads_state_other.1 = (f32[512,256]{1,0:T(8,128)}, f32[512,256]{1,0:T(8,128)}) custom-call(f32[512,256]{1,0:T(8,128)S(1)} %copy-done, f32[512,256]{1,0:T(8,128)S(1)} %copy-done.1, f32[512,256]{1,0:T(8,128)S(1)} %get-tuple-element.54.gk_local_ref, f32[512,256]{1,0:T(8,128)S(1)} %get-tuple-element.55.gv_local_ref, ...), custom_call_target="tpu_custom_call", output_to_operand_aliasing={{0}: (6, {}), {1}: (7, {})} | custom-call | flops 100663296 | bytes 6553600 | tf_op jit(solution)/shard_map/grads_state_other/pallas_call | solution.py:79
  (29 shorter events, 1.2 us)
Async XLA Ops:
  0.6 2.2 %copy-start.2 = (f32[512,256]{1,0:T(8,128)S(1)}, f32[512,256]{1,0:T(8,128)}, u32[]{:S(2)}) copy-start(f32[512,256]{1,0:T(8,128)} %q_ref.1) | copy-start | bytes 1572868
  0.6 2.2 %copy-start.3 = (f32[512,256]{1,0:T(8,128)S(1)}, f32[512,256]{1,0:T(8,128)}, u32[]{:S(2)}) copy-start(f32[512,256]{1,0:T(8,128)} %cot_ref.1) | copy-start | bytes 1572868
  2.3 1.4 %collective-permute-start.2 = (f32[128,128]{1,0:T(8,128)S(1)}, f32[128,128]{1,0:T(8,128)S(1)}, u32[]{:S(2)}, u32[]{:S(2)}) collective-permute-start(f32[128,128]{1,0:T(8,128)S(1)} %get-tuple-element.44), channel_id=1, source_target_pairs={{0,4},{4,0},{8,12},{12,8},{16,20},{20,16},{24,28},{28,24},{1,5},{5... | collective-permute-start | bytes 196616 | tf_op jit(solution)/shard_map/ppermute | solution.py:347
  3.7 6.1 %collective-permute-start.3 = (f32[128,128]{1,0:T(8,128)S(1)}, f32[128,128]{1,0:T(8,128)S(1)}, u32[]{:S(2)}, u32[]{:S(2)}) collective-permute-start(f32[128,128]{1,0:T(8,128)S(1)} %add.44), channel_id=1, source_target_pairs={{0,28},{4,24},{8,20},{12,16},{16,12},{20,8},{24,4},{28,0},{1,29},{... | collective-permute-start | bytes 196616 | tf_op jit(solution)/shard_map/ppermute | solution.py:347
  7.4 4.2 %collective-permute-start.4 = (f32[128,128]{1,0:T(8,128)S(1)}, f32[128,128]{1,0:T(8,128)S(1)}, u32[]{:S(2)}, u32[]{:S(2)}) collective-permute-start(f32[128,128]{1,0:T(8,128)S(1)} %add.44), channel_id=1, source_target_pairs={{0,12},{4,8},{8,4},{12,0},{16,28},{20,24},{24,20},{28,16},{1,13},{... | collective-permute-start | bytes 196616 | tf_op jit(solution)/shard_map/ppermute | solution.py:347
  7.9 4.3 %collective-permute-start.5 = (f32[128,128]{1,0:T(8,128)S(1)}, f32[128,128]{1,0:T(8,128)S(1)}, u32[]{:S(2)}, u32[]{:S(2)}) collective-permute-start(f32[128,128]{1,0:T(8,128)S(1)} %add.44), channel_id=1, source_target_pairs={{0,16},{4,20},{8,24},{12,28},{16,0},{20,4},{24,8},{28,12},{1,17},{... | collective-permute-start | bytes 196616 | tf_op jit(solution)/shard_map/ppermute | solution.py:347
  8.0 4.2 %collective-permute-start = (f32[256,512]{1,0:T(8,128)S(1)}, f32[256,512]{1,0:T(8,128)S(1)}, u32[]{:S(2)}, u32[]{:S(2)}) collective-permute-start(f32[256,512]{1,0:T(8,128)S(1)} %get-tuple-element.38.pack_other_ref.pack_ref), channel_id=1, source_target_pairs={{0,4},{4,0},{8,12},{12,8},{16,20},{20,16},{24,28},{28,24},{1,5},{5... | collective-permute-start | bytes 1572872 | tf_op jit(solution)/shard_map/ppermute | solution.py:347
  9.3 2.9 %collective-permute-start.1 = (f32[128,512]{1,0:T(8,128)S(1)}, f32[128,512]{1,0:T(8,128)S(1)}, u32[]{:S(2)}, u32[]{:S(2)}) collective-permute-start(f32[128,512]{1,0:T(8,128)S(1)} %get-tuple-element.42.local_ref), channel_id=1, source_target_pairs={{0,4},{4,0},{8,12},{12,8},{16,20},{20,16},{24,28},{28,24},{1,5},{5... | collective-permute-start | bytes 786440 | tf_op jit(solution)/shard_map/ppermute | solution.py:347
  12.6 1.3 %collective-permute-start.6 = (f32[144,128]{1,0:T(8,128)S(1)}, f32[144,128]{1,0:T(8,128)S(1)}, u32[]{:S(2)}, u32[]{:S(2)}) collective-permute-start(f32[144,128]{1,0:T(8,128)S(1)} %pad_maximum_fusion), channel_id=1, source_target_pairs={{0,4},{4,0},{8,12},{12,8},{16,20},{20,16},{24,28},{28,24},{1,5},{5... | collective-permute-start | bytes 221192 | tf_op jit(solution)/shard_map/ppermute | solution.py:347
  13.9 4.2 %collective-permute-start.7 = (f32[16,128]{1,0:T(8,128)S(1)}, f32[16,128]{1,0:T(8,128)S(1)}, u32[]{:S(2)}, u32[]{:S(2)}) collective-permute-start(f32[16,128]{1,0:T(8,128)S(1)} %slice_add_fusion.pair_sums_ref), channel_id=1, source_target_pairs={{0,6},{1,7},{2,4},{3,5},{4,2},{5,3},{6,0},{7,1},{8,14},{9,15},{10,... | collective-permute-start | bytes 24584 | tf_op jit(solution)/shard_map/ppermute | solution.py:377
  16.3 4.9 %collective-permute-start.8 = (f32[16,128]{1,0:T(8,128)S(1)}, f32[16,128]{1,0:T(8,128)S(1)}, u32[]{:S(2)}, u32[]{:S(2)}) collective-permute-start(f32[16,128]{1,0:T(8,128)S(1)} %slice_add_fusion.pair_sums_ref), channel_id=1, source_target_pairs={{0,7},{1,6},{2,5},{3,4},{4,3},{5,2},{6,1},{7,0},{8,15},{9,14},{10,... | collective-permute-start | bytes 24584 | tf_op jit(solution)/shard_map/ppermute | solution.py:377
  17.6 3.6 %collective-permute-start.9 = (f32[16,128]{1,0:T(8,128)S(1)}, f32[16,128]{1,0:T(8,128)S(1)}, u32[]{:S(2)}, u32[]{:S(2)}) collective-permute-start(f32[16,128]{1,0:T(8,128)S(1)} %slice_add_fusion.pair_sums_ref), channel_id=1, source_target_pairs={{0,5},{1,4},{2,7},{3,6},{4,1},{5,0},{6,3},{7,2},{8,13},{9,12},{10,... | collective-permute-start | bytes 24584 | tf_op jit(solution)/shard_map/ppermute | solution.py:377
  21.1 3.7 %copy-start = (f32[512,256]{1,0:T(8,128)S(1)}, f32[512,256]{1,0:T(8,128)}, u32[]{:S(2)}) copy-start(f32[512,256]{1,0:T(8,128)} %k_ref.5) | copy-start | bytes 1572868
  21.2 3.7 %copy-start.1 = (f32[512,256]{1,0:T(8,128)S(1)}, f32[512,256]{1,0:T(8,128)}, u32[]{:S(2)}) copy-start(f32[512,256]{1,0:T(8,128)} %v_ref.5) | copy-start | bytes 1572868
  21.5 6.1 %collective-permute-start.10 = (f32[128,128]{1,0:T(8,128)S(1)}, f32[128,128]{1,0:T(8,128)S(1)}, u32[]{:S(2)}, u32[]{:S(2)}) collective-permute-start(f32[128,128]{1,0:T(8,128)S(1)} %get-tuple-element.56), channel_id=1, source_target_pairs={{0,28},{4,24},{8,20},{12,16},{16,12},{20,8},{24,4},{28,0},{1,29},{... | collective-permute-start | bytes 196616 | tf_op jit(solution)/shard_map/ppermute | solution.py:347
  23.7 4.1 %collective-permute-start.11 = (f32[128,128]{1,0:T(8,128)S(1)}, f32[128,128]{1,0:T(8,128)S(1)}, u32[]{:S(2)}, u32[]{:S(2)}) collective-permute-start(f32[128,128]{1,0:T(8,128)S(1)} %get-tuple-element.56), channel_id=1, source_target_pairs={{0,12},{4,8},{8,4},{12,0},{16,28},{20,24},{24,20},{28,16},{1,13},{... | collective-permute-start | bytes 196616 | tf_op jit(solution)/shard_map/ppermute | solution.py:347
  24.0 4.3 %collective-permute-start.12 = (f32[128,128]{1,0:T(8,128)S(1)}, f32[128,128]{1,0:T(8,128)S(1)}, u32[]{:S(2)}, u32[]{:S(2)}) collective-permute-start(f32[128,128]{1,0:T(8,128)S(1)} %get-tuple-element.56), channel_id=1, source_target_pairs={{0,16},{4,20},{8,24},{12,28},{16,0},{20,4},{24,8},{28,12},{1,17},{... | collective-permute-start | bytes 196616 | tf_op jit(solution)/shard_map/ppermute | solution.py:347
  28.4 1.3 %collective-permute-start.13 = (f32[128,128]{1,0:T(8,128)S(1)}, f32[128,128]{1,0:T(8,128)S(1)}, u32[]{:S(2)}, u32[]{:S(2)}) collective-permute-start(f32[128,128]{1,0:T(8,128)S(1)} %select_add_fusion.1), channel_id=1, source_target_pairs={{0,4},{4,0},{8,12},{12,8},{16,20},{20,16},{24,28},{28,24},{1,5},{5... | collective-permute-start | bytes 196616 | tf_op jit(solution)/shard_map/ppermute | solution.py:347

commit v7 on v6

--- a/solution.py
+++ b/solution.py
@@ -50,6 +50,11 @@
     if transposed:
         return jnp.concatenate([beside(high, high), beside(low, jnp.zeros_like(low))], axis=0)
     return jnp.concatenate([beside(high, low), beside(high, jnp.zeros_like(low))], axis=0)
+
+
+def product_parts(left, operand, transposed):
+    wide = mul(left, operand, NT if transposed else NN)
+    return wide[:, :HD] + wide[:, HD:]
 
 
 def product_state(left, operand, transposed):
@@ -260,7 +265,7 @@
     pair_ref[...] = own_total_ref[...] + sib_total_ref[...]
 
 
-def grads_local(full_width, sums_ref, got_ref, high_ref, low_ref, att_other_ref, pack_mine_ref, pack_other_ref, k_ref, v_ref, keep_ref, before_mine_ref, before_other_ref, total_ref, gq_hbm, gk_ref, gv_ref, after_ref, same_total_ref, gq_ref, grad_high, grad_low, sems):
+def grads_local(full_width, sums_ref, got_ref, high_ref, low_ref, att_other_ref, pack_mine_ref, pack_other_ref, k_ref, v_ref, keep_ref, before_mine_ref, before_other_ref, total_ref, gq_hbm, gk_ref, gv_ref, after_ref, same_total_ref, k_parts_ref, v_parts_ref, gq_ref, grad_high, grad_low, sems):
     rows, width = k_ref.shape
     half = width // 2
     sums_rows = 4 * rows // LANES
@@ -309,6 +314,8 @@
             for row in blocks(rows):
                 grad = grad_high[row, place], grad_low[row, place]
                 query, key, value = split(pack_ref[head, row].T), split(k_ref[row, col]), split(v_ref[row, col])
+                parts = slice(2 * place.start, 2 * place.stop)
+                k_parts_ref[row, parts], v_parts_ref[row, parts] = beside(*key), beside(*value)
                 mask = causal_mask(row.stop - row.start, True)
                 mixing = jnp.where(mask, product_nt(value, grad), 0.0)
                 gk_ref[row, place] = product_nn(split(mixing), query)
@@ -320,7 +327,7 @@
 
 def grads_state(mine, k_ref, v_ref, gk_local_ref, gv_local_ref, state_ref, after_ref, *refs):
     gk_hbm, gv_hbm, gk_ref, gv_ref, sems = refs[-5:]
-    rows, width = k_ref.shape
+    rows, width = gk_local_ref.shape
     half = width // 2
     last = len(blocks(rows)) - 1
     copies = []
@@ -332,11 +339,12 @@
     for head in heads(half):
         col = half_cols(half, mine, head.start, HD)
         place = head if mine else slice(half + head.start, half + head.stop)
+        parts = slice(2 * place.start, 2 * place.stop)
         for n, row in enumerate(blocks(rows)):
             here = state_ref[head, :] if n == last else state_ref[head, :] + after_ref[n, head, :]
-            gk_ref[row, head] = gk_local_ref[row, place] + product_state(split(v_ref[row, col]), state_operand(here, False), False)
+            gk_ref[row, head] = gk_local_ref[row, place] + product_parts(v_ref[row, parts], state_operand(here, False), False)
             leave(gk_ref, gk_hbm, row, head, col)
-            gv_ref[row, head] = gv_local_ref[row, place] + product_state(split(k_ref[row, col]), state_operand(here, True), True)
+            gv_ref[row, head] = gv_local_ref[row, place] + product_parts(k_ref[row, parts], state_operand(here, True), True)
             leave(gv_ref, gv_hbm, row, head, col)
     for copy in copies:
         copy.wait()
@@ -353,7 +361,7 @@
     ahead = lambda d: (chip ^ d) > chip if reverse else (chip ^ d) < chip
     total = jnp.zeros_like(pair)
     if on_grid():
-        got = [(d, swap(pair, "seq", 2 * d + d % 2)) for d in (3, 1, 2)]
+        got = [(d, swap(pair, "seq", 2 * d + d % 2)) for d in (2, 1, 3)]
         for d, part in got:
             total = total + jnp.where(ahead(d), part, 0.0)
         return total
@@ -372,7 +380,7 @@
         return lax.psum(same_x, "head")
     parts = []
     seqs = range(lax.axis_size("seq"))
-    for d in sorted(range(1, count), key=lambda d: (d != count // 2, -d)):
+    for d in sorted(range(1, count), key=lambda d: (d == count // 2, d)):
         pairs = [(i * count + z, (i ^ 1) * count + (z ^ d)) for i in seqs for z in range(count)]
         parts.append(lax.ppermute(x, ("seq", "head"), pairs))
     for part in parts:
@@ -428,8 +436,9 @@
         [sums, pack_mine, sibling, attended, sibling_attended],
     )
     later = from_other_chips(pair, True)
-    grad_q, local_k, local_v, after_other, own_grad = call(
-        functools.partial(grads_local, full_width), "grads_local", [whole, whole, whole, inner, state], 14 * square,
+    grad_q, local_k, local_v, after_other, own_grad, key_parts, value_parts = call(
+        functools.partial(grads_local, full_width), "grads_local",
+        [whole, whole, whole, inner, state, ((rows, 2 * width), BF16), ((rows, 2 * width), BF16)], 14 * square,
         [sums, got, high, low, attended_other, pack_mine, pack_other, keys, values, keep, before_mine, before_other, own_grad],
         [pltpu.VMEM(whole, F32), pltpu.VMEM(whole, BF16), pltpu.VMEM(whole, BF16), pltpu.SemaphoreType.DMA((units,))],
         hbm_out=(0,),
@@ -439,11 +448,11 @@
     scratch = [pltpu.VMEM(halves, F32), pltpu.VMEM(halves, F32), pltpu.SemaphoreType.DMA((units,))]
     grad_k, grad_v = call(
         functools.partial(grads_state, True), "grads_state_mine", [whole] * 2, square,
-        [keys, values, local_k, local_v, keep_later, after_mine], scratch, hbm_out=(0, 1),
+        [key_parts, value_parts, local_k, local_v, keep_later, after_mine], scratch, hbm_out=(0, 1),
     )
     grad_k, grad_v = call(
         functools.partial(grads_state, False), "grads_state_other", [whole] * 2, square,
-        [keys, values, local_k, local_v, got_later, after_other, grad_k, grad_v], scratch,
+        [key_parts, value_parts, local_k, local_v, got_later, after_other, grad_k, grad_v], scratch,
         hbm_in=(6, 7), hbm_out=(0, 1), aliases={6: 0, 7: 1},
     )
     return grad_q, grad_k, grad_v

time: 31 us -> 30.9 us (level)
  no operation moved by 1% of the time
where the time goes in v7:
time: 30.9 us; the launch traced here: 30.8 us
  starting transfers between devices  12.7 us (41%)
  Pallas kernels  9.1 us (29%)
  waiting for transfers between devices  8.1 us (26%)
  between operations  0.82 us (3%)
    pallas_call x9, Pallas kernels, call(): pl.pallas_call(body, out_shape=outs, in_specs=[place(i in hbm_in) for i i...  9.1 us
    ppermute x11, starting transfers between devices, swap(): return lax.ppermute(x, axis, [(i, i ^ distance) for i in range(count)])  8.78 us
    ppermute x11, waiting for transfers between devices, swap(): return lax.ppermute(x, axis, [(i, i ^ distance) for i in range(count)])  5.05 us
    ppermute x3, starting transfers between devices, sum_over_heads(): parts.append(lax.ppermute(x, ('seq', 'head'), pairs))  3.89 us
    ppermute x3, waiting for transfers between devices, sum_over_heads(): parts.append(lax.ppermute(x, ('seq', 'head'), pairs))  3.06 us
  transfers between devices with their start and end apart: 14, of which 9 were waited for; matrix products, arithmetic and copies ran while one was open for 0% of the time, Pallas kernels for 18%

profile of v7, /device:TPU:0, one launch (start us, length us, event | category | flops | bytes accessed | tf_op | source)
XLA Modules:
  0.0 30.8 jit_solution(15550048643727077668)
XLA Ops:
  0.7 1.6 %key_states_other.1 = (f32[128,128]{1,0:T(8,128)S(1)}, f32[1,128,128]{2,1,0:T(8,128)S(1)}, f32[512,256]{1,0:T(8,128)S(1)}, f32[512,256]{1,0:T(8,128)S(1)}, f32[1,256]{1,0:T(1,128)S(1)}) custom-call(f32[512,256]{1,0:T(8,128)} %k_ref.1, f32[512,256]{1,0:T(8,128)} %v_ref.1, f32[1,256]{1,0:T(1,128)} %bitcast.1), custom_call_target="tpu_custom_call" | custom-call | flops 50331648 | bytes 2099200 | tf_op jit(solution)/shard_map/key_states_other/pallas_call | solution.py:84
  2.3 0.5 %collective-permute-start.2 = (f32[128,128]{1,0:T(8,128)S(1)}, f32[128,128]{1,0:T(8,128)S(1)}, u32[]{:S(2)}, u32[]{:S(2)}) collective-permute-start(f32[128,128]{1,0:T(8,128)S(1)} %get-tuple-element.46), channel_id=1, source_target_pairs={{0,4},{4,0},{8,12},{12,8},{16,20},{20,16},{24,28},{28,24},{1,5},{5... | collective-permute-start | bytes 196616 | tf_op jit(solution)/shard_map/ppermute | solution.py:355
  2.8 0.4 %key_states_mine.1 = (f32[128,128]{1,0:T(8,128)S(1)}, f32[1,128,128]{2,1,0:T(8,128)S(1)}, f32[256,512]{1,0:T(8,128)S(1)}, f32[256,512]{1,0:T(8,128)S(1)}) custom-call(f32[512,256]{1,0:T(8,128)S(1)} %get-tuple-element.36.k_ref, f32[512,256]{1,0:T(8,128)S(1)} %get-tuple-element.37.v_ref, f32[512,256]{1,0:T(8,128)S(1)} %copy-done.2, f32[512,256]{1,0:T(8,128)S(1)} %copy-done.3, ...), custom_call_target="tpu_custom_call" | custom-call | flops 50331648 | bytes 4196352 | tf_op jit(solution)/shard_map/key_states_mine/pallas_call | solution.py:84
  3.3 0.5 %collective-permute-done.2 = f32[128,128]{1,0:T(8,128)S(1)} collective-permute-done((f32[128,128]{1,0:T(8,128)S(1)}, f32[128,128]{1,0:T(8,128)S(1)}, u32[]{:S(2)}, u32[]{:S(2)}) %collective-permute-start.2) | collective-permute-done | bytes 65568 | tf_op jit(solution)/shard_map/ppermute | solution.py:355
  3.7 3.6 %collective-permute-start.5 = (f32[128,128]{1,0:T(8,128)S(1)}, f32[128,128]{1,0:T(8,128)S(1)}, u32[]{:S(2)}, u32[]{:S(2)}) collective-permute-start(f32[128,128]{1,0:T(8,128)S(1)} %add.44), channel_id=1, source_target_pairs={{0,28},{4,24},{8,20},{12,16},{16,12},{20,8},{24,4},{28,0},{1,29},{... | collective-permute-start | bytes 196616 | tf_op jit(solution)/shard_map/ppermute | solution.py:355
  7.4 0.5 %collective-permute-start.4 = (f32[128,128]{1,0:T(8,128)S(1)}, f32[128,128]{1,0:T(8,128)S(1)}, u32[]{:S(2)}, u32[]{:S(2)}) collective-permute-start(f32[128,128]{1,0:T(8,128)S(1)} %add.44), channel_id=1, source_target_pairs={{0,12},{4,8},{8,4},{12,0},{16,28},{20,24},{24,20},{28,16},{1,13},{... | collective-permute-start | bytes 196616 | tf_op jit(solution)/shard_map/ppermute | solution.py:355
  8.1 1.2 %attend_local.1 = (f32[128,512]{1,0:T(8,128)S(1)}, f32[128,512]{1,0:T(8,128)S(1)}) custom-call(f32[256,512]{1,0:T(8,128)S(1)} %get-tuple-element.39.pack_mine_ref.own_ref, f32[256,512]{1,0:T(8,128)S(1)} %get-tuple-element.40.pack_other_ref.pack_ref, f32[512,256]{1,0:T(8,128)S(1)} %get-tuple-element.36.k_ref, f32[512,256]{1,0:T(8,128)S(1)} %get-tuple-element.37.v_ref, ...), custom_call_target="tpu_custom_call" | custom-call | flops 503316480 | bytes 4456448 | tf_op jit(solution)/shard_map/attend_local/pallas_call | solution.py:84
  9.3 0.5 %collective-permute-start.1 = (f32[128,512]{1,0:T(8,128)S(1)}, f32[128,512]{1,0:T(8,128)S(1)}, u32[]{:S(2)}, u32[]{:S(2)}) collective-permute-start(f32[128,512]{1,0:T(8,128)S(1)} %get-tuple-element.44.local_ref), channel_id=1, source_target_pairs={{0,4},{4,0},{8,12},{12,8},{16,20},{20,16},{24,28},{28,24},{1,5},{5... | collective-permute-start | bytes 786440 | tf_op jit(solution)/shard_map/ppermute | solution.py:355
  9.8 1.7 %collective-permute-done.4 = f32[128,128]{1,0:T(8,128)S(1)} collective-permute-done((f32[128,128]{1,0:T(8,128)S(1)}, f32[128,128]{1,0:T(8,128)S(1)}, u32[]{:S(2)}, u32[]{:S(2)}) %collective-permute-start.4) | collective-permute-done | bytes 65568 | tf_op jit(solution)/shard_map/ppermute | solution.py:355
  11.6 0.5 %collective-permute-done.3 = f32[128,128]{1,0:T(8,128)S(1)} collective-permute-done((f32[128,128]{1,0:T(8,128)S(1)}, f32[128,128]{1,0:T(8,128)S(1)}, u32[]{:S(2)}, u32[]{:S(2)}) %collective-permute-start.3) | collective-permute-done | bytes 65568 | tf_op jit(solution)/shard_map/ppermute | solution.py:355
  12.2 0.4 %attend_state.1 = (f32[128,512]{1,0:T(8,128)S(1)}, f32[128,512]{1,0:T(8,128)S(1)}, f32[16,128]{1,0:T(8,128)S(1)}) custom-call(f32[256,512]{1,0:T(8,128)S(1)} %get-tuple-element.39.pack_mine_ref.own_ref, f32[128,512]{1,0:T(8,128)S(1)} %get-tuple-element.43.own_local_ref, f32[256,512]{1,0:T(8,128)S(1)} %collective-permute-done.sib_ref, ...), custom_call_target="tpu_custom_call" | custom-call | flops 100663296 | bytes 3407872 | tf_op jit(solution)/shard_map/attend_state/pallas_call | solution.py:84
  12.7 1.3 %collective-permute-done.6.got_ref = f32[144,128]{1,0:T(8,128)S(1)} collective-permute-done((f32[144,128]{1,0:T(8,128)S(1)}, f32[144,128]{1,0:T(8,128)S(1)}, u32[]{:S(2)}, u32[]{:S(2)}) %collective-permute-start.6) | collective-permute-done | bytes 73760 | tf_op jit(solution)/shard_map/ppermute | solution.py:355
  13.9 2.4 %collective-permute-start.9 = (f32[16,128]{1,0:T(8,128)S(1)}, f32[16,128]{1,0:T(8,128)S(1)}, u32[]{:S(2)}, u32[]{:S(2)}) collective-permute-start(f32[16,128]{1,0:T(8,128)S(1)} %slice_add_fusion.pair_sums_ref), channel_id=1, source_target_pairs={{0,6},{1,7},{2,4},{3,5},{4,2},{5,3},{6,0},{7,1},{8,14},{9,15},{10,... | collective-permute-start | bytes 24584 | tf_op jit(solution)/shard_map/ppermute | solution.py:385
  16.3 1.3 %collective-permute-start.8 = (f32[16,128]{1,0:T(8,128)S(1)}, f32[16,128]{1,0:T(8,128)S(1)}, u32[]{:S(2)}, u32[]{:S(2)}) collective-permute-start(f32[16,128]{1,0:T(8,128)S(1)} %slice_add_fusion.pair_sums_ref), channel_id=1, source_target_pairs={{0,7},{1,6},{2,5},{3,4},{4,3},{5,2},{6,1},{7,0},{8,15},{9,14},{10,... | collective-permute-start | bytes 24584 | tf_op jit(solution)/shard_map/ppermute | solution.py:385
  17.8 0.3 attend_other.1
  18.1 3.1 %collective-permute-done.8 = f32[16,128]{1,0:T(8,128)S(1)} collective-permute-done((f32[16,128]{1,0:T(8,128)S(1)}, f32[16,128]{1,0:T(8,128)S(1)}, u32[]{:S(2)}, u32[]{:S(2)}) %collective-permute-start.8) | collective-permute-done | bytes 8224 | tf_op jit(solution)/shard_map/ppermute | solution.py:385
  21.2 0.4 %grad_states.1 = (f32[128,128]{1,0:T(8,128)S(1)}, f32[128,128]{1,0:T(8,128)S(1)}, f32[128,128]{1,0:T(8,128)S(1)}, f32[1,128,128]{2,1,0:T(8,128)S(1)}, bf16[128,5...) custom-call(f32[16,128]{1,0:T(8,128)S(1)} %add_add_fusion.sums_ref, ...), custom_call_target="tpu_custom_call" | custom-call | flops 100663296 | bytes 3162112 | tf_op jit(solution)/shard_map/grad_states/pallas_call | solution.py:84
  21.5 2.2 %collective-permute-start.12 = (f32[128,128]{1,0:T(8,128)S(1)}, f32[128,128]{1,0:T(8,128)S(1)}, u32[]{:S(2)}, u32[]{:S(2)}) collective-permute-start(f32[128,128]{1,0:T(8,128)S(1)} %get-tuple-element.60), channel_id=1, source_target_pairs={{0,28},{4,24},{8,20},{12,16},{16,12},{20,8},{24,4},{28,0},{1,29},{... | collective-permute-start | bytes 196616 | tf_op jit(solution)/shard_map/ppermute | solution.py:355
  23.7 0.3 collective-permute-start.11
  24.0 0.8 %collective-permute-start.10 = (f32[128,128]{1,0:T(8,128)S(1)}, f32[128,128]{1,0:T(8,128)S(1)}, u32[]{:S(2)}, u32[]{:S(2)}) collective-permute-start(f32[128,128]{1,0:T(8,128)S(1)} %get-tuple-element.60), channel_id=1, source_target_pairs={{0,16},{4,20},{8,24},{12,28},{16,0},{20,4},{24,8},{28,12},{1,17},{... | collective-permute-start | bytes 196616 | tf_op jit(solution)/shard_map/ppermute | solution.py:355
  24.8 2.8 %grads_local.1 = (f32[512,256]{1,0:T(8,128)}, f32[512,256]{1,0:T(8,128)S(1)}, f32[512,256]{1,0:T(8,128)S(1)}, f32[1,128,128]{2,1,0:T(8,128)S(1)}, f32[128,128]{1...) custom-call(f32[16,128]{1,0:T(8,128)S(1)} %add_add_fusion.sums_ref, ...), custom_call_target="tpu_custom_call" | custom-call | flops 1409286144 | bytes 5931008 | tf_op jit(solution)/shard_map/grads_local/pallas_call | solution.py:84
  27.8 0.6 %collective-permute-done.10 = f32[128,128]{1,0:T(8,128)S(1)} collective-permute-done((f32[128,128]{1,0:T(8,128)S(1)}, f32[128,128]{1,0:T(8,128)S(1)}, u32[]{:S(2)}, u32[]{:S(2)}) %collective-permute-start.10) | collective-permute-done | bytes 65568 | tf_op jit(solution)/shard_map/ppermute | solution.py:355
  28.5 1.1 %grads_state_mine.1 = (f32[512,256]{1,0:T(8,128)}, f32[512,256]{1,0:T(8,128)}) custom-call(bf16[512,512]{1,0:T(8,128)(2,1)S(1)} %get-tuple-element.56.k_ref, bf16[512,512]{1,0:T(8,128)(2,1)S(1)} %get-tuple-element.57.v_ref, f32[512,256]{1,0:T(8,128)S(1)} %get-tuple-element.58.gk_local_ref, f32[512,256]{1,0:T(8,128)S(1)} %get-tuple-element.59.gv_local_ref, ...), custom_call_target="tpu_custom_call" | custom-call | flops 100663296 | bytes 4456448 | tf_op jit(solution)/shard_map/grads_state_mine/pallas_call | solution.py:84
  29.8 1.0 %grads_state_other.1 = (f32[512,256]{1,0:T(8,128)}, f32[512,256]{1,0:T(8,128)}) custom-call(bf16[512,512]{1,0:T(8,128)(2,1)S(1)} %get-tuple-element.56.k_ref, bf16[512,512]{1,0:T(8,128)(2,1)S(1)} %get-tuple-element.57.v_ref, f32[512,256]{1,0:T(8,128)S(1)} %get-tuple-element.58.gk_local_ref, ...), custom_call_target="tpu_custom_call", output_to_operand_aliasing={{0}: (6, {}), {1}: (7, {})} | custom-call | flops 100663296 | bytes 6553600 | tf_op jit(solution)/shard_map/grads_state_other/pallas_call | solution.py:84
  (29 shorter events, 1.2 us)
Async XLA Ops:
  0.6 2.2 %copy-start.2 = (f32[512,256]{1,0:T(8,128)S(1)}, f32[512,256]{1,0:T(8,128)}, u32[]{:S(2)}) copy-start(f32[512,256]{1,0:T(8,128)} %q_ref.1) | copy-start | bytes 1572868
  0.6 2.2 %copy-start.3 = (f32[512,256]{1,0:T(8,128)S(1)}, f32[512,256]{1,0:T(8,128)}, u32[]{:S(2)}) copy-start(f32[512,256]{1,0:T(8,128)} %cot_ref.1) | copy-start | bytes 1572868
  2.3 1.4 %collective-permute-start.2 = (f32[128,128]{1,0:T(8,128)S(1)}, f32[128,128]{1,0:T(8,128)S(1)}, u32[]{:S(2)}, u32[]{:S(2)}) collective-permute-start(f32[128,128]{1,0:T(8,128)S(1)} %get-tuple-element.46), channel_id=1, source_target_pairs={{0,4},{4,0},{8,12},{12,8},{16,20},{20,16},{24,28},{28,24},{1,5},{5... | collective-permute-start | bytes 196616 | tf_op jit(solution)/shard_map/ppermute | solution.py:355
  3.7 6.1 %collective-permute-start.5 = (f32[128,128]{1,0:T(8,128)S(1)}, f32[128,128]{1,0:T(8,128)S(1)}, u32[]{:S(2)}, u32[]{:S(2)}) collective-permute-start(f32[128,128]{1,0:T(8,128)S(1)} %add.44), channel_id=1, source_target_pairs={{0,28},{4,24},{8,20},{12,16},{16,12},{20,8},{24,4},{28,0},{1,29},{... | collective-permute-start | bytes 196616 | tf_op jit(solution)/shard_map/ppermute | solution.py:355
  7.4 4.2 %collective-permute-start.4 = (f32[128,128]{1,0:T(8,128)S(1)}, f32[128,128]{1,0:T(8,128)S(1)}, u32[]{:S(2)}, u32[]{:S(2)}) collective-permute-start(f32[128,128]{1,0:T(8,128)S(1)} %add.44), channel_id=1, source_target_pairs={{0,12},{4,8},{8,4},{12,0},{16,28},{20,24},{24,20},{28,16},{1,13},{... | collective-permute-start | bytes 196616 | tf_op jit(solution)/shard_map/ppermute | solution.py:355
  7.9 4.3 %collective-permute-start.3 = (f32[128,128]{1,0:T(8,128)S(1)}, f32[128,128]{1,0:T(8,128)S(1)}, u32[]{:S(2)}, u32[]{:S(2)}) collective-permute-start(f32[128,128]{1,0:T(8,128)S(1)} %add.44), channel_id=1, source_target_pairs={{0,16},{4,20},{8,24},{12,28},{16,0},{20,4},{24,8},{28,12},{1,17},{... | collective-permute-start | bytes 196616 | tf_op jit(solution)/shard_map/ppermute | solution.py:355
  8.0 4.2 %collective-permute-start = (f32[256,512]{1,0:T(8,128)S(1)}, f32[256,512]{1,0:T(8,128)S(1)}, u32[]{:S(2)}, u32[]{:S(2)}) collective-permute-start(f32[256,512]{1,0:T(8,128)S(1)} %get-tuple-element.40.pack_other_ref.pack_ref), channel_id=1, source_target_pairs={{0,4},{4,0},{8,12},{12,8},{16,20},{20,16},{24,28},{28,24},{1,5},{5... | collective-permute-start | bytes 1572872 | tf_op jit(solution)/shard_map/ppermute | solution.py:355
  9.3 2.9 %collective-permute-start.1 = (f32[128,512]{1,0:T(8,128)S(1)}, f32[128,512]{1,0:T(8,128)S(1)}, u32[]{:S(2)}, u32[]{:S(2)}) collective-permute-start(f32[128,512]{1,0:T(8,128)S(1)} %get-tuple-element.44.local_ref), channel_id=1, source_target_pairs={{0,4},{4,0},{8,12},{12,8},{16,20},{20,16},{24,28},{28,24},{1,5},{5... | collective-permute-start | bytes 786440 | tf_op jit(solution)/shard_map/ppermute | solution.py:355
  12.6 1.3 %collective-permute-start.6 = (f32[144,128]{1,0:T(8,128)S(1)}, f32[144,128]{1,0:T(8,128)S(1)}, u32[]{:S(2)}, u32[]{:S(2)}) collective-permute-start(f32[144,128]{1,0:T(8,128)S(1)} %pad_maximum_fusion), channel_id=1, source_target_pairs={{0,4},{4,0},{8,12},{12,8},{16,20},{20,16},{24,28},{28,24},{1,5},{5... | collective-permute-start | bytes 221192 | tf_op jit(solution)/shard_map/ppermute | solution.py:355
  13.9 4.2 %collective-permute-start.9 = (f32[16,128]{1,0:T(8,128)S(1)}, f32[16,128]{1,0:T(8,128)S(1)}, u32[]{:S(2)}, u32[]{:S(2)}) collective-permute-start(f32[16,128]{1,0:T(8,128)S(1)} %slice_add_fusion.pair_sums_ref), channel_id=1, source_target_pairs={{0,6},{1,7},{2,4},{3,5},{4,2},{5,3},{6,0},{7,1},{8,14},{9,15},{10,... | collective-permute-start | bytes 24584 | tf_op jit(solution)/shard_map/ppermute | solution.py:385
  16.3 4.9 %collective-permute-start.8 = (f32[16,128]{1,0:T(8,128)S(1)}, f32[16,128]{1,0:T(8,128)S(1)}, u32[]{:S(2)}, u32[]{:S(2)}) collective-permute-start(f32[16,128]{1,0:T(8,128)S(1)} %slice_add_fusion.pair_sums_ref), channel_id=1, source_target_pairs={{0,7},{1,6},{2,5},{3,4},{4,3},{5,2},{6,1},{7,0},{8,15},{9,14},{10,... | collective-permute-start | bytes 24584 | tf_op jit(solution)/shard_map/ppermute | solution.py:385
  17.6 3.6 %collective-permute-start.7 = (f32[16,128]{1,0:T(8,128)S(1)}, f32[16,128]{1,0:T(8,128)S(1)}, u32[]{:S(2)}, u32[]{:S(2)}) collective-permute-start(f32[16,128]{1,0:T(8,128)S(1)} %slice_add_fusion.pair_sums_ref), channel_id=1, source_target_pairs={{0,5},{1,4},{2,7},{3,6},{4,1},{5,0},{6,3},{7,2},{8,13},{9,12},{10,... | collective-permute-start | bytes 24584 | tf_op jit(solution)/shard_map/ppermute | solution.py:385
  21.1 3.7 %copy-start = (f32[512,256]{1,0:T(8,128)S(1)}, f32[512,256]{1,0:T(8,128)}, u32[]{:S(2)}) copy-start(f32[512,256]{1,0:T(8,128)} %k_ref.1) | copy-start | bytes 1572868
  21.2 3.7 %copy-start.1 = (f32[512,256]{1,0:T(8,128)S(1)}, f32[512,256]{1,0:T(8,128)}, u32[]{:S(2)}) copy-start(f32[512,256]{1,0:T(8,128)} %v_ref.1) | copy-start | bytes 1572868
  21.5 6.0 %collective-permute-start.12 = (f32[128,128]{1,0:T(8,128)S(1)}, f32[128,128]{1,0:T(8,128)S(1)}, u32[]{:S(2)}, u32[]{:S(2)}) collective-permute-start(f32[128,128]{1,0:T(8,128)S(1)} %get-tuple-element.60), channel_id=1, source_target_pairs={{0,28},{4,24},{8,20},{12,16},{16,12},{20,8},{24,4},{28,0},{1,29},{... | collective-permute-start | bytes 196616 | tf_op jit(solution)/shard_map/ppermute | solution.py:355
  23.7 4.1 %collective-permute-start.11 = (f32[128,128]{1,0:T(8,128)S(1)}, f32[128,128]{1,0:T(8,128)S(1)}, u32[]{:S(2)}, u32[]{:S(2)}) collective-permute-start(f32[128,128]{1,0:T(8,128)S(1)} %get-tuple-element.60), channel_id=1, source_target_pairs={{0,12},{4,8},{8,4},{12,0},{16,28},{20,24},{24,20},{28,16},{1,13},{... | collective-permute-start | bytes 196616 | tf_op jit(solution)/shard_map/ppermute | solution.py:355
  24.0 4.3 %collective-permute-start.10 = (f32[128,128]{1,0:T(8,128)S(1)}, f32[128,128]{1,0:T(8,128)S(1)}, u32[]{:S(2)}, u32[]{:S(2)}) collective-permute-start(f32[128,128]{1,0:T(8,128)S(1)} %get-tuple-element.60), channel_id=1, source_target_pairs={{0,16},{4,20},{8,24},{12,28},{16,0},{20,4},{24,8},{28,12},{1,17},{... | collective-permute-start | bytes 196616 | tf_op jit(solution)/shard_map/ppermute | solution.py:355
  28.4 1.3 %collective-permute-start.13 = (f32[128,128]{1,0:T(8,128)S(1)}, f32[128,128]{1,0:T(8,128)S(1)}, u32[]{:S(2)}, u32[]{:S(2)}) collective-permute-start(f32[128,128]{1,0:T(8,128)S(1)} %select_add_fusion.1), channel_id=1, source_target_pairs={{0,4},{4,0},{8,12},{12,8},{16,20},{20,16},{24,28},{28,24},{1,5},{5... | collective-permute-start | bytes 196616 | tf_op jit(solution)/shard_map/ppermute | solution.py:355

commit v8 on v6

--- a/solution.py
+++ b/solution.py
@@ -332,10 +332,11 @@
     for head in heads(half):
         col = half_cols(half, mine, head.start, HD)
         place = head if mine else slice(half + head.start, half + head.stop)
-        for n, row in enumerate(blocks(rows)):
-            here = state_ref[head, :] if n == last else state_ref[head, :] + after_ref[n, head, :]
+        states = [state_ref[head, :] if n == last else state_ref[head, :] + after_ref[n, head, :] for n in range(last + 1)]
+        for here, row in zip(states, blocks(rows)):
             gk_ref[row, head] = gk_local_ref[row, place] + product_state(split(v_ref[row, col]), state_operand(here, False), False)
             leave(gk_ref, gk_hbm, row, head, col)
+        for here, row in zip(states, blocks(rows)):
             gv_ref[row, head] = gv_local_ref[row, place] + product_state(split(k_ref[row, col]), state_operand(here, True), True)
             leave(gv_ref, gv_hbm, row, head, col)
     for copy in copies:

time: 31 us -> 31 us (level)
  no operation moved by 1% of the time
where the time goes in v8:
time: 31 us; the launch traced here: 30.8 us
  starting transfers between devices  12.7 us (41%)
  Pallas kernels  9.14 us (29%)
  waiting for transfers between devices  8.09 us (26%)
  between operations  0.82 us (3%)
    pallas_call x9, Pallas kernels, call(): pl.pallas_call(body, out_shape=outs, in_specs=[place(i in hbm_in) for i i...  9.14 us
    ppermute x11, starting transfers between devices, swap(): return lax.ppermute(x, axis, [(i, i ^ distance) for i in range(count)])  8.78 us
    ppermute x11, waiting for transfers between devices, swap(): return lax.ppermute(x, axis, [(i, i ^ distance) for i in range(count)])  5.03 us
    ppermute x3, starting transfers between devices, sum_over_heads(): parts.append(lax.ppermute(x, ('seq', 'head'), pairs))  3.89 us
    ppermute x3, waiting for transfers between devices, sum_over_heads(): parts.append(lax.ppermute(x, ('seq', 'head'), pairs))  3.06 us
  transfers between devices with their start and end apart: 14, of which 9 were waited for; matrix products, arithmetic and copies ran while one was open for 0% of the time, Pallas kernels for 18%

profile of v8, /device:TPU:0, one launch (start us, length us, event | category | flops | bytes accessed | tf_op | source)
XLA Modules:
  0.0 30.8 jit_solution(14857482313008153873)
XLA Ops:
  0.7 1.6 %key_states_other.1 = (f32[128,128]{1,0:T(8,128)S(1)}, f32[1,128,128]{2,1,0:T(8,128)S(1)}, f32[512,256]{1,0:T(8,128)S(1)}, f32[512,256]{1,0:T(8,128)S(1)}, f32[1,256]{1,0:T(1,128)S(1)}) custom-call(f32[512,256]{1,0:T(8,128)} %k_ref.5, f32[512,256]{1,0:T(8,128)} %v_ref.5, f32[1,256]{1,0:T(1,128)} %bitcast.1), custom_call_target="tpu_custom_call" | custom-call | flops 50331648 | bytes 2099200 | tf_op jit(solution)/shard_map/key_states_other/pallas_call | solution.py:79
  2.3 0.5 %collective-permute-start.2 = (f32[128,128]{1,0:T(8,128)S(1)}, f32[128,128]{1,0:T(8,128)S(1)}, u32[]{:S(2)}, u32[]{:S(2)}) collective-permute-start(f32[128,128]{1,0:T(8,128)S(1)} %get-tuple-element.44), channel_id=1, source_target_pairs={{0,4},{4,0},{8,12},{12,8},{16,20},{20,16},{24,28},{28,24},{1,5},{5... | collective-permute-start | bytes 196616 | tf_op jit(solution)/shard_map/ppermute | solution.py:348
  2.8 0.4 %key_states_mine.1 = (f32[128,128]{1,0:T(8,128)S(1)}, f32[1,128,128]{2,1,0:T(8,128)S(1)}, f32[256,512]{1,0:T(8,128)S(1)}, f32[256,512]{1,0:T(8,128)S(1)}) custom-call(f32[512,256]{1,0:T(8,128)S(1)} %get-tuple-element.34.k_ref, f32[512,256]{1,0:T(8,128)S(1)} %get-tuple-element.35.v_ref, f32[512,256]{1,0:T(8,128)S(1)} %copy-done.2, f32[512,256]{1,0:T(8,128)S(1)} %copy-done.3, ...), custom_call_target="tpu_custom_call" | custom-call | flops 50331648 | bytes 4196352 | tf_op jit(solution)/shard_map/key_states_mine/pallas_call | solution.py:79
  3.3 0.5 %collective-permute-done.2 = f32[128,128]{1,0:T(8,128)S(1)} collective-permute-done((f32[128,128]{1,0:T(8,128)S(1)}, f32[128,128]{1,0:T(8,128)S(1)}, u32[]{:S(2)}, u32[]{:S(2)}) %collective-permute-start.2) | collective-permute-done | bytes 65568 | tf_op jit(solution)/shard_map/ppermute | solution.py:348
  3.7 3.6 %collective-permute-start.3 = (f32[128,128]{1,0:T(8,128)S(1)}, f32[128,128]{1,0:T(8,128)S(1)}, u32[]{:S(2)}, u32[]{:S(2)}) collective-permute-start(f32[128,128]{1,0:T(8,128)S(1)} %add.44), channel_id=1, source_target_pairs={{0,28},{4,24},{8,20},{12,16},{16,12},{20,8},{24,4},{28,0},{1,29},{... | collective-permute-start | bytes 196616 | tf_op jit(solution)/shard_map/ppermute | solution.py:348
  7.4 0.5 %collective-permute-start.4 = (f32[128,128]{1,0:T(8,128)S(1)}, f32[128,128]{1,0:T(8,128)S(1)}, u32[]{:S(2)}, u32[]{:S(2)}) collective-permute-start(f32[128,128]{1,0:T(8,128)S(1)} %add.44), channel_id=1, source_target_pairs={{0,12},{4,8},{8,4},{12,0},{16,28},{20,24},{24,20},{28,16},{1,13},{... | collective-permute-start | bytes 196616 | tf_op jit(solution)/shard_map/ppermute | solution.py:348
  8.1 1.2 %attend_local.1 = (f32[128,512]{1,0:T(8,128)S(1)}, f32[128,512]{1,0:T(8,128)S(1)}) custom-call(f32[256,512]{1,0:T(8,128)S(1)} %get-tuple-element.37.pack_mine_ref.own_ref, f32[256,512]{1,0:T(8,128)S(1)} %get-tuple-element.38.pack_other_ref.pack_ref, f32[512,256]{1,0:T(8,128)S(1)} %get-tuple-element.34.k_ref, f32[512,256]{1,0:T(8,128)S(1)} %get-tuple-element.35.v_ref, ...), custom_call_target="tpu_custom_call" | custom-call | flops 503316480 | bytes 4456448 | tf_op jit(solution)/shard_map/attend_local/pallas_call | solution.py:79
  9.3 0.5 %collective-permute-start.1 = (f32[128,512]{1,0:T(8,128)S(1)}, f32[128,512]{1,0:T(8,128)S(1)}, u32[]{:S(2)}, u32[]{:S(2)}) collective-permute-start(f32[128,512]{1,0:T(8,128)S(1)} %get-tuple-element.42.local_ref), channel_id=1, source_target_pairs={{0,4},{4,0},{8,12},{12,8},{16,20},{20,16},{24,28},{28,24},{1,5},{5... | collective-permute-start | bytes 786440 | tf_op jit(solution)/shard_map/ppermute | solution.py:348
  9.8 1.7 %collective-permute-done.4 = f32[128,128]{1,0:T(8,128)S(1)} collective-permute-done((f32[128,128]{1,0:T(8,128)S(1)}, f32[128,128]{1,0:T(8,128)S(1)}, u32[]{:S(2)}, u32[]{:S(2)}) %collective-permute-start.4) | collective-permute-done | bytes 65568 | tf_op jit(solution)/shard_map/ppermute | solution.py:348
  11.6 0.5 %collective-permute-done.5 = f32[128,128]{1,0:T(8,128)S(1)} collective-permute-done((f32[128,128]{1,0:T(8,128)S(1)}, f32[128,128]{1,0:T(8,128)S(1)}, u32[]{:S(2)}, u32[]{:S(2)}) %collective-permute-start.5) | collective-permute-done | bytes 65568 | tf_op jit(solution)/shard_map/ppermute | solution.py:348
  12.2 0.4 %attend_state.1 = (f32[128,512]{1,0:T(8,128)S(1)}, f32[128,512]{1,0:T(8,128)S(1)}, f32[16,128]{1,0:T(8,128)S(1)}) custom-call(f32[256,512]{1,0:T(8,128)S(1)} %get-tuple-element.37.pack_mine_ref.own_ref, f32[128,512]{1,0:T(8,128)S(1)} %get-tuple-element.41.own_local_ref, f32[256,512]{1,0:T(8,128)S(1)} %collective-permute-done.sib_ref, ...), custom_call_target="tpu_custom_call" | custom-call | flops 100663296 | bytes 3407872 | tf_op jit(solution)/shard_map/attend_state/pallas_call | solution.py:79
  12.7 1.3 %collective-permute-done.6.got_ref = f32[144,128]{1,0:T(8,128)S(1)} collective-permute-done((f32[144,128]{1,0:T(8,128)S(1)}, f32[144,128]{1,0:T(8,128)S(1)}, u32[]{:S(2)}, u32[]{:S(2)}) %collective-permute-start.6) | collective-permute-done | bytes 73760 | tf_op jit(solution)/shard_map/ppermute | solution.py:348
  13.9 2.4 %collective-permute-start.7 = (f32[16,128]{1,0:T(8,128)S(1)}, f32[16,128]{1,0:T(8,128)S(1)}, u32[]{:S(2)}, u32[]{:S(2)}) collective-permute-start(f32[16,128]{1,0:T(8,128)S(1)} %slice_add_fusion.pair_sums_ref), channel_id=1, source_target_pairs={{0,6},{1,7},{2,4},{3,5},{4,2},{5,3},{6,0},{7,1},{8,14},{9,15},{10,... | collective-permute-start | bytes 24584 | tf_op jit(solution)/shard_map/ppermute | solution.py:378
  16.3 1.3 %collective-permute-start.8 = (f32[16,128]{1,0:T(8,128)S(1)}, f32[16,128]{1,0:T(8,128)S(1)}, u32[]{:S(2)}, u32[]{:S(2)}) collective-permute-start(f32[16,128]{1,0:T(8,128)S(1)} %slice_add_fusion.pair_sums_ref), channel_id=1, source_target_pairs={{0,7},{1,6},{2,5},{3,4},{4,3},{5,2},{6,1},{7,0},{8,15},{9,14},{10,... | collective-permute-start | bytes 24584 | tf_op jit(solution)/shard_map/ppermute | solution.py:378
  17.8 0.3 attend_other.1
  18.1 3.1 %collective-permute-done.8 = f32[16,128]{1,0:T(8,128)S(1)} collective-permute-done((f32[16,128]{1,0:T(8,128)S(1)}, f32[16,128]{1,0:T(8,128)S(1)}, u32[]{:S(2)}, u32[]{:S(2)}) %collective-permute-start.8) | collective-permute-done | bytes 8224 | tf_op jit(solution)/shard_map/ppermute | solution.py:378
  21.2 0.4 %grad_states.1 = (f32[128,128]{1,0:T(8,128)S(1)}, f32[128,128]{1,0:T(8,128)S(1)}, f32[128,128]{1,0:T(8,128)S(1)}, f32[1,128,128]{2,1,0:T(8,128)S(1)}, bf16[128,5...) custom-call(f32[16,128]{1,0:T(8,128)S(1)} %add_add_fusion.sums_ref, ...), custom_call_target="tpu_custom_call" | custom-call | flops 100663296 | bytes 3162112 | tf_op jit(solution)/shard_map/grad_states/pallas_call | solution.py:79
  21.5 2.2 %collective-permute-start.10 = (f32[128,128]{1,0:T(8,128)S(1)}, f32[128,128]{1,0:T(8,128)S(1)}, u32[]{:S(2)}, u32[]{:S(2)}) collective-permute-start(f32[128,128]{1,0:T(8,128)S(1)} %get-tuple-element.56), channel_id=1, source_target_pairs={{0,28},{4,24},{8,20},{12,16},{16,12},{20,8},{24,4},{28,0},{1,29},{... | collective-permute-start | bytes 196616 | tf_op jit(solution)/shard_map/ppermute | solution.py:348
  23.7 0.3 collective-permute-start.11
  24.0 0.8 %collective-permute-start.12 = (f32[128,128]{1,0:T(8,128)S(1)}, f32[128,128]{1,0:T(8,128)S(1)}, u32[]{:S(2)}, u32[]{:S(2)}) collective-permute-start(f32[128,128]{1,0:T(8,128)S(1)} %get-tuple-element.56), channel_id=1, source_target_pairs={{0,16},{4,20},{8,24},{12,28},{16,0},{20,4},{24,8},{28,12},{1,17},{... | collective-permute-start | bytes 196616 | tf_op jit(solution)/shard_map/ppermute | solution.py:348
  24.8 2.8 %grads_local.1 = (f32[512,256]{1,0:T(8,128)}, f32[512,256]{1,0:T(8,128)S(1)}, f32[512,256]{1,0:T(8,128)S(1)}, f32[1,128,128]{2,1,0:T(8,128)S(1)}, f32[128,128]{1,0:T(8,128)S(1)}) custom-call(f32[16,128]{1,0:T(8,128)S(1)} %add_add_fusion.sums_ref, f32[144,128]{1,0:T(8,128)S(1)} %collective-permute-done.6.got_ref, ...), custom_call_target="tpu_custom_call" | custom-call | flops 1409286144 | bytes 5931008 | tf_op jit(solution)/shard_map/grads_local/pallas_call | solution.py:79
  27.8 0.6 %collective-permute-done.12 = f32[128,128]{1,0:T(8,128)S(1)} collective-permute-done((f32[128,128]{1,0:T(8,128)S(1)}, f32[128,128]{1,0:T(8,128)S(1)}, u32[]{:S(2)}, u32[]{:S(2)}) %collective-permute-start.12) | collective-permute-done | bytes 65568 | tf_op jit(solution)/shard_map/ppermute | solution.py:348
  28.5 1.1 %grads_state_mine.1 = (f32[512,256]{1,0:T(8,128)}, f32[512,256]{1,0:T(8,128)}) custom-call(f32[512,256]{1,0:T(8,128)S(1)} %copy-done, f32[512,256]{1,0:T(8,128)S(1)} %copy-done.1, f32[512,256]{1,0:T(8,128)S(1)} %get-tuple-element.54.gk_local_ref, f32[512,256]{1,0:T(8,128)S(1)} %get-tuple-element.55.gv_local_ref, f32[128,128]{1,0:T(8,128)S(1)} %get-tuple-element.65.state_ref, ...), custom_call_target="tpu_custom_call" | custom-call | flops 100663296 | bytes 4456448 | tf_op jit(solution)/shard_map/grads_state_mine/pallas_call | solution.py:79
  29.8 1.1 %grads_state_other.1 = (f32[512,256]{1,0:T(8,128)}, f32[512,256]{1,0:T(8,128)}) custom-call(f32[512,256]{1,0:T(8,128)S(1)} %copy-done, f32[512,256]{1,0:T(8,128)S(1)} %copy-done.1, f32[512,256]{1,0:T(8,128)S(1)} %get-tuple-element.54.gk_local_ref, f32[512,256]{1,0:T(8,128)S(1)} %get-tuple-element.55.gv_local_ref, ...), custom_call_target="tpu_custom_call", output_to_operand_aliasing={{0}: (6, {}), {1}: (7, {})} | custom-call | flops 100663296 | bytes 6553600 | tf_op jit(solution)/shard_map/grads_state_other/pallas_call | solution.py:79
  (29 shorter events, 1.1 us)
Async XLA Ops:
  0.6 2.2 %copy-start.2 = (f32[512,256]{1,0:T(8,128)S(1)}, f32[512,256]{1,0:T(8,128)}, u32[]{:S(2)}) copy-start(f32[512,256]{1,0:T(8,128)} %q_ref.1) | copy-start | bytes 1572868
  0.6 2.2 %copy-start.3 = (f32[512,256]{1,0:T(8,128)S(1)}, f32[512,256]{1,0:T(8,128)}, u32[]{:S(2)}) copy-start(f32[512,256]{1,0:T(8,128)} %cot_ref.1) | copy-start | bytes 1572868
  2.3 1.4 %collective-permute-start.2 = (f32[128,128]{1,0:T(8,128)S(1)}, f32[128,128]{1,0:T(8,128)S(1)}, u32[]{:S(2)}, u32[]{:S(2)}) collective-permute-start(f32[128,128]{1,0:T(8,128)S(1)} %get-tuple-element.44), channel_id=1, source_target_pairs={{0,4},{4,0},{8,12},{12,8},{16,20},{20,16},{24,28},{28,24},{1,5},{5... | collective-permute-start | bytes 196616 | tf_op jit(solution)/shard_map/ppermute | solution.py:348
  3.7 6.1 %collective-permute-start.3 = (f32[128,128]{1,0:T(8,128)S(1)}, f32[128,128]{1,0:T(8,128)S(1)}, u32[]{:S(2)}, u32[]{:S(2)}) collective-permute-start(f32[128,128]{1,0:T(8,128)S(1)} %add.44), channel_id=1, source_target_pairs={{0,28},{4,24},{8,20},{12,16},{16,12},{20,8},{24,4},{28,0},{1,29},{... | collective-permute-start | bytes 196616 | tf_op jit(solution)/shard_map/ppermute | solution.py:348
  7.4 4.2 %collective-permute-start.4 = (f32[128,128]{1,0:T(8,128)S(1)}, f32[128,128]{1,0:T(8,128)S(1)}, u32[]{:S(2)}, u32[]{:S(2)}) collective-permute-start(f32[128,128]{1,0:T(8,128)S(1)} %add.44), channel_id=1, source_target_pairs={{0,12},{4,8},{8,4},{12,0},{16,28},{20,24},{24,20},{28,16},{1,13},{... | collective-permute-start | bytes 196616 | tf_op jit(solution)/shard_map/ppermute | solution.py:348
  7.9 4.3 %collective-permute-start.5 = (f32[128,128]{1,0:T(8,128)S(1)}, f32[128,128]{1,0:T(8,128)S(1)}, u32[]{:S(2)}, u32[]{:S(2)}) collective-permute-start(f32[128,128]{1,0:T(8,128)S(1)} %add.44), channel_id=1, source_target_pairs={{0,16},{4,20},{8,24},{12,28},{16,0},{20,4},{24,8},{28,12},{1,17},{... | collective-permute-start | bytes 196616 | tf_op jit(solution)/shard_map/ppermute | solution.py:348
  8.0 4.2 %collective-permute-start = (f32[256,512]{1,0:T(8,128)S(1)}, f32[256,512]{1,0:T(8,128)S(1)}, u32[]{:S(2)}, u32[]{:S(2)}) collective-permute-start(f32[256,512]{1,0:T(8,128)S(1)} %get-tuple-element.38.pack_other_ref.pack_ref), channel_id=1, source_target_pairs={{0,4},{4,0},{8,12},{12,8},{16,20},{20,16},{24,28},{28,24},{1,5},{5... | collective-permute-start | bytes 1572872 | tf_op jit(solution)/shard_map/ppermute | solution.py:348
  9.3 2.9 %collective-permute-start.1 = (f32[128,512]{1,0:T(8,128)S(1)}, f32[128,512]{1,0:T(8,128)S(1)}, u32[]{:S(2)}, u32[]{:S(2)}) collective-permute-start(f32[128,512]{1,0:T(8,128)S(1)} %get-tuple-element.42.local_ref), channel_id=1, source_target_pairs={{0,4},{4,0},{8,12},{12,8},{16,20},{20,16},{24,28},{28,24},{1,5},{5... | collective-permute-start | bytes 786440 | tf_op jit(solution)/shard_map/ppermute | solution.py:348
  12.6 1.3 %collective-permute-start.6 = (f32[144,128]{1,0:T(8,128)S(1)}, f32[144,128]{1,0:T(8,128)S(1)}, u32[]{:S(2)}, u32[]{:S(2)}) collective-permute-start(f32[144,128]{1,0:T(8,128)S(1)} %pad_maximum_fusion), channel_id=1, source_target_pairs={{0,4},{4,0},{8,12},{12,8},{16,20},{20,16},{24,28},{28,24},{1,5},{5... | collective-permute-start | bytes 221192 | tf_op jit(solution)/shard_map/ppermute | solution.py:348
  13.9 4.2 %collective-permute-start.7 = (f32[16,128]{1,0:T(8,128)S(1)}, f32[16,128]{1,0:T(8,128)S(1)}, u32[]{:S(2)}, u32[]{:S(2)}) collective-permute-start(f32[16,128]{1,0:T(8,128)S(1)} %slice_add_fusion.pair_sums_ref), channel_id=1, source_target_pairs={{0,6},{1,7},{2,4},{3,5},{4,2},{5,3},{6,0},{7,1},{8,14},{9,15},{10,... | collective-permute-start | bytes 24584 | tf_op jit(solution)/shard_map/ppermute | solution.py:378
  16.3 4.9 %collective-permute-start.8 = (f32[16,128]{1,0:T(8,128)S(1)}, f32[16,128]{1,0:T(8,128)S(1)}, u32[]{:S(2)}, u32[]{:S(2)}) collective-permute-start(f32[16,128]{1,0:T(8,128)S(1)} %slice_add_fusion.pair_sums_ref), channel_id=1, source_target_pairs={{0,7},{1,6},{2,5},{3,4},{4,3},{5,2},{6,1},{7,0},{8,15},{9,14},{10,... | collective-permute-start | bytes 24584 | tf_op jit(solution)/shard_map/ppermute | solution.py:378
  17.6 3.6 %collective-permute-start.9 = (f32[16,128]{1,0:T(8,128)S(1)}, f32[16,128]{1,0:T(8,128)S(1)}, u32[]{:S(2)}, u32[]{:S(2)}) collective-permute-start(f32[16,128]{1,0:T(8,128)S(1)} %slice_add_fusion.pair_sums_ref), channel_id=1, source_target_pairs={{0,5},{1,4},{2,7},{3,6},{4,1},{5,0},{6,3},{7,2},{8,13},{9,12},{10,... | collective-permute-start | bytes 24584 | tf_op jit(solution)/shard_map/ppermute | solution.py:378
  21.1 3.7 %copy-start = (f32[512,256]{1,0:T(8,128)S(1)}, f32[512,256]{1,0:T(8,128)}, u32[]{:S(2)}) copy-start(f32[512,256]{1,0:T(8,128)} %k_ref.5) | copy-start | bytes 1572868
  21.2 3.7 %copy-start.1 = (f32[512,256]{1,0:T(8,128)S(1)}, f32[512,256]{1,0:T(8,128)}, u32[]{:S(2)}) copy-start(f32[512,256]{1,0:T(8,128)} %v_ref.5) | copy-start | bytes 1572868
  21.5 6.1 %collective-permute-start.10 = (f32[128,128]{1,0:T(8,128)S(1)}, f32[128,128]{1,0:T(8,128)S(1)}, u32[]{:S(2)}, u32[]{:S(2)}) collective-permute-start(f32[128,128]{1,0:T(8,128)S(1)} %get-tuple-element.56), channel_id=1, source_target_pairs={{0,28},{4,24},{8,20},{12,16},{16,12},{20,8},{24,4},{28,0},{1,29},{... | collective-permute-start | bytes 196616 | tf_op jit(solution)/shard_map/ppermute | solution.py:348
  23.7 4.1 %collective-permute-start.11 = (f32[128,128]{1,0:T(8,128)S(1)}, f32[128,128]{1,0:T(8,128)S(1)}, u32[]{:S(2)}, u32[]{:S(2)}) collective-permute-start(f32[128,128]{1,0:T(8,128)S(1)} %get-tuple-element.56), channel_id=1, source_target_pairs={{0,12},{4,8},{8,4},{12,0},{16,28},{20,24},{24,20},{28,16},{1,13},{... | collective-permute-start | bytes 196616 | tf_op jit(solution)/shard_map/ppermute | solution.py:348
  24.0 4.3 %collective-permute-start.12 = (f32[128,128]{1,0:T(8,128)S(1)}, f32[128,128]{1,0:T(8,128)S(1)}, u32[]{:S(2)}, u32[]{:S(2)}) collective-permute-start(f32[128,128]{1,0:T(8,128)S(1)} %get-tuple-element.56), channel_id=1, source_target_pairs={{0,16},{4,20},{8,24},{12,28},{16,0},{20,4},{24,8},{28,12},{1,17},{... | collective-permute-start | bytes 196616 | tf_op jit(solution)/shard_map/ppermute | solution.py:348
  28.4 1.3 %collective-permute-start.13 = (f32[128,128]{1,0:T(8,128)S(1)}, f32[128,128]{1,0:T(8,128)S(1)}, u32[]{:S(2)}, u32[]{:S(2)}) collective-permute-start(f32[128,128]{1,0:T(8,128)S(1)} %select_add_fusion.1), channel_id=1, source_target_pairs={{0,4},{4,0},{8,12},{12,8},{16,20},{20,16},{24,28},{28,24},{1,5},{5... | collective-permute-start | bytes 196616 | tf_op jit(solution)/shard_map/ppermute | solution.py:348
